TPU v7x, 32 devices: a whole 2x2x4 slice. The times are simulated.
32 devices in a mesh: row: 2 (over core), col: 4 (over y, x), cfg: 4 (over z).
Axes of the slice: x: 2, y: 2, z: 4, core: 2. Of those that a mesh axis runs over, the one named last changes fastest.
Arguments:
- eigvec: bfloat16 [18432, 18432], P('row', ('col', 'cfg')), may hold values from -0.046875 to 0.046875
- force_const: bfloat16 [18432, 18432], P(('col', 'cfg'), 'row'), may hold values from -0.046875 to 0.046875
- amplitudes: bfloat16 [18432, 512], P(('col', 'cfg')), may hold values from -6 to 6
- mlip_forces: bfloat16 [18432, 512], P(('col', 'cfg'), 'row'), may hold values from -6 to 6
- frequency: float32 [18432], P(('col', 'cfg')), may hold values from 0.25 to 4
Outputs:
- gradient: float32 [18432, 18432], P(('col', 'cfg'), 'row')
All inputs are finite; a program needn't handle non-finite values.
Results may differ from a plain program's by a relative error of at most 0.0055.
Values may be sent and summed in bfloat16 or wider, within the bound.
No kernel may reach another device: no remote copies, remote signals or barrier semaphores. Data moves between devices by JAX's collectives and lax.ppermute only.
A program may use at most 192 MiB of HBM per device.

v0:
```python
import jax
import jax.numpy as jnp
from jax import lax
from jax.sharding import PartitionSpec as P


def local(eigvec, force_const, amplitudes, mlip_forces, frequency):
    mode_scale = 1.0 / jnp.sqrt(2.0 * frequency)
    scaled_amp = (mode_scale[:, None] * amplitudes.astype(jnp.float32)).astype(jnp.bfloat16)
    own_rows = lax.psum_scatter(
        lax.dot_general(
            scaled_amp, eigvec, (((0,), (1,)), ((), ())), preferred_element_type=jnp.float32
        ),
        ("col", "cfg"),
        scatter_dimension=0,
        tiled=True,
    )
    displaced = lax.all_gather(own_rows.astype(jnp.bfloat16), ("col", "cfg"), axis=0, tiled=True)
    harmonic = lax.dot_general(
        force_const, displaced, (((1,), (1,)), ((), ())), preferred_element_type=jnp.float32
    )
    own_width = mlip_forces.shape[1]
    placed = lax.dynamic_update_slice_in_dim(
        jnp.zeros_like(harmonic),
        mlip_forces.astype(jnp.float32),
        lax.axis_index("row") * own_width,
        1,
    )
    residual = lax.psum(harmonic + placed, "row").astype(jnp.bfloat16)
    total = jnp.dot(residual, displaced, preferred_element_type=jnp.float32)
    return total / jnp.sqrt(jnp.float32(displaced.shape[0]))


def solution(mesh):
    return jax.shard_map(
        local,
        mesh=mesh,
        in_specs=(
            P("row", ("col", "cfg")),
            P(("col", "cfg"), "row"),
            P(("col", "cfg"), None),
            P(("col", "cfg"), "row"),
            P(("col", "cfg")),
        ),
        out_specs=P(("col", "cfg"), "row"),
        check_vma=False,
    )
```

profile of v0, /device:TPU:0, one launch (start us, length us, event | category | flops | bytes accessed | tf_op | source)
XLA Modules:
  0.0 500.7 jit_solution(17180297933116774590)
XLA Ops:
  6.5 0.0 reduce-scatter.2.cloned.1.call-start
  6.5 0.7 multiply_rsqrt_fusion
  7.2 20.4 %fusion = f32[512,9216]{1,0:T(8,128)} fusion(bf16[9216,1152]{1,0:T(8,128)(2,1)} %param.5, bf16[1152,512]{1,0:T(8,128)(2,1)} %param.7, f32[1152]{0:T(1024)S(1)} %multiply_rsqrt_fusion), kind=kOutput, calls=%fused_computation.2 | convolution fusion | flops 10873405440 | bytes 41292288 | tf_op jit(solution)/shard_map/dot_general | solution.py:11
  27.6 0.0 reduce-scatter.2.cloned.1.call-update
  27.6 0.0 copy-start.1
  27.7 0.0 all-gather.2.cloned.1.call-start
  27.7 287.8 %reduce-scatter.2.cloned.1.call-done = f32[32,9216]{1,0:T(8,128)} async-done(((f32[512,9216]{1,0:T(8,128)}), f32[32,9216]{1,0:T(8,128)}) %reduce-scatter.2.cloned.1.call-update) | async-done | bytes 1179664 | tf_op jit(solution)/shard_map/reduce_scatter | solution.py:10
  315.5 2.1 convert_element_type.17
  317.6 0.0 all-gather.2.cloned.1.call-update
  317.7 0.0 copy-done.1
  317.7 0.3 copy.6
  318.0 121.9 %all-gather.2.cloned.1.call-done = bf16[512,9216]{1,0:T(8,128)(2,1)} async-done(((bf16[32,9216]{1,0:T(8,128)(2,1)}), bf16[512,9216]{1,0:T(8,128)(2,1)}) %all-gather.2.cloned.1.call-update) | async-done | bytes 9437200 | tf_op jit(solution)/shard_map/all_gather | solution.py:18
  439.9 19.4 %fusion.4 = f32[512,1152]{1,0:T(8,128)} fusion(bf16[512,9216]{1,0:T(8,128)(2,1)} %all-gather.2.cloned.1.call-done, bf16[1152,9216]{1,0:T(8,128)(2,1)} %param.6), kind=kOutput, calls=%fused_computation.8 | convolution fusion | flops 10871635968 | bytes 33030144 | tf_op jit(solution)/shard_map/dot_general | solution.py:19
  459.3 0.0 copy-start
  459.3 1.8 copy.7
  461.1 0.6 copy-done
  461.7 0.1 fusion.1
  461.8 9.8 %all-reduce.1 = bf16[1152,512]{0,1:T(8,128)(2,1)S(1)} all-reduce(f32[1152,512]{0,1:T(8,128)S(1)} %fusion.1), channel_id=1, replica_groups=mesh['row'=2,'col'=4,'cfg'=4] {'row'}, use_global_device_ids=true, to_apply=%region_1.0 | all-reduce | flops 589824 | bytes 3538944 | tf_op jit(solution)/shard_map/psum | solution.py:29
  471.6 22.2 %convolution_multiply_fusion = f32[1152,9216]{1,0:T(8,128)} fusion(bf16[512,9216]{1,0:T(8,128)(2,1)} %all-gather.2.cloned.1.call-done, bf16[1152,512]{0,1:T(8,128)(2,1)S(1)} %all-reduce.1), kind=kOutput, calls=%fused_computation | convolution fusion | flops 10882252800 | bytes 53084160 | tf_op jit(solution)/shard_map/dot_general | solution.py:30
Async XLA Ops:
  6.5 308.9 %reduce-scatter.2.cloned.1.call-start = ((), (), s32[]{:S(2)}) async-start(), calls=%async_computation.1 | async-start | bytes 20054016 | tf_op jit(solution)/shard_map/reduce_scatter | solution.py:10
  27.6 290.0 %copy-start.1 = (bf16[1152,256]{1,0:T(8,128)(2,1)S(1)}, bf16[1152,256]{1,0:T(8,128)(2,1)}, u32[]{:S(2)}) copy-start(bf16[1152,256]{1,0:T(8,128)(2,1)} %param.8) | copy-start | bytes 1769476
  27.7 412.2 %all-gather.2.cloned.1.call-start = ((), (), s32[]{:S(2)}) async-start(), calls=%async_computation.2 | async-start | bytes 10027008 | tf_op jit(solution)/shard_map/all_gather | solution.py:18
  459.3 2.4 copy-start
Sparse Core Ops, SparseCore 0:
  27.8 287.6 reduce-scatter.1
  318.2 121.5 all-gather.1
where the time goes:
time: 501 us
  waiting for transfers between devices  410 us (82%)
  matrix products  62 us (12%)
  between operations  13.4 us (3%)
  blocking collectives  9.85 us (2%)
    reduce_scatter x1, waiting for transfers between devices, local(): lax.psum_scatter(lax.dot_general(scaled_amp, eigvec, (((0,), (1,)), ((),...  288 us
    all_gather x1, waiting for transfers between devices, local(): lax.all_gather(own_rows.astype(jnp.bfloat16), ('col', 'cfg'), axis=0, til...  122 us
    dot_general x1, matrix products, local(): total = jnp.dot(residual, displaced, preferred_element_type=jnp.float32)  22.2 us
    dot_general x1, matrix products, local(): lax.dot_general(scaled_amp, eigvec, (((0,), (1,)), ((), ())), preferred_e...  20.4 us
    dot_general x1, matrix products, local(): lax.dot_general(force_const, displaced, (((1,), (1,)), ((), ())), preferr...  19.4 us
  transfers between devices with their start and end apart: 2, of which 2 were waited for; matrix products, arithmetic and copies ran while one was open for 0% of the time, Pallas kernels for 0%

commit v1 on v0

v1 whole, which is shorter than its diff:
```python
import jax
import jax.numpy as jnp
from jax import lax
from jax.experimental import pallas as pl
from jax.experimental.pallas import tpu as pltpu
from jax.sharding import PartitionSpec as P

BF = jnp.bfloat16
F32 = jnp.float32
MESH = ("row", "col", "cfg")
VMEM = 44 * 1024 * 1024
PARTS = (("apbq", 7), ("abpq", 7), ("abpq", 6), ("pabq", 8), ("apbq", 8))
ORDER = (
    (1, 3, 0, 4, 2, 1, 0, 3, 1, 4, 0, 1, 2, 0, 3, 2, 4, 3, 1, 4,)
    + (0, 2, 0, 3, 1, 3, 4, 1, 2, 4, 0, 3, 2, 1, 4, 2, 0, 4, 3, 2,)
)


def bits_of(size):
    assert size & (size - 1) == 0
    return size.bit_length() - 1


class Grid:
    def __init__(self, sizes):
        self.sizes = sizes
        self.at = tuple(lax.axis_index(name) for name in MESH)
        self.flip = self.at[0] & 1

    def order(self, kind):
        levels = []
        for letter in kind:
            axis = 1 if letter in "ab" else 2
            first = 0 if letter in "ap" else 1
            stop = first + 1 if first == 0 else bits_of(self.sizes[axis])
            levels += [(axis, bit) for bit in range(first, stop)]
        return levels

    def mask(self, level, flip):
        axis, bit = level
        if axis == 2:
            return 0, 1 << bit
        bits = bits_of(self.sizes[1])
        return (1 << (bits - 1 - bit) if flip else 1 << bit), 0

    def mine(self, level):
        axis, bit = level
        if axis == 2:
            return (self.at[2] >> bit) & 1
        bits = bits_of(self.sizes[1])
        return (self.at[1] >> jnp.where(self.flip == 1, bits - 1 - bit, bit)) & 1

    def swap(self, value, level):
        nrow, ncol, ncfg = self.sizes
        pairs = []
        for r in range(nrow):
            dc, dz = self.mask(level, r & 1)
            for c in range(ncol):
                for z in range(ncfg):
                    pairs.append(
                        ((r * ncol + c) * ncfg + z, (r * ncol + (c ^ dc)) * ncfg + (z ^ dz))
                    )
        return lax.ppermute(value, MESH, pairs)


def rows_of(value, start, size):
    return lax.dynamic_slice_in_dim(value, start, size, 0)


def ordered(flag, mine, other, axis=0):
    return jnp.where(
        flag == 0,
        jnp.concatenate([mine, other], axis),
        jnp.concatenate([other, mine], axis),
    )


def tiles_of(size, most):
    count = -(-size // most)
    while size % (16 * count):
        count += 1
    return count, size // count


def params():
    return pltpu.CompilerParams(vmem_limit_bytes=VMEM)


def cost(flops, moved):
    return pl.CostEstimate(flops=flops, bytes_accessed=moved, transcendentals=0)


def piece_kernel(eigvec, amp, row, size, terms, keep):
    count, tile = tiles_of(size, 512)
    depth, configs = amp.shape

    def kernel(at, e, a, *refs):
        value = jnp.dot(e[...], a[...], preferred_element_type=F32)
        for index, term in enumerate(refs[: len(terms)]):
            first = pl.multiple_of(at[index + 1] + pl.program_id(0) * tile, 16)
            value = value + term[pl.ds(first, tile), :].astype(F32)
        refs[len(terms)][...] = value.astype(BF)
        if keep:
            refs[len(terms) + 1][...] = value

    out = pl.BlockSpec((tile, configs), lambda i, at: (i, 0))
    spec = pltpu.PrefetchScalarGridSpec(
        num_scalar_prefetch=1,
        grid=(count,),
        in_specs=[
            pl.BlockSpec(
                (pl.Element(tile), pl.Element(depth)),
                lambda i, at: (pl.multiple_of(at[0] + i * tile, 16), 0),
            ),
            pl.BlockSpec((depth, configs), lambda i, at: (0, 0)),
        ]
        + [pl.BlockSpec(term.shape, lambda i, at: (0, 0)) for term, _ in terms],
        out_specs=[out, out] if keep else [out],
    )
    shapes = [jax.ShapeDtypeStruct((size, configs), BF)]
    if keep:
        shapes.append(jax.ShapeDtypeStruct((size, configs), F32))
    at = jnp.stack([jnp.asarray(v, jnp.int32) for v in [row] + [o for _, o in terms]])
    return pl.pallas_call(
        kernel,
        grid_spec=spec,
        out_shape=shapes,
        compiler_params=params(),
        cost_estimate=cost(2 * size * depth * configs, 2 * size * (depth + configs)),
    )(at, eigvec, amp, *[term for term, _ in terms])


def finish_kernel(force_const, harmonic, displaced, mine, other, base, flag):
    half, configs = mine.shape
    rows = force_const.shape[0]
    count, tile = tiles_of(rows, 288)
    first = harmonic is None

    def kernel(at, k_mine, k_other, d_mine, d_other, *refs):
        total, block = refs[-2:]
        value = jnp.dot(k_mine[...], d_mine[...], preferred_element_type=F32)
        value += jnp.dot(k_other[...], d_other[...], preferred_element_type=F32)
        total[...] = value if first else refs[0][...] + value

        @pl.when(pl.program_id(0) == 0)
        def _():
            block[pl.ds(pl.multiple_of(at[0] * half, 16), half), :] = d_mine[...]
            block[pl.ds(pl.multiple_of((1 - at[0]) * half, 16), half), :] = d_other[...]

    def column(own):
        def index(i, at):
            side = at[0] if own else 1 - at[0]
            return i * tile, pl.multiple_of(base + side * half, 128)

        return pl.BlockSpec((pl.Element(tile), pl.Element(half)), index)

    sums = pl.BlockSpec((tile, configs), lambda i, at: (i, 0))
    whole = pl.BlockSpec((half, configs), lambda i, at: (0, 0))
    extra_specs = [] if first else [sums, pl.BlockSpec(memory_space=pl.ANY)]
    extra = [] if first else [harmonic, displaced]
    spec = pltpu.PrefetchScalarGridSpec(
        num_scalar_prefetch=1,
        grid=(count,),
        in_specs=[column(True), column(False), whole, whole] + extra_specs,
        out_specs=[
            sums,
            pl.BlockSpec((pl.Element(2 * half), pl.Element(configs)), lambda i, at: (base, 0)),
        ],
    )
    return pl.pallas_call(
        kernel,
        grid_spec=spec,
        out_shape=[
            jax.ShapeDtypeStruct((rows, configs), F32),
            jax.ShapeDtypeStruct((force_const.shape[1], configs), BF),
        ],
        input_output_aliases={} if first else {5: 0, 6: 1},
        compiler_params=params(),
        cost_estimate=cost(4 * rows * half * configs, 4 * rows * half),
    )(jnp.asarray(flag, jnp.int32)[None], force_const, force_const, mine, other, *extra)


def gradient_kernel(forces, harmonic, got, displaced):
    rows, configs = harmonic.shape
    columns = displaced.shape[0]
    tile = 512
    scale = float(1.0 / configs**0.5)

    def kernel(f, h, g, d, out, residual):
        @pl.when(pl.program_id(0) == 0)
        def _():
            total = f[...].astype(F32) + (h[...] + g[...].astype(F32))
            residual[...] = total.astype(BF)

        value = lax.dot_general(
            residual[...], d[...], (((1,), (1,)), ((), ())), preferred_element_type=F32
        )
        out[...] = value * scale

    whole = pl.BlockSpec((rows, configs), lambda i: (0, 0))
    return pl.pallas_call(
        kernel,
        grid=(columns // tile,),
        in_specs=[whole, whole, whole, pl.BlockSpec((tile, configs), lambda i: (i, 0))],
        out_specs=pl.BlockSpec((rows, tile), lambda i: (0, i)),
        out_shape=jax.ShapeDtypeStruct((rows, columns), F32),
        scratch_shapes=[pltpu.VMEM((rows, configs), BF)],
        compiler_params=params(),
        cost_estimate=cost(2 * rows * columns * configs, 4 * rows * columns),
    )(forces, harmonic, got, displaced)


def part_steps(g, piece, kind, base, rows, finish):
    row, size, terms = base, rows, []
    levels = g.order(kind)
    pin = yield None
    for level in levels[:-1]:
        size //= 2
        mine = g.mine(level)
        away = (1 - mine) * size
        sent = piece(pin, row + away, size, [(t, o + away) for t, o in terms], False)[0]
        got = g.swap(sent, level)
        pin = yield sent
        terms = [(t, o + mine * size) for t, o in terms] + [(got, 0)]
        row = row + mine * size
    sent, own = piece(pin, row, size, terms, True)
    got = g.swap(sent, levels[-1])
    pin = yield sent
    block = (pin(own) + got.astype(F32)).astype(BF)
    for level in reversed(levels[1:-1]):
        other = g.swap(block, level)
        pin = yield block
        block = ordered(g.mine(level), pin(block), other)
    other = g.swap(block, levels[0])
    pin = yield block
    yield finish(base, pin(block), other, g.mine(levels[0]))


def local(sizes, eigvec, force_const, amplitudes, mlip_forces, frequency):
    g = Grid(sizes)
    rows = eigvec.shape[0]
    tiled = rows % (36 * 2 * 16 * sizes[1] * sizes[2] // 2) == 0
    mode_scale = 1.0 / jnp.sqrt(2.0 * frequency)
    scaled_amp = (mode_scale[:, None] * amplitudes.astype(F32)).astype(BF)
    configs = scaled_amp.shape[1]

    def piece(pin, row, size, terms, keep):
        if tiled:
            return piece_kernel(eigvec, pin(scaled_amp), row, size, terms, keep)
        value = jnp.dot(rows_of(eigvec, row, size), pin(scaled_amp), preferred_element_type=F32)
        for term, offset in terms:
            value = value + rows_of(term, offset, size).astype(F32)
        return value.astype(BF), value

    forces = mlip_forces
    for bit in range(bits_of(sizes[0])):
        pairs = [(r, r ^ (1 << bit)) for r in range(sizes[0])]
        forces = ordered((g.at[0] >> bit) & 1, forces, lax.ppermute(forces, "row", pairs), 1)
    state = {"harmonic": None, "displaced": None}

    def finish(base, mine, other, flag):
        harmonic, displaced = state["harmonic"], state["displaced"]
        if tiled:
            harmonic, displaced = finish_kernel(
                force_const, harmonic, displaced, mine, other, base, flag
            )
        else:
            block = ordered(flag, mine, other)
            count = block.shape[0]
            if harmonic is None:
                harmonic = jnp.zeros((force_const.shape[0], configs), F32)
                displaced = jnp.zeros((rows, configs), BF)
            harmonic = harmonic + jnp.dot(
                force_const[:, base : base + count], block, preferred_element_type=F32
            )
            displaced = lax.dynamic_update_slice_in_dim(displaced, block, base, 0)
        state["harmonic"], state["displaced"] = harmonic, displaced
        return harmonic

    steps, base = [], 0
    for kind, units in PARTS:
        count = rows * units // 36
        steps.append(part_steps(g, piece, kind, base, count, finish))
        next(steps[-1])
        base += count
    assert base == rows
    last = [None]

    def pin(value):
        if last[0] is None:
            return value
        return lax.optimization_barrier((value, last[0]))[0]

    for index in schedule(len(PARTS), 2 * len(g.order(PARTS[0][0]))):
        last[0] = steps[index].send(pin)
    harmonic, displaced = state["harmonic"], state["displaced"]
    for bit in range(bits_of(sizes[0])):
        pairs = [(r, r ^ (1 << bit)) for r in range(sizes[0])]
        got = lax.ppermute(harmonic.astype(BF), "row", pairs)
        if not tiled or bit + 1 < bits_of(sizes[0]):
            harmonic = harmonic + got.astype(F32)
    if tiled:
        return gradient_kernel(forces, harmonic, got, displaced)
    residual = (forces.astype(F32) + harmonic).astype(BF)
    out = lax.dot_general(
        residual, displaced, (((1,), (1,)), ((), ())), preferred_element_type=F32
    )
    return out / jnp.sqrt(F32(configs))


def schedule(parts, steps):
    if len(ORDER) == parts * steps:
        return ORDER
    return [part for _ in range(steps) for part in range(parts)]


def solution(mesh):
    sizes = tuple(mesh.shape[name] for name in MESH)

    def body(*args):
        return local(sizes, *args)

    return jax.shard_map(
        body,
        mesh=mesh,
        in_specs=(
            P("row", ("col", "cfg")),
            P(("col", "cfg"), "row"),
            P(("col", "cfg"), None),
            P(("col", "cfg"), "row"),
            P(("col", "cfg")),
        ),
        out_specs=P(("col", "cfg"), "row"),
        check_vma=False,
    )
```

time: 501 us -> 230 us (0.46)
  the two profiles are of different devices: /device:TPU:0 before, /device:TPU:27 now
where the time goes in v1:
time: 230 us; the launch traced here: 228 us
  Pallas kernels  118 us (51%)
  waiting for transfers between devices  53.7 us (23%)
  starting transfers between devices  36 us (16%)
  other arithmetic  18.6 us (8%)
    pallas_call x20, Pallas kernels, piece_kernel(): pl.pallas_call(kernel, grid_spec=spec, out_shape=shapes, compiler_params=...  62.8 us
    ppermute x35, waiting for transfers between devices, swap(): return lax.ppermute(value, MESH, pairs)  50.2 us
    pallas_call x5, Pallas kernels, finish_kernel(): pl.pallas_call(kernel, grid_spec=spec, out_shape=[jax.ShapeDtypeStruct((r...  30.9 us
    ppermute x35, starting transfers between devices, swap(): return lax.ppermute(value, MESH, pairs)  24.5 us
    pallas_call x1, Pallas kernels, gradient_kernel(): pl.pallas_call(kernel, grid=(columns // tile,), in_specs=[whole, whole, w...  24.1 us
    ppermute x1, starting transfers between devices, local(): got = lax.ppermute(harmonic.astype(BF), 'row', pairs)  11.5 us
    select_n x11, other arithmetic, ordered(): jnp.where(flag == 0, jnp.concatenate([mine, other], axis), jnp.concatenat...  11 us
  transfers between devices with their start and end apart: 37, of which 12 were waited for; matrix products, arithmetic and copies ran while one was open for 7% of the time, Pallas kernels for 37%

profile of v1, /device:TPU:27, one launch (start us, length us, event | category | flops | bytes accessed | tf_op | source)
XLA Modules:
  0.0 228.5 jit_solution(8081898387413275489)
XLA Ops:
  0.7 1.6 multiply_convert_fusion.a
  2.3 3.6 %shard_map.55 = bf16[896,512]{1,0:T(8,128)(2,1)} custom-call(s32[1]{0:T(128)} %bitcast.30.at, bf16[9216,1152]{1,0:T(8,128)(2,1)} %e.39, bf16[1152,512]{1,0:T(8,128)(2,1)S(1)} %multiply_convert_fusion.a), custom_call_target="tpu_custom_call" | custom-call | flops 1056964608 | bytes 2981888 | tf_op jit(solution)/shard_map/pallas_call | solution.py:124
  7.1 3.8 %shard_map.56 = bf16[1024,512]{1,0:T(8,128)(2,1)} custom-call(s32[1]{0:T(128)} %bitcast.29.at, bf16[9216,1152]{1,0:T(8,128)(2,1)} %e.39, bf16[1152,512]{1,0:T(8,128)(2,1)S(1)} %multiply_convert_fusion.a), custom_call_target="tpu_custom_call" | custom-call | flops 1207959552 | bytes 3407872 | tf_op jit(solution)/shard_map/pallas_call | solution.py:124
  11.0 3.5 %shard_map.57 = bf16[896,512]{1,0:T(8,128)(2,1)} custom-call(s32[1]{0:T(128)} %bitcast.28.at, bf16[9216,1152]{1,0:T(8,128)(2,1)} %e.39, bf16[1152,512]{1,0:T(8,128)(2,1)S(1)} %multiply_convert_fusion.a), custom_call_target="tpu_custom_call" | custom-call | flops 1056964608 | bytes 2981888 | tf_op jit(solution)/shard_map/pallas_call | solution.py:124
  14.8 3.8 %shard_map.58 = bf16[1024,512]{1,0:T(8,128)(2,1)} custom-call(s32[1]{0:T(128)} %bitcast.27.at, bf16[9216,1152]{1,0:T(8,128)(2,1)} %e.39, bf16[1152,512]{1,0:T(8,128)(2,1)S(1)} %multiply_convert_fusion.a), custom_call_target="tpu_custom_call" | custom-call | flops 1207959552 | bytes 3407872 | tf_op jit(solution)/shard_map/pallas_call | solution.py:124
  19.8 3.3 %shard_map.59 = bf16[768,512]{1,0:T(8,128)(2,1)} custom-call(s32[1]{0:T(128)} %bitcast.26.at, bf16[9216,1152]{1,0:T(8,128)(2,1)} %e.39, bf16[1152,512]{1,0:T(8,128)(2,1)S(1)} %multiply_convert_fusion.a), custom_call_target="tpu_custom_call" | custom-call | flops 905969664 | bytes 2555904 | tf_op jit(solution)/shard_map/pallas_call | solution.py:124
  23.6 3.6 %shard_map.60 = bf16[448,512]{1,0:T(8,128)(2,1)} custom-call(s32[2]{0:T(128)S(1)} %pad_add_fusion.11.at, bf16[9216,1152]{1,0:T(8,128)(2,1)} %e.39, bf16[1152,512]{1,0:T(8,128)(2,1)S(1)} %multiply_convert_fusion.a, bf16[896,512]{1,0:T(8,128)(2,1)} %collective-permute-done.1.refs_0_), custom_call_target="tpu_custom_call" | custom-call | flops 528482304 | bytes 1490944 | tf_op jit(solution)/shard_map/pallas_call | solution.py:124
  28.5 3.6 %shard_map.61 = bf16[448,512]{1,0:T(8,128)(2,1)} custom-call(s32[2]{0:T(128)S(1)} %pad_add_fusion.10.at, bf16[9216,1152]{1,0:T(8,128)(2,1)} %e.39, bf16[1152,512]{1,0:T(8,128)(2,1)S(1)} %multiply_convert_fusion.a, bf16[896,512]{1,0:T(8,128)(2,1)} %collective-permute-done.2.refs_0_), custom_call_target="tpu_custom_call" | custom-call | flops 528482304 | bytes 1490944 | tf_op jit(solution)/shard_map/pallas_call | solution.py:124
  32.6 3.4 %collective-permute-done.3.refs_0_ = bf16[1024,512]{1,0:T(8,128)(2,1)S(1)} collective-permute-done((bf16[1024,512]{1,0:T(8,128)(2,1)}, bf16[1024,512]{1,0:T(8,128)(2,1)S(1)}, u32[]{:S(2)}, u32[]{:S(2)}) %collective-permute-start.3) | collective-permute-done | bytes 1048608 | tf_op jit(solution)/shard_map/ppermute | solution.py:63
  36.0 3.5 %shard_map.62 = bf16[512,512]{1,0:T(8,128)(2,1)} custom-call(s32[2]{0:T(128)S(1)} %pad_add_fusion.9.at, bf16[9216,1152]{1,0:T(8,128)(2,1)} %e.39, bf16[1152,512]{1,0:T(8,128)(2,1)S(1)} %multiply_convert_fusion.a, bf16[1024,512]{1,0:T(8,128)(2,1)S(1)} %collective-permute-done.3.refs_0_), custom_call_target="tpu_custom_call" | custom-call | flops 603979776 | bytes 1703936 | tf_op jit(solution)/shard_map/pallas_call | solution.py:124
  40.1 3.2 %shard_map.63 = bf16[224,512]{1,0:T(8,128)(2,1)} custom-call(s32[3]{0:T(128)S(1)} %pad_add_fusion.8.at, bf16[9216,1152]{1,0:T(8,128)(2,1)} %e.39, bf16[1152,512]{1,0:T(8,128)(2,1)S(1)} %multiply_convert_fusion.a, bf16[896,512]{1,0:T(8,128)(2,1)} %collective-permute-done.1.refs_0_, bf16[448,512]{1,0:T(8,128)(2,1)} %collective-permute-done.4.refs_1_), custom_call_target="tpu_custom_call" | custom-call | flops 264241152 | bytes 745472 | tf_op jit(solution)/shard_map/pallas_call | solution.py:124
  43.3 1.3 collective-permute-start.7
  44.7 3.5 %shard_map.64 = bf16[512,512]{1,0:T(8,128)(2,1)} custom-call(s32[2]{0:T(128)S(1)} %pad_add_fusion.7.at, bf16[9216,1152]{1,0:T(8,128)(2,1)} %e.39, bf16[1152,512]{1,0:T(8,128)(2,1)S(1)} %multiply_convert_fusion.a, bf16[1024,512]{1,0:T(8,128)(2,1)S(1)} %collective-permute-done.5.refs_0_), custom_call_target="tpu_custom_call" | custom-call | flops 603979776 | bytes 1703936 | tf_op jit(solution)/shard_map/pallas_call | solution.py:124
  48.2 3.2 %shard_map.65 = bf16[224,512]{1,0:T(8,128)(2,1)} custom-call(s32[3]{0:T(128)S(1)} %pad_add_fusion.6.at, bf16[9216,1152]{1,0:T(8,128)(2,1)} %e.39, bf16[1152,512]{1,0:T(8,128)(2,1)S(1)} %multiply_convert_fusion.a, bf16[896,512]{1,0:T(8,128)(2,1)} %collective-permute-done.2.refs_0_, bf16[448,512]{1,0:T(8,128)(2,1)} %collective-permute-done.6.refs_1_), custom_call_target="tpu_custom_call" | custom-call | flops 264241152 | bytes 745472 | tf_op jit(solution)/shard_map/pallas_call | solution.py:124
  51.8 2.6 %shard_map.66 = (bf16[224,512]{1,0:T(8,128)(2,1)S(1)}, f32[224,512]{1,0:T(8,128)S(1)}) custom-call(s32[4]{0:T(128)S(1)} %pad_add_fusion.2.at, bf16[9216,1152]{1,0:T(8,128)(2,1)} %e.39, bf16[1152,512]{1,0:T(8,128)(2,1)S(1)} %multiply_convert_fusion.a, bf16[896,512]{1,0:T(8,128)(2,1)} %collective-permute-done.1.refs_0_, ...), custom_call_target="tpu_custom_call" | custom-call | flops 264241152 | bytes 745472 | tf_op jit(solution)/shard_map/pallas_call | solution.py:124
  54.4 3.4 %shard_map.67 = bf16[384,512]{1,0:T(8,128)(2,1)} custom-call(s32[2]{0:T(128)S(1)} %pad_add_fusion.5.at, bf16[9216,1152]{1,0:T(8,128)(2,1)} %e.39, bf16[1152,512]{1,0:T(8,128)(2,1)S(1)} %multiply_convert_fusion.a, bf16[768,512]{1,0:T(8,128)(2,1)} %collective-permute-done.8.refs_0_), custom_call_target="tpu_custom_call" | custom-call | flops 452984832 | bytes 1277952 | tf_op jit(solution)/shard_map/pallas_call | solution.py:124
  59.4 2.5 %shard_map.68 = (bf16[224,512]{1,0:T(8,128)(2,1)S(1)}, f32[224,512]{1,0:T(8,128)S(1)}) custom-call(s32[4]{0:T(128)S(1)} %pad_add_fusion.3.at, bf16[9216,1152]{1,0:T(8,128)(2,1)} %e.39, bf16[1152,512]{1,0:T(8,128)(2,1)S(1)} %multiply_convert_fusion.a, bf16[896,512]{1,0:T(8,128)(2,1)} %collective-permute-done.2.refs_0_, ...), custom_call_target="tpu_custom_call" | custom-call | flops 264241152 | bytes 745472 | tf_op jit(solution)/shard_map/pallas_call | solution.py:124
  61.9 3.0 %shard_map.69 = bf16[256,512]{1,0:T(8,128)(2,1)} custom-call(s32[3]{0:T(128)S(1)} %add_add_fusion.1.at, bf16[9216,1152]{1,0:T(8,128)(2,1)} %e.39, bf16[1152,512]{1,0:T(8,128)(2,1)S(1)} %multiply_convert_fusion.a, bf16[1024,512]{1,0:T(8,128)(2,1)S(1)} %collective-permute-done.3.refs_0_, bf16[512,512]{1,0:T(8,128)(2,1)} %collective-permute-done.10.refs_1_), custom_call_target="tpu_custom_call" | custom-call | flops 301989888 | bytes 851968 | tf_op jit(solution)/shard_map/pallas_call | solution.py:124
  65.3 2.2 collective-permute-start.16
  67.5 3.0 %shard_map.70 = bf16[192,512]{1,0:T(8,128)(2,1)} custom-call(s32[3]{0:T(128)S(1)} %pad_add_fusion.12.at, bf16[9216,1152]{1,0:T(8,128)(2,1)} %e.39, bf16[1152,512]{1,0:T(8,128)(2,1)S(1)} %multiply_convert_fusion.a, bf16[768,512]{1,0:T(8,128)(2,1)} %collective-permute-done.8.refs_0_, bf16[384,512]{1,0:T(8,128)(2,1)} %collective-permute-done.11.refs_1_), custom_call_target="tpu_custom_call" | custom-call | flops 226492416 | bytes 638976 | tf_op jit(solution)/shard_map/pallas_call | solution.py:124
  70.5 2.3 shard_map.71
  74.1 3.0 %shard_map.72 = (bf16[256,512]{1,0:T(8,128)(2,1)}, f32[256,512]{1,0:T(8,128)S(1)}) custom-call(s32[4]{0:T(128)S(1)} %pad_add_fusion.at, bf16[9216,1152]{1,0:T(8,128)(2,1)} %e.39, bf16[1152,512]{1,0:T(8,128)(2,1)S(1)} %multiply_convert_fusion.a, bf16[1024,512]{1,0:T(8,128)(2,1)S(1)} %collective-permute-done.3.refs_0_, ...), custom_call_target="tpu_custom_call" | custom-call | flops 301989888 | bytes 851968 | tf_op jit(solution)/shard_map/pallas_call | solution.py:124
  77.1 1.9 add_convert_fusion.3
  79.0 2.3 %shard_map.73 = (bf16[256,512]{1,0:T(8,128)(2,1)S(1)}, f32[256,512]{1,0:T(8,128)S(1)}) custom-call(s32[4]{0:T(128)S(1)} %pad_add_fusion.1.at, bf16[9216,1152]{1,0:T(8,128)(2,1)} %e.39, bf16[1152,512]{1,0:T(8,128)(2,1)S(1)} %multiply_convert_fusion.a, bf16[1024,512]{1,0:T(8,128)(2,1)S(1)} %collective-permute-done.5.refs_0_, ...), custom_call_target="tpu_custom_call" | custom-call | flops 301989888 | bytes 851968 | tf_op jit(solution)/shard_map/pallas_call | solution.py:124
  83.8 3.5 %collective-permute-done.17.refs_2_ = bf16[192,512]{1,0:T(8,128)(2,1)S(1)} collective-permute-done((bf16[192,512]{1,0:T(8,128)(2,1)}, bf16[192,512]{1,0:T(8,128)(2,1)S(1)}, u32[]{:S(2)}, u32[]{:S(2)}) %collective-permute-start.17) | collective-permute-done | bytes 196640 | tf_op jit(solution)/shard_map/ppermute | solution.py:63
  87.3 2.4 %shard_map.74 = (bf16[192,512]{1,0:T(8,128)(2,1)S(1)}, f32[192,512]{1,0:T(8,128)S(1)}) custom-call(s32[4]{0:T(128)S(1)} %pad_add_fusion.4.at, bf16[9216,1152]{1,0:T(8,128)(2,1)} %e.39, bf16[1152,512]{1,0:T(8,128)(2,1)S(1)} %multiply_convert_fusion.a, bf16[768,512]{1,0:T(8,128)(2,1)} %collective-permute-done.8.refs_0_, ...), custom_call_target="tpu_custom_call" | custom-call | flops 226492416 | bytes 638976 | tf_op jit(solution)/shard_map/pallas_call | solution.py:124
  90.6 1.7 collective-permute-done.19
  93.5 1.4 maximum_select_fusion.9
  95.4 2.7 %collective-permute-start.24 = (bf16[192,512]{1,0:T(8,128)(2,1)S(1)}, bf16[192,512]{1,0:T(8,128)(2,1)}, u32[]{:S(2)}, u32[]{:S(2)}) collective-permute-start(bf16[192,512]{1,0:T(8,128)(2,1)S(1)} %get-tuple-element.93), channel_id=1, source_target_pairs={{0,2},{1,3},{2,0},{3,1},{4,6},{5,7},{6,4},{7,5},{8,10},{9,11},{10,... | collective-permute-start | bytes 589832 | tf_op jit(solution)/shard_map/ppermute | solution.py:63
  99.1 10.7 %collective-permute-done.22 = bf16[256,512]{1,0:T(8,128)(2,1)S(1)} collective-permute-done((bf16[256,512]{1,0:T(8,128)(2,1)S(1)}, bf16[256,512]{1,0:T(8,128)(2,1)S(1)}, u32[]{:S(2)}, u32[]{:S(2)}) %collective-permute-start.22) | collective-permute-done | bytes 262176 | tf_op jit(solution)/shard_map/ppermute | solution.py:63
  110.3 1.3 collective-permute-start.29
  113.2 1.5 collective-permute-start.28
  114.7 2.7 %collective-permute-done.25 = bf16[256,512]{1,0:T(8,128)(2,1)} collective-permute-done((bf16[256,512]{1,0:T(8,128)(2,1)S(1)}, bf16[256,512]{1,0:T(8,128)(2,1)}, u32[]{:S(2)}, u32[]{:S(2)}) %collective-permute-start.25) | collective-permute-done | bytes 262176 | tf_op jit(solution)/shard_map/ppermute | solution.py:63
  118.6 1.5 collective-permute-start.30
  120.1 4.3 %collective-permute-done.26 = bf16[448,512]{1,0:T(8,128)(2,1)} collective-permute-done((bf16[448,512]{1,0:T(8,128)(2,1)}, bf16[448,512]{1,0:T(8,128)(2,1)}, u32[]{:S(2)}, u32[]{:S(2)}) %collective-permute-start.26) | collective-permute-done | bytes 458784 | tf_op jit(solution)/shard_map/ppermute | solution.py:63
  124.4 1.7 maximum_select_fusion.4.d_mine
  126.7 11.3 %collective-permute-done.27 = bf16[512,512]{1,0:T(8,128)(2,1)S(1)} collective-permute-done((bf16[512,512]{1,0:T(8,128)(2,1)}, bf16[512,512]{1,0:T(8,128)(2,1)S(1)}, u32[]{:S(2)}, u32[]{:S(2)}) %collective-permute-start.27) | collective-permute-done | bytes 524320 | tf_op jit(solution)/shard_map/ppermute | solution.py:63
  138.0 1.6 maximum_select_fusion.1.d_mine
  141.8 6.2 %shard_map.75 = (f32[1152,512]{1,0:T(8,128)S(1)}, bf16[9216,512]{1,0:T(8,128)(2,1)}) custom-call(s32[1]{0:T(128)} %bitcast.at, bf16[1152,9216]{1,0:T(8,128)(2,1)} %k_other.9, bf16[1152,9216]{1,0:T(8,128)(2,1)} %k_other.9, bf16[896,512]{1,0:T(8,128)(2,1)S(1)} %maximum_select_fusion.3.d_mine, bf16[896,512]{1,0:T(8,128)(2,1)S(1)} %copy-done.1), custom_call_target="tpu_custom_call" | custom-call | flops 2113929216 | bytes 4128768 | tf_op jit(solution)/shard_map/pallas_call | solution.py:170
  150.0 10.9 %collective-permute-done.31 = bf16[384,512]{1,0:T(8,128)(2,1)S(1)} collective-permute-done((bf16[384,512]{1,0:T(8,128)(2,1)S(1)}, bf16[384,512]{1,0:T(8,128)(2,1)S(1)}, u32[]{:S(2)}, u32[]{:S(2)}) %collective-permute-start.31) | collective-permute-done | bytes 393248 | tf_op jit(solution)/shard_map/ppermute | solution.py:63
  161.6 6.2 %shard_map.76 = (f32[1152,512]{1,0:T(8,128)S(1)}, bf16[9216,512]{1,0:T(8,128)(2,1)}) custom-call(s32[1]{0:T(128)} %bitcast.at, bf16[1152,9216]{1,0:T(8,128)(2,1)} %k_other.9, bf16[1152,9216]{1,0:T(8,128)(2,1)} %k_other.9, bf16[896,512]{1,0:T(8,128)(2,1)S(1)} %maximum_select_fusion.4.d_mine, ...), custom_call_target="tpu_custom_call", output_to_operand_aliasing={{0}: (5, {}), {1}: (6, {})} | custom-call | flops 2113929216 | bytes 4128768 | tf_op jit(solution)/shard_map/pallas_call | solution.py:170
  167.8 6.5 %shard_map.77 = (f32[1152,512]{1,0:T(8,128)S(1)}, bf16[9216,512]{1,0:T(8,128)(2,1)}) custom-call(s32[1]{0:T(128)} %bitcast.at, bf16[1152,9216]{1,0:T(8,128)(2,1)} %k_other.9, bf16[1152,9216]{1,0:T(8,128)(2,1)} %k_other.9, bf16[1024,512]{1,0:T(8,128)(2,1)S(1)} %maximum_select_fusion.2.d_mine, ...), custom_call_target="tpu_custom_call", output_to_operand_aliasing={{0}: (5, {}), {1}: (6, {})} | custom-call | flops 2415919104 | bytes 4718592 | tf_op jit(solution)/shard_map/pallas_call | solution.py:170
  174.3 6.4 %shard_map.78 = (f32[1152,512]{1,0:T(8,128)S(1)}, bf16[9216,512]{1,0:T(8,128)(2,1)}) custom-call(s32[1]{0:T(128)} %bitcast.44.at, bf16[1152,9216]{1,0:T(8,128)(2,1)} %k_other.9, bf16[1152,9216]{1,0:T(8,128)(2,1)} %k_other.9, bf16[1024,512]{1,0:T(8,128)(2,1)S(1)} %maximum_select_fusion.1.d_mine, ...), custom_call_target="tpu_custom_call", output_to_operand_aliasing={{0}: (5, {}), {1}: (6, {})} | custom-call | flops 2415919104 | bytes 4718592 | tf_op jit(solution)/shard_map/pallas_call | solution.py:170
  180.8 5.6 %shard_map.79 = (f32[1152,512]{1,0:T(8,128)S(1)}, bf16[9216,512]{1,0:T(8,128)(2,1)}) custom-call(s32[1]{0:T(128)} %bitcast.at, bf16[1152,9216]{1,0:T(8,128)(2,1)} %k_other.9, bf16[1152,9216]{1,0:T(8,128)(2,1)} %k_other.9, bf16[768,512]{1,0:T(8,128)(2,1)S(1)} %maximum_select_fusion.5.d_mine, ...), custom_call_target="tpu_custom_call", output_to_operand_aliasing={{0}: (5, {}), {1}: (6, {})} | custom-call | flops 1811939328 | bytes 3538944 | tf_op jit(solution)/shard_map/pallas_call | solution.py:170
  187.5 11.5 %collective-permute-start.36 = (bf16[1152,512]{1,0:T(8,128)(2,1)}, bf16[1152,512]{1,0:T(8,128)(2,1)S(1)}, u32[]{:S(2)}, u32[]{:S(2)}) collective-permute-start(bf16[1152,512]{1,0:T(8,128)(2,1)} %convert_element_type.51), channel_id=1, source_target_pairs={{0,16},{16,0},{1,17},{17,1},{2,18},{18,2},{3,19},{19,3},{4,20},{20... | collective-permute-start | bytes 3538952 | tf_op jit(solution)/shard_map/ppermute | solution.py:299
  199.0 3.5 %collective-permute-done = bf16[1152,256]{1,0:T(8,128)(2,1)} collective-permute-done((bf16[1152,256]{1,0:T(8,128)(2,1)}, bf16[1152,256]{1,0:T(8,128)(2,1)}, u32[]{:S(2)}, u32[]{:S(2)}) %collective-permute-start) | collective-permute-done | bytes 589856 | tf_op jit(solution)/shard_map/ppermute | solution.py:258
  202.5 1.9 maximum_select_fusion.f
  204.4 24.1 %shard_map.80 = f32[1152,9216]{1,0:T(8,128)} custom-call(bf16[1152,512]{1,0:T(8,128)(2,1)S(1)} %maximum_select_fusion.f, f32[1152,512]{1,0:T(8,128)S(1)} %get-tuple-element.121.h, bf16[1152,512]{1,0:T(8,128)(2,1)S(1)} %collective-permute-done.36.g, bf16[9216,512]{1,0:T(8,128)(2,1)} %get-tuple-element.122.d), custom_call_target="tpu_custom_call" | custom-call | flops 10871635968 | bytes 42467328 | tf_op jit(solution)/shard_map/pallas_call | solution.py:201
  (106 shorter events, 26.5 us)
Async XLA Ops:
  5.9 17.8 %collective-permute-start.1 = (bf16[896,512]{1,0:T(8,128)(2,1)}, bf16[896,512]{1,0:T(8,128)(2,1)}, u32[]{:S(2)}, u32[]{:S(2)}) collective-permute-start(bf16[896,512]{1,0:T(8,128)(2,1)} %shard_map.55), channel_id=1, source_target_pairs={{0,4},{1,5},{2,6},{3,7},{4,0},{5,1},{6,2},{7,3},{8,12},{9,13},{10,... | collective-permute-start | bytes 2752520 | tf_op jit(solution)/shard_map/ppermute | solution.py:63
  10.9 25.1 %collective-permute-start.3 = (bf16[1024,512]{1,0:T(8,128)(2,1)}, bf16[1024,512]{1,0:T(8,128)(2,1)S(1)}, u32[]{:S(2)}, u32[]{:S(2)}) collective-permute-start(bf16[1024,512]{1,0:T(8,128)(2,1)} %shard_map.56), channel_id=1, source_target_pairs={{0,1},{1,0},{2,3},{3,2},{4,5},{5,4},{6,7},{7,6},{8,9},{9,8},{10,11... | collective-permute-start | bytes 3145736 | tf_op jit(solution)/shard_map/ppermute | solution.py:63
  14.6 14.0 %collective-permute-start.2 = (bf16[896,512]{1,0:T(8,128)(2,1)}, bf16[896,512]{1,0:T(8,128)(2,1)}, u32[]{:S(2)}, u32[]{:S(2)}) collective-permute-start(bf16[896,512]{1,0:T(8,128)(2,1)} %shard_map.57), channel_id=1, source_target_pairs={{0,4},{1,5},{2,6},{3,7},{4,0},{5,1},{6,2},{7,3},{8,12},{9,13},{10,... | collective-permute-start | bytes 2752520 | tf_op jit(solution)/shard_map/ppermute | solution.py:63
  18.6 26.2 %collective-permute-start.5 = (bf16[1024,512]{1,0:T(8,128)(2,1)}, bf16[1024,512]{1,0:T(8,128)(2,1)S(1)}, u32[]{:S(2)}, u32[]{:S(2)}) collective-permute-start(bf16[1024,512]{1,0:T(8,128)(2,1)} %shard_map.58), channel_id=1, source_target_pairs={{0,4},{1,5},{2,6},{3,7},{4,0},{5,1},{6,2},{7,3},{8,12},{9,13},{10,... | collective-permute-start | bytes 3145736 | tf_op jit(solution)/shard_map/ppermute | solution.py:63
  23.1 31.3 %collective-permute-start.8 = (bf16[768,512]{1,0:T(8,128)(2,1)}, bf16[768,512]{1,0:T(8,128)(2,1)}, u32[]{:S(2)}, u32[]{:S(2)}) collective-permute-start(bf16[768,512]{1,0:T(8,128)(2,1)} %shard_map.59), channel_id=1, source_target_pairs={{0,4},{1,5},{2,6},{3,7},{4,0},{5,1},{6,2},{7,3},{8,12},{9,13},{10,... | collective-permute-start | bytes 2359304 | tf_op jit(solution)/shard_map/ppermute | solution.py:63
  27.2 12.9 %collective-permute-start.4 = (bf16[448,512]{1,0:T(8,128)(2,1)}, bf16[448,512]{1,0:T(8,128)(2,1)}, u32[]{:S(2)}, u32[]{:S(2)}) collective-permute-start(bf16[448,512]{1,0:T(8,128)(2,1)} %shard_map.60), channel_id=1, source_target_pairs={{0,8},{1,9},{2,10},{3,11},{4,12},{5,13},{6,14},{7,15},{8,0},{9,1},... | collective-permute-start | bytes 1376264 | tf_op jit(solution)/shard_map/ppermute | solution.py:63
  32.1 16.1 %collective-permute-start.6 = (bf16[448,512]{1,0:T(8,128)(2,1)}, bf16[448,512]{1,0:T(8,128)(2,1)}, u32[]{:S(2)}, u32[]{:S(2)}) collective-permute-start(bf16[448,512]{1,0:T(8,128)(2,1)} %shard_map.61), channel_id=1, source_target_pairs={{0,1},{1,0},{2,3},{3,2},{4,5},{5,4},{6,7},{7,6},{8,9},{9,8},{10,11... | collective-permute-start | bytes 1376264 | tf_op jit(solution)/shard_map/ppermute | solution.py:63
  39.5 22.5 %collective-permute-start.10 = (bf16[512,512]{1,0:T(8,128)(2,1)}, bf16[512,512]{1,0:T(8,128)(2,1)}, u32[]{:S(2)}, u32[]{:S(2)}) collective-permute-start(bf16[512,512]{1,0:T(8,128)(2,1)} %shard_map.62), channel_id=1, source_target_pairs={{0,4},{1,5},{2,6},{3,7},{4,0},{5,1},{6,2},{7,3},{8,12},{9,13},{10,... | collective-permute-start | bytes 1572872 | tf_op jit(solution)/shard_map/ppermute | solution.py:63
  43.3 8.5 %collective-permute-start.7 = (bf16[224,512]{1,0:T(8,128)(2,1)}, bf16[224,512]{1,0:T(8,128)(2,1)}, u32[]{:S(2)}, u32[]{:S(2)}) collective-permute-start(bf16[224,512]{1,0:T(8,128)(2,1)} %shard_map.63), channel_id=1, source_target_pairs={{0,1},{1,0},{2,3},{3,2},{4,5},{5,4},{6,7},{7,6},{8,9},{9,8},{10,11... | collective-permute-start | bytes 688136 | tf_op jit(solution)/shard_map/ppermute | solution.py:63
  51.4 8.0 %collective-permute-start.9 = (bf16[224,512]{1,0:T(8,128)(2,1)}, bf16[224,512]{1,0:T(8,128)(2,1)S(1)}, u32[]{:S(2)}, u32[]{:S(2)}) collective-permute-start(bf16[224,512]{1,0:T(8,128)(2,1)} %shard_map.65), channel_id=1, source_target_pairs={{0,8},{1,9},{2,10},{3,11},{4,12},{5,13},{6,14},{7,15},{8,0},{9,1},... | collective-permute-start | bytes 688136 | tf_op jit(solution)/shard_map/ppermute | solution.py:63
  51.6 18.9 %collective-permute-start.12 = (bf16[512,512]{1,0:T(8,128)(2,1)}, bf16[512,512]{1,0:T(8,128)(2,1)}, u32[]{:S(2)}, u32[]{:S(2)}) collective-permute-start(bf16[512,512]{1,0:T(8,128)(2,1)} %shard_map.64), channel_id=1, source_target_pairs={{0,1},{1,0},{2,3},{3,2},{4,5},{5,4},{6,7},{7,6},{8,9},{9,8},{10,11... | collective-permute-start | bytes 1572872 | tf_op jit(solution)/shard_map/ppermute | solution.py:63
  54.4 3.4 %copy-start.4 = (f32[224,512]{1,0:T(8,128)}, f32[224,512]{1,0:T(8,128)S(1)}, u32[]{:S(2)}) copy-start(f32[224,512]{1,0:T(8,128)S(1)} %get-tuple-element.86) | copy-start | bytes 1376260
  54.4 3.4 %copy-start.8 = (bf16[224,512]{1,0:T(8,128)(2,1)}, bf16[224,512]{1,0:T(8,128)(2,1)S(1)}, u32[]{:S(2)}) copy-start(bf16[224,512]{1,0:T(8,128)(2,1)S(1)} %get-tuple-element.75) | copy-start | bytes 688132
  57.8 9.7 %collective-permute-start.11 = (bf16[384,512]{1,0:T(8,128)(2,1)}, bf16[384,512]{1,0:T(8,128)(2,1)}, u32[]{:S(2)}, u32[]{:S(2)}) collective-permute-start(bf16[384,512]{1,0:T(8,128)(2,1)} %shard_map.67), channel_id=1, source_target_pairs={{0,8},{1,9},{2,10},{3,11},{4,12},{5,13},{6,14},{7,15},{8,0},{9,1},... | collective-permute-start | bytes 1179656 | tf_op jit(solution)/shard_map/ppermute | solution.py:63
  59.2 17.9 %collective-permute-start.14 = (bf16[224,512]{1,0:T(8,128)(2,1)}, bf16[224,512]{1,0:T(8,128)(2,1)}, u32[]{:S(2)}, u32[]{:S(2)}) collective-permute-start(bf16[224,512]{1,0:T(8,128)(2,1)} %copy-done.8), channel_id=1, source_target_pairs={{0,2},{1,3},{2,0},{3,1},{4,6},{5,7},{6,4},{7,5},{8,10},{9,11},{10,... | collective-permute-start | bytes 688136 | tf_op jit(solution)/shard_map/ppermute | solution.py:63
  61.9 3.0 %copy-start.6 = (f32[224,512]{1,0:T(8,128)}, f32[224,512]{1,0:T(8,128)S(1)}, u32[]{:S(2)}) copy-start(f32[224,512]{1,0:T(8,128)S(1)} %get-tuple-element.89) | copy-start | bytes 1376260
  61.9 3.0 %copy-start.9 = (bf16[224,512]{1,0:T(8,128)(2,1)}, bf16[224,512]{1,0:T(8,128)(2,1)S(1)}, u32[]{:S(2)}) copy-start(bf16[224,512]{1,0:T(8,128)(2,1)S(1)} %get-tuple-element.80) | copy-start | bytes 688132
  64.9 9.2 %collective-permute-start.13 = (bf16[256,512]{1,0:T(8,128)(2,1)}, bf16[256,512]{1,0:T(8,128)(2,1)S(1)}, u32[]{:S(2)}, u32[]{:S(2)}) collective-permute-start(bf16[256,512]{1,0:T(8,128)(2,1)} %shard_map.69), channel_id=1, source_target_pairs={{0,8},{1,9},{2,10},{3,11},{4,12},{5,13},{6,14},{7,15},{8,0},{9,1},... | collective-permute-start | bytes 786440 | tf_op jit(solution)/shard_map/ppermute | solution.py:63
  65.3 16.0 %collective-permute-start.16 = (bf16[224,512]{1,0:T(8,128)(2,1)}, bf16[224,512]{1,0:T(8,128)(2,1)S(1)}, u32[]{:S(2)}, u32[]{:S(2)}) collective-permute-start(bf16[224,512]{1,0:T(8,128)(2,1)} %copy-done.9), channel_id=1, source_target_pairs={{0,2},{1,3},{2,0},{3,1},{4,6},{5,7},{6,4},{7,5},{8,10},{9,11},{10,... | collective-permute-start | bytes 688136 | tf_op jit(solution)/shard_map/ppermute | solution.py:63
  72.8 4.3 %copy-start.5 = (f32[224,512]{1,0:T(8,128)S(1)}, f32[224,512]{1,0:T(8,128)}, u32[]{:S(2)}) copy-start(f32[224,512]{1,0:T(8,128)} %copy-done.4) | copy-start | bytes 1376260
  72.8 6.2 %collective-permute-start.15 = (bf16[256,512]{1,0:T(8,128)(2,1)S(1)}, bf16[256,512]{1,0:T(8,128)(2,1)S(1)}, u32[]{:S(2)}, u32[]{:S(2)}) collective-permute-start(bf16[256,512]{1,0:T(8,128)(2,1)S(1)} %shard_map.71), channel_id=1, source_target_pairs={{0,8},{1,9},{2,10},{3,11},{4,12},{5,13},{6,14},{7,15},{8,0},{9,1},... | collective-permute-start | bytes 786440 | tf_op jit(solution)/shard_map/ppermute | solution.py:63
  77.1 4.2 %copy-start.2 = (f32[256,512]{1,0:T(8,128)}, f32[256,512]{1,0:T(8,128)S(1)}, u32[]{:S(2)}) copy-start(f32[256,512]{1,0:T(8,128)S(1)} %get-tuple-element.95) | copy-start | bytes 1572868
  79.0 2.3 %copy-start.7 = (f32[224,512]{1,0:T(8,128)S(1)}, f32[224,512]{1,0:T(8,128)}, u32[]{:S(2)}) copy-start(f32[224,512]{1,0:T(8,128)} %copy-done.6) | copy-start | bytes 1376260
  81.4 8.3 %collective-permute-start.18 = (bf16[224,512]{1,0:T(8,128)(2,1)S(1)}, bf16[224,512]{1,0:T(8,128)(2,1)S(1)}, u32[]{:S(2)}, u32[]{:S(2)}) collective-permute-start(bf16[224,512]{1,0:T(8,128)(2,1)S(1)} %add_convert_fusion.2), channel_id=1, source_target_pairs={{0,8},{1,9},{2,10},{3,11},{4,12},{5,13},{6,14},{7,15},{8,0},{9,1},... | collective-permute-start | bytes 688136 | tf_op jit(solution)/shard_map/ppermute | solution.py:63
  82.2 5.1 %collective-permute-start.17 = (bf16[192,512]{1,0:T(8,128)(2,1)}, bf16[192,512]{1,0:T(8,128)(2,1)S(1)}, u32[]{:S(2)}, u32[]{:S(2)}) collective-permute-start(bf16[192,512]{1,0:T(8,128)(2,1)} %shard_map.70), channel_id=1, source_target_pairs={{0,1},{1,0},{2,3},{3,2},{4,5},{5,4},{6,7},{7,6},{8,9},{9,8},{10,11... | collective-permute-start | bytes 589832 | tf_op jit(solution)/shard_map/ppermute | solution.py:63
  83.1 9.2 %collective-permute-start.19 = (bf16[256,512]{1,0:T(8,128)(2,1)}, bf16[256,512]{1,0:T(8,128)(2,1)S(1)}, u32[]{:S(2)}, u32[]{:S(2)}) collective-permute-start(bf16[256,512]{1,0:T(8,128)(2,1)} %get-tuple-element.85), channel_id=1, source_target_pairs={{0,2},{1,3},{2,0},{3,1},{4,6},{5,7},{6,4},{7,5},{8,10},{9,11},{10,... | collective-permute-start | bytes 786440 | tf_op jit(solution)/shard_map/ppermute | solution.py:63
  83.2 9.1 %copy-start.3 = (f32[256,512]{1,0:T(8,128)S(1)}, f32[256,512]{1,0:T(8,128)}, u32[]{:S(2)}) copy-start(f32[256,512]{1,0:T(8,128)} %copy-done.2) | copy-start | bytes 1572868
  83.2 10.3 %collective-permute-start.20 = (bf16[224,512]{1,0:T(8,128)(2,1)}, bf16[224,512]{1,0:T(8,128)(2,1)}, u32[]{:S(2)}, u32[]{:S(2)}) collective-permute-start(bf16[224,512]{1,0:T(8,128)(2,1)} %add_convert_fusion.3), channel_id=1, source_target_pairs={{0,1},{1,0},{2,3},{3,2},{4,5},{5,4},{6,7},{7,6},{8,9},{9,8},{10,11... | collective-permute-start | bytes 688136 | tf_op jit(solution)/shard_map/ppermute | solution.py:63
  92.4 5.7 %collective-permute-start.21 = (bf16[256,512]{1,0:T(8,128)(2,1)S(1)}, bf16[256,512]{1,0:T(8,128)(2,1)S(1)}, u32[]{:S(2)}, u32[]{:S(2)}) collective-permute-start(bf16[256,512]{1,0:T(8,128)(2,1)S(1)} %add_convert_fusion.1), channel_id=1, source_target_pairs={{0,8},{1,9},{2,10},{3,11},{4,12},{5,13},{6,14},{7,15},{8,0},{9,1},... | collective-permute-start | bytes 786440 | tf_op jit(solution)/shard_map/ppermute | solution.py:63
  93.5 16.4 %collective-permute-start.22 = (bf16[256,512]{1,0:T(8,128)(2,1)S(1)}, bf16[256,512]{1,0:T(8,128)(2,1)S(1)}, u32[]{:S(2)}, u32[]{:S(2)}) collective-permute-start(bf16[256,512]{1,0:T(8,128)(2,1)S(1)} %get-tuple-element.88), channel_id=1, source_target_pairs={{0,2},{1,3},{2,0},{3,1},{4,6},{5,7},{6,4},{7,5},{8,10},{9,11},{10,... | collective-permute-start | bytes 786440 | tf_op jit(solution)/shard_map/ppermute | solution.py:63
  94.9 15.0 %collective-permute-start.23 = (bf16[448,512]{1,0:T(8,128)(2,1)S(1)}, bf16[448,512]{1,0:T(8,128)(2,1)S(1)}, u32[]{:S(2)}, u32[]{:S(2)}) collective-permute-start(bf16[448,512]{1,0:T(8,128)(2,1)S(1)} %maximum_select_fusion.9), channel_id=1, source_target_pairs={{0,8},{1,9},{2,10},{3,11},{4,12},{5,13},{6,14},{7,15},{8,0},{9,1},... | collective-permute-start | bytes 1376264 | tf_op jit(solution)/shard_map/ppermute | solution.py:63
  95.4 16.8 %collective-permute-start.24 = (bf16[192,512]{1,0:T(8,128)(2,1)S(1)}, bf16[192,512]{1,0:T(8,128)(2,1)}, u32[]{:S(2)}, u32[]{:S(2)}) collective-permute-start(bf16[192,512]{1,0:T(8,128)(2,1)S(1)} %get-tuple-element.93), channel_id=1, source_target_pairs={{0,2},{1,3},{2,0},{3,1},{4,6},{5,7},{6,4},{7,5},{8,10},{9,11},{10,... | collective-permute-start | bytes 589832 | tf_op jit(solution)/shard_map/ppermute | solution.py:63
  110.3 29.4 %collective-permute-start.29 = (bf16[896,512]{1,0:T(8,128)(2,1)S(1)}, bf16[896,512]{1,0:T(8,128)(2,1)S(1)}, u32[]{:S(2)}, u32[]{:S(2)}) collective-permute-start(bf16[896,512]{1,0:T(8,128)(2,1)S(1)} %maximum_select_fusion.3.d_mine), channel_id=1, source_target_pairs={{0,4},{1,5},{2,6},{3,7},{4,0},{5,1},{6,2},{7,3},{8,12},{9,13},{10,... | collective-permute-start | bytes 2752520 | tf_op jit(solution)/shard_map/ppermute | solution.py:63
  111.6 12.8 %collective-permute-start.26 = (bf16[448,512]{1,0:T(8,128)(2,1)}, bf16[448,512]{1,0:T(8,128)(2,1)}, u32[]{:S(2)}, u32[]{:S(2)}) collective-permute-start(bf16[448,512]{1,0:T(8,128)(2,1)} %maximum_select_fusion.8), channel_id=1, source_target_pairs={{0,1},{1,0},{2,3},{3,2},{4,5},{5,4},{6,7},{7,6},{8,9},{9,8},{10,11... | collective-permute-start | bytes 1376264 | tf_op jit(solution)/shard_map/ppermute | solution.py:63
  111.6 26.4 %collective-permute-start.27 = (bf16[512,512]{1,0:T(8,128)(2,1)}, bf16[512,512]{1,0:T(8,128)(2,1)S(1)}, u32[]{:S(2)}, u32[]{:S(2)}) collective-permute-start(bf16[512,512]{1,0:T(8,128)(2,1)} %maximum_select_fusion.6), channel_id=1, source_target_pairs={{0,4},{1,5},{2,6},{3,7},{4,0},{5,1},{6,2},{7,3},{8,12},{9,13},{10,... | collective-permute-start | bytes 1572872 | tf_op jit(solution)/shard_map/ppermute | solution.py:63
  111.9 5.5 %collective-permute-start.25 = (bf16[256,512]{1,0:T(8,128)(2,1)S(1)}, bf16[256,512]{1,0:T(8,128)(2,1)}, u32[]{:S(2)}, u32[]{:S(2)}) collective-permute-start(bf16[256,512]{1,0:T(8,128)(2,1)S(1)} %add_convert_fusion), channel_id=1, source_target_pairs={{0,8},{1,9},{2,10},{3,11},{4,12},{5,13},{6,14},{7,15},{8,0},{9,1},... | collective-permute-start | bytes 786440 | tf_op jit(solution)/shard_map/ppermute | solution.py:63
  113.2 26.4 %collective-permute-start.28 = (bf16[192,512]{1,0:T(8,128)(2,1)S(1)}, bf16[192,512]{1,0:T(8,128)(2,1)S(1)}, u32[]{:S(2)}, u32[]{:S(2)}) collective-permute-start(bf16[192,512]{1,0:T(8,128)(2,1)S(1)} %add_convert_fusion.4), channel_id=1, source_target_pairs={{0,1},{1,0},{2,3},{3,2},{4,5},{5,4},{6,7},{7,6},{8,9},{9,8},{10,11... | collective-permute-start | bytes 589832 | tf_op jit(solution)/shard_map/ppermute | solution.py:63
  118.6 29.4 %collective-permute-start.30 = (bf16[512,512]{1,0:T(8,128)(2,1)S(1)}, bf16[512,512]{1,0:T(8,128)(2,1)S(1)}, u32[]{:S(2)}, u32[]{:S(2)}) collective-permute-start(bf16[512,512]{1,0:T(8,128)(2,1)S(1)} %maximum_select_fusion.7), channel_id=1, source_target_pairs={{0,1},{1,0},{2,3},{3,2},{4,5},{5,4},{6,7},{7,6},{8,9},{9,8},{10,11... | collective-permute-start | bytes 1572872 | tf_op jit(solution)/shard_map/ppermute | solution.py:63
  126.1 35.5 %collective-permute-start.32 = (bf16[896,512]{1,0:T(8,128)(2,1)S(1)}, bf16[896,512]{1,0:T(8,128)(2,1)S(1)}, u32[]{:S(2)}, u32[]{:S(2)}) collective-permute-start(bf16[896,512]{1,0:T(8,128)(2,1)S(1)} %maximum_select_fusion.4.d_mine), channel_id=1, source_target_pairs={{0,4},{1,5},{2,6},{3,7},{4,0},{5,1},{6,2},{7,3},{8,12},{9,13},{10,... | collective-permute-start | bytes 2752520 | tf_op jit(solution)/shard_map/ppermute | solution.py:63
  139.7 0.9 copy-start
  140.7 1.2 copy-start.1
  148.5 19.4 %collective-permute-start.33 = (bf16[1024,512]{1,0:T(8,128)(2,1)S(1)}, bf16[1024,512]{1,0:T(8,128)(2,1)S(1)}, u32[]{:S(2)}, u32[]{:S(2)}) collective-permute-start(bf16[1024,512]{1,0:T(8,128)(2,1)S(1)} %maximum_select_fusion.2.d_mine), channel_id=1, source_target_pairs={{0,4},{1,5},{2,6},{3,7},{4,0},{5,1},{6,2},{7,3},{8,12},{9,13},{10,... | collective-permute-start | bytes 3145736 | tf_op jit(solution)/shard_map/ppermute | solution.py:63
  149.7 11.2 %collective-permute-start.31 = (bf16[384,512]{1,0:T(8,128)(2,1)S(1)}, bf16[384,512]{1,0:T(8,128)(2,1)S(1)}, u32[]{:S(2)}, u32[]{:S(2)}) collective-permute-start(bf16[384,512]{1,0:T(8,128)(2,1)S(1)} %maximum_select_fusion.10), channel_id=1, source_target_pairs={{0,8},{1,9},{2,10},{3,11},{4,12},{5,13},{6,14},{7,15},{8,0},{9,1},... | collective-permute-start | bytes 1179656 | tf_op jit(solution)/shard_map/ppermute | solution.py:63
  150.0 24.4 %collective-permute-start.34 = (bf16[1024,512]{1,0:T(8,128)(2,1)S(1)}, bf16[1024,512]{1,0:T(8,128)(2,1)S(1)}, u32[]{:S(2)}, u32[]{:S(2)}) collective-permute-start(bf16[1024,512]{1,0:T(8,128)(2,1)S(1)} %maximum_select_fusion.1.d_mine), channel_id=1, source_target_pairs={{0,1},{1,0},{2,3},{3,2},{4,5},{5,4},{6,7},{7,6},{8,9},{9,8},{10,11... | collective-permute-start | bytes 3145736 | tf_op jit(solution)/shard_map/ppermute | solution.py:63
  161.2 19.6 %collective-permute-start.35 = (bf16[768,512]{1,0:T(8,128)(2,1)S(1)}, bf16[768,512]{1,0:T(8,128)(2,1)S(1)}, u32[]{:S(2)}, u32[]{:S(2)}) collective-permute-start(bf16[768,512]{1,0:T(8,128)(2,1)S(1)} %maximum_select_fusion.5.d_mine), channel_id=1, source_target_pairs={{0,4},{1,5},{2,6},{3,7},{4,0},{5,1},{6,2},{7,3},{8,12},{9,13},{10,... | collective-permute-start | bytes 2359304 | tf_op jit(solution)/shard_map/ppermute | solution.py:63
  187.5 16.9 %collective-permute-start.36 = (bf16[1152,512]{1,0:T(8,128)(2,1)}, bf16[1152,512]{1,0:T(8,128)(2,1)S(1)}, u32[]{:S(2)}, u32[]{:S(2)}) collective-permute-start(bf16[1152,512]{1,0:T(8,128)(2,1)} %convert_element_type.51), channel_id=1, source_target_pairs={{0,16},{16,0},{1,17},{17,1},{2,18},{18,2},{3,19},{19,3},{4,20},{20... | collective-permute-start | bytes 3538952 | tf_op jit(solution)/shard_map/ppermute | solution.py:299
  199.0 3.5 %collective-permute-start = (bf16[1152,256]{1,0:T(8,128)(2,1)}, bf16[1152,256]{1,0:T(8,128)(2,1)}, u32[]{:S(2)}, u32[]{:S(2)}) collective-permute-start(bf16[1152,256]{1,0:T(8,128)(2,1)} %param.8), channel_id=1, source_target_pairs={{0,16},{16,0},{1,17},{17,1},{2,18},{18,2},{3,19},{19,3},{4,20},{20... | collective-permute-start | bytes 1769480 | tf_op jit(solution)/shard_map/ppermute | solution.py:258

commit v2 on v1

v2 whole, which is shorter than its diff:
```python
import jax
import jax.numpy as jnp
from jax import lax
from jax.experimental import pallas as pl
from jax.experimental.pallas import tpu as pltpu
from jax.sharding import PartitionSpec as P

BF = jnp.bfloat16
F32 = jnp.float32
MESH = ("row", "col", "cfg")
PARTS = (("abpq", 7), ("apbq", 8), ("abpq", 6), ("pabq", 8), ("apbq", 7))
ORDER = (
    (0, 3, 1, 4, 2, 0, 1, 3, 0, 4, 1, 0, 2, 1, 3, 2, 4, 3, 0, 4,)
    + (1, 2, 1, 0, 3, 0, 4, 3, 2, 4, 1, 0, 2, 3, 4, 2, 1, 4, 3, 2,)
)


def bits_of(size):
    assert size & (size - 1) == 0
    return size.bit_length() - 1


class Grid:
    def __init__(self, sizes):
        self.sizes = sizes
        self.at = tuple(lax.axis_index(name) for name in MESH)
        self.flip = self.at[0] & 1

    def order(self, kind):
        levels = []
        for letter in kind:
            axis = 1 if letter in "ab" else 2
            first = 0 if letter in "ap" else 1
            stop = first + 1 if first == 0 else bits_of(self.sizes[axis])
            levels += [(axis, bit) for bit in range(first, stop)]
        return levels

    def mask(self, level, flip):
        axis, bit = level
        if axis == 2:
            return 0, 1 << bit
        bits = bits_of(self.sizes[1])
        return (1 << (bits - 1 - bit) if flip else 1 << bit), 0

    def mine(self, level):
        axis, bit = level
        if axis == 2:
            return (self.at[2] >> bit) & 1
        bits = bits_of(self.sizes[1])
        return (self.at[1] >> jnp.where(self.flip == 1, bits - 1 - bit, bit)) & 1

    def swap(self, value, level):
        nrow, ncol, ncfg = self.sizes
        pairs = []
        for r in range(nrow):
            dc, dz = self.mask(level, r & 1)
            for c in range(ncol):
                for z in range(ncfg):
                    pairs.append(
                        ((r * ncol + c) * ncfg + z, (r * ncol + (c ^ dc)) * ncfg + (z ^ dz))
                    )
        return lax.ppermute(value, MESH, pairs)


def rows_of(value, start, size):
    return lax.dynamic_slice_in_dim(value, start, size, 0)


def ordered(flag, mine, other, axis=0):
    return jnp.where(
        flag == 0,
        jnp.concatenate([mine, other], axis),
        jnp.concatenate([other, mine], axis),
    )


def tiles_of(size, most, whole):
    count = -(-size // most)
    length = -(-size // (count * whole)) * whole
    return [(at, min(length, size - at)) for at in range(0, size, length)]


def params(mib):
    return pltpu.CompilerParams(vmem_limit_bytes=mib * 1024 * 1024)


def cost(flops, moved):
    return pl.CostEstimate(flops=flops, bytes_accessed=moved, transcendentals=0)


def scalars(values):
    return jnp.stack([jnp.asarray(value, jnp.int32) for value in values])


IN_SMEM = pl.BlockSpec(memory_space=pltpu.SMEM)
IN_VMEM = pl.BlockSpec(memory_space=pltpu.VMEM)
ANYWHERE = pl.BlockSpec(memory_space=pl.ANY)


def finish_kernel(force_const, harmonic, mine, other, base, flag, final):
    half, configs = mine.shape
    rows = force_const.shape[0]
    first = harmonic is None
    chunks = tiles_of(half, 512, 128)
    loads = [(side, start, length) for side in (0, 1) for start, length in chunks]

    def kernel(at, k, d_mine, d_other, *refs):
        total, (held, block, sem, d_sem) = refs[1 - first], refs[-4:]
        copies, blocks = [], []
        for side, source in enumerate((d_mine, d_other)):
            blocks.append(pltpu.make_async_copy(source, block.at[side], d_sem.at[side]))
        for index, (side, start, length) in enumerate(loads):
            which = at[0] if side == 0 else 1 - at[0]
            column = pl.multiple_of(base + which * half + start, 128)
            copies.append(
                pltpu.make_async_copy(
                    k.at[:, pl.ds(column, length)],
                    held.at[:, pl.ds(side * half + start, length)],
                    sem.at[index],
                )
            )
        for copy in [blocks[0], copies[0], blocks[1]] + copies[1:]:
            copy.start()
        for index, (side, start, length) in enumerate(loads):
            if start == 0:
                blocks[side].wait()
            copies[index].wait()
            value = jnp.dot(
                held[:, pl.ds(side * half + start, length)],
                block[side, pl.ds(start, length), :],
                preferred_element_type=F32,
            )
            if index > 0:
                value = value + total[...]
            elif not first:
                value = value + refs[0][...]
            total[...] = value
            if final and index + 1 == len(loads):
                refs[-5][...] = value.astype(BF)

    shapes = [jax.ShapeDtypeStruct((rows, configs), F32)]
    if final:
        shapes.append(jax.ShapeDtypeStruct((rows, configs), BF))
    return pl.pallas_call(
        kernel,
        in_specs=[IN_SMEM, ANYWHERE, ANYWHERE, ANYWHERE] + ([] if first else [IN_VMEM]),
        out_specs=[IN_VMEM] * len(shapes),
        out_shape=shapes,
        scratch_shapes=[
            pltpu.VMEM((rows, 2 * half), BF),
            pltpu.VMEM((2, half, configs), BF),
            pltpu.SemaphoreType.DMA((len(loads),)),
            pltpu.SemaphoreType.DMA((2,)),
        ],
        input_output_aliases={} if first else {4: 0},
        compiler_params=params(44),
        cost_estimate=cost(4 * rows * half * configs, 4 * rows * half),
    )(scalars([flag]), force_const, mine, other, *([] if first else [harmonic]))


def gradient_kernel(side, own_forces, other_forces, harmonic, got, blocks):
    rows, configs = harmonic.shape
    width = own_forces.shape[1]
    scale = float(1.0 / configs**0.5)
    columns = sum(2 * block[2].shape[0] for block in blocks)
    halves, tiles = [], []
    for index, (base, _, mine, other) in enumerate(blocks):
        for part, value in enumerate((mine, other)):
            for start, length in tiles_of(value.shape[0], 512, 128):
                tiles.append((index, part, len(halves), base, value.shape[0], start, length))
            halves.append(value)
    widest = max(tile[-1] for tile in tiles)
    slots = 4

    def kernel(at, f_own, f_other, h, g, *refs):
        sources, out = refs[: len(halves)], refs[len(halves)]
        residual, made, sem, loaded = refs[len(halves) + 1 : len(halves) + 5]
        held = refs[len(halves) + 5 :]
        loads = [
            pltpu.make_async_copy(source, target, loaded.at[index])
            for index, (source, target) in enumerate(zip(sources, held))
        ]
        for load in loads:
            load.start()
        for part, forces in ((0, f_own), (1, f_other)):
            which = at[0] if part == 0 else 1 - at[0]
            lanes = pl.ds(pl.multiple_of(which * width, 128), width)
            total = forces[...].astype(F32) + (h[:, lanes] + g[:, lanes].astype(F32))
            residual[:, lanes] = total.astype(BF)
        copies = []
        for number, (index, part, half, base, size, start, length) in enumerate(tiles):
            slot = number % slots
            if number >= slots:
                copies[number - slots].wait()
            if start == 0:
                loads[half].wait()
            value = lax.dot_general(
                residual[...],
                held[half][pl.ds(start, length), :],
                (((1,), (1,)), ((), ())),
                preferred_element_type=F32,
            )
            made[slot, :, pl.ds(0, length)] = value * scale
            which = at[index + 1] if part == 0 else 1 - at[index + 1]
            column = pl.multiple_of(base + which * size + start, 128)
            copies.append(
                pltpu.make_async_copy(
                    made.at[slot, :, pl.ds(0, length)],
                    out.at[:, pl.ds(column, length)],
                    sem.at[slot],
                )
            )
            copies[-1].start()
        for copy in copies[-slots:]:
            copy.wait()

    return pl.pallas_call(
        kernel,
        in_specs=[IN_SMEM] + [IN_VMEM] * 4 + [ANYWHERE] * len(halves),
        out_specs=ANYWHERE,
        out_shape=jax.ShapeDtypeStruct((rows, columns), F32),
        scratch_shapes=[
            pltpu.VMEM((rows, configs), BF),
            pltpu.VMEM((slots, rows, widest), F32),
            pltpu.SemaphoreType.DMA((slots,)),
            pltpu.SemaphoreType.DMA((len(halves),)),
        ]
        + [pltpu.VMEM(half.shape, BF) for half in halves],
        compiler_params=params(58),
        cost_estimate=cost(2 * rows * columns * configs, 4 * rows * columns),
    )(
        scalars([side] + [block[1] for block in blocks]),
        own_forces,
        other_forces,
        harmonic,
        got,
        *halves,
    )


def part_steps(g, piece, kind, base, rows, finish):
    row, size, terms = base, rows, []
    levels = g.order(kind)
    pin = yield None
    for level in levels[:-1]:
        size //= 2
        mine = g.mine(level)
        away = (1 - mine) * size
        sent = piece(pin, row + away, size, [(t, o + away) for t, o in terms]).astype(BF)
        got = g.swap(sent, level)
        pin = yield sent
        terms = [(t, o + mine * size) for t, o in terms] + [(got, 0)]
        row = row + mine * size
    own = piece(pin, row, size, terms)
    sent = own.astype(BF)
    got = g.swap(sent, levels[-1])
    pin = yield sent
    block = (pin(own) + got.astype(F32)).astype(BF)
    for level in reversed(levels[1:-1]):
        other = g.swap(block, level)
        pin = yield block
        block = ordered(g.mine(level), pin(block), other)
    other = g.swap(block, levels[0])
    pin = yield block
    yield finish(base, pin(block), other, g.mine(levels[0]))


def local(sizes, eigvec, force_const, amplitudes, mlip_forces, frequency):
    g = Grid(sizes)
    rows = eigvec.shape[0]
    tiled = sizes[0] == 2 and rows % (36 * 256) == 0 and sizes[1] * sizes[2] == 16
    mode_scale = 1.0 / jnp.sqrt(2.0 * frequency)
    scaled_amp = (mode_scale[:, None] * amplitudes.astype(F32)).astype(BF)
    configs = scaled_amp.shape[1]

    def piece(pin, row, size, terms):
        value = jnp.dot(rows_of(eigvec, row, size), pin(scaled_amp), preferred_element_type=F32)
        for term, offset in terms:
            value = value + rows_of(term, offset, size).astype(F32)
        return value

    def row_swap(value, bit):
        pairs = [(r, r ^ (1 << bit)) for r in range(sizes[0])]
        return lax.ppermute(value, "row", pairs)

    state = {"harmonic": None, "displaced": jnp.zeros((rows, configs), BF)}
    blocks = []

    def finish(base, mine, other, flag):
        if tiled:
            blocks.append((base, flag, mine, other))
            final = len(blocks) == len(PARTS)
            sums = finish_kernel(
                force_const, state["harmonic"], mine, other, base, flag, final
            )
            state["harmonic"] = sums[0]
            return sums[-1]
        block = ordered(flag, mine, other)
        term = jnp.dot(
            force_const[:, base : base + block.shape[0]], block, preferred_element_type=F32
        )
        state["harmonic"] = term if state["harmonic"] is None else state["harmonic"] + term
        state["displaced"] = lax.dynamic_update_slice_in_dim(state["displaced"], block, base, 0)
        return state["harmonic"]

    steps, base = [], 0
    for kind, units in PARTS:
        count = rows * units // 36
        steps.append(part_steps(g, piece, kind, base, count, finish))
        next(steps[-1])
        base += count
    assert base == rows
    last = [None]

    def pin(value):
        if last[0] is None:
            return value
        return lax.optimization_barrier((value, last[0]))[0]

    for number, index in enumerate(schedule(len(PARTS), 2 * len(g.order(PARTS[0][0])))):
        last[0] = steps[index].send(pin)
        if tiled and number == len(PARTS):
            other_forces = row_swap(pin(mlip_forces), 0)
        if tiled and number == 3 * len(PARTS):
            last[0] = (last[0], other_forces)
    harmonic = state["harmonic"]
    if tiled:
        got = row_swap(last[0], 0)
        return gradient_kernel(g.at[0], mlip_forces, other_forces, harmonic, got, blocks)
    forces = mlip_forces
    for bit in range(bits_of(sizes[0])):
        forces = ordered((g.at[0] >> bit) & 1, forces, row_swap(forces, bit), 1)
    for bit in range(bits_of(sizes[0])):
        harmonic = harmonic + row_swap(harmonic.astype(BF), bit).astype(F32)
    residual = (forces.astype(F32) + harmonic).astype(BF)
    out = lax.dot_general(
        residual, state["displaced"], (((1,), (1,)), ((), ())), preferred_element_type=F32
    )
    return out / jnp.sqrt(F32(configs))


def schedule(parts, steps):
    if len(ORDER) == parts * steps:
        return ORDER
    return [part for _ in range(steps) for part in range(parts)]


def solution(mesh):
    sizes = tuple(mesh.shape[name] for name in MESH)

    def body(*args):
        return local(sizes, *args)

    return jax.shard_map(
        body,
        mesh=mesh,
        in_specs=(
            P("row", ("col", "cfg")),
            P(("col", "cfg"), "row"),
            P(("col", "cfg"), None),
            P(("col", "cfg"), "row"),
            P(("col", "cfg")),
        ),
        out_specs=P(("col", "cfg"), "row"),
        check_vma=False,
    )
```

time: 230 us -> 205 us (0.89)
  the two profiles are of different devices: /device:TPU:27 before, /device:TPU:0 now
where the time goes in v2:
time: 205 us; the launch traced here: 204 us
  starting transfers between devices  49.4 us (24%)
  waiting for transfers between devices  47.6 us (23%)
  matrix products  46.1 us (22%)
  Pallas kernels  43.6 us (21%)
  other arithmetic  10.5 us (5%)
  local copies, waits for them, and re-layouts  6.17 us (3%)
    ppermute x35, starting transfers between devices, swap(): return lax.ppermute(value, MESH, pairs)  49.4 us
    dot_general x20, matrix products, piece(): jnp.dot(rows_of(eigvec, row, size), pin(scaled_amp), preferred_element_ty...  46.1 us
    ppermute x35, waiting for transfers between devices, swap(): return lax.ppermute(value, MESH, pairs)  45.3 us
    pallas_call x5, Pallas kernels, finish_kernel(): pl.pallas_call(kernel, in_specs=[IN_SMEM, ANYWHERE, ANYWHERE, ANYWHERE] +...  23 us
    pallas_call x1, Pallas kernels, gradient_kernel(): pl.pallas_call(kernel, in_specs=[IN_SMEM] + [IN_VMEM] * 4 + [ANYWHERE] *...  20.6 us
    unnamed x36, local copies, waits for them, and re-layouts  5.53 us
  transfers between devices with their start and end apart: 37, of which 13 were waited for; matrix products, arithmetic and copies ran while one was open for 25% of the time, Pallas kernels for 9%

profile of v2, /device:TPU:0, one launch (start us, length us, event | category | flops | bytes accessed | tf_op | source)
XLA Modules:
  0.0 204.0 jit_solution(10958344149013476052)
XLA Ops:
  0.7 1.6 multiply_convert_fusion
  2.3 3.9 %fusion.19 = bf16[896,512]{1,0:T(8,128)(2,1)} fusion(bf16[1152,512]{1,0:T(8,128)(2,1)S(1)} %multiply_convert_fusion, bf16[9216,1152]{1,0:T(8,128)(2,1)} %param.5, s32[]{:T(128)S(6)} %select_n.233), kind=kOutput, calls=%fused_computation.14 | convolution fusion | flops 1057423360 | bytes 4161540 | tf_op jit(solution)/shard_map/dot_general | solution.py:277
  6.2 2.9 %collective-permute-start = (bf16[896,512]{1,0:T(8,128)(2,1)}, bf16[896,512]{1,0:T(8,128)(2,1)S(1)}, u32[]{:S(2)}, u32[]{:S(2)}) collective-permute-start(bf16[896,512]{1,0:T(8,128)(2,1)} %fusion.19), channel_id=1, source_target_pairs={{0,4},{1,5},{2,6},{3,7},{4,0},{5,1},{6,2},{7,3},{8,12},{9,13},{10,... | collective-permute-start | bytes 2752520 | tf_op jit(solution)/shard_map/ppermute | solution.py:62
  9.1 4.1 %fusion.13 = bf16[1024,512]{1,0:T(8,128)(2,1)} fusion(bf16[1152,512]{1,0:T(8,128)(2,1)S(1)} %multiply_convert_fusion, bf16[9216,1152]{1,0:T(8,128)(2,1)} %param.5, s32[]{:T(128)S(6)} %select_n.232), kind=kOutput, calls=%fused_computation.12 | convolution fusion | flops 1208483840 | bytes 4587524 | tf_op jit(solution)/shard_map/dot_general | solution.py:277
  13.3 4.2 %fusion.10 = bf16[1024,512]{1,0:T(8,128)(2,1)} fusion(bf16[1152,512]{1,0:T(8,128)(2,1)S(1)} %multiply_convert_fusion, bf16[9216,1152]{1,0:T(8,128)(2,1)} %param.5, s32[]{:T(128)S(6)} %select_n.231), kind=kOutput, calls=%fused_computation.11 | convolution fusion | flops 1208483840 | bytes 4587524 | tf_op jit(solution)/shard_map/dot_general | solution.py:277
  17.4 2.1 %collective-permute-start.3 = (bf16[1024,512]{1,0:T(8,128)(2,1)}, bf16[1024,512]{1,0:T(8,128)(2,1)S(1)}, u32[]{:S(2)}, u32[]{:S(2)}) collective-permute-start(bf16[1024,512]{1,0:T(8,128)(2,1)} %fusion.13), channel_id=1, source_target_pairs={{0,1},{1,0},{2,3},{3,2},{4,5},{5,4},{6,7},{7,6},{8,9},{9,8},{10,11... | collective-permute-start | bytes 3145736 | tf_op jit(solution)/shard_map/ppermute | solution.py:62
  19.6 3.9 %fusion.16 = bf16[896,512]{1,0:T(8,128)(2,1)} fusion(bf16[1152,512]{1,0:T(8,128)(2,1)S(1)} %multiply_convert_fusion, bf16[9216,1152]{1,0:T(8,128)(2,1)} %param.5, s32[]{:T(128)S(6)} %select_n.230), kind=kOutput, calls=%fused_computation.13 | convolution fusion | flops 1057423360 | bytes 4161540 | tf_op jit(solution)/shard_map/dot_general | solution.py:277
  24.9 3.6 %fusion.22 = bf16[768,512]{1,0:T(8,128)(2,1)} fusion(bf16[1152,512]{1,0:T(8,128)(2,1)S(1)} %multiply_convert_fusion, bf16[9216,1152]{1,0:T(8,128)(2,1)} %param.5, s32[]{:T(128)S(6)} %select_n.229), kind=kOutput, calls=%fused_computation.15 | convolution fusion | flops 906362880 | bytes 3735556 | tf_op jit(solution)/shard_map/dot_general | solution.py:277
  30.0 2.0 add_convert_fusion.3
  32.0 1.6 collective-permute-start.4
  33.6 2.2 %add_convert_fusion.1 = bf16[512,512]{1,0:T(8,128)(2,1)S(1)} fusion(bf16[1024,512]{1,0:T(8,128)(2,1)} %collective-permute-done.2, s32[]{:T(128)S(6)} %select_n.246, bf16[1152,512]{1,0:T(8,128)(2,1)S(1)} %multiply_convert_fusion, bf16[9216,1152]{1,0:T(8,128)(2,1)} %param.5, s32[]{:T(128)S(6)} %select_n.245), kind=kOutput, calls=%fused_computation.26 | convolution fusion | flops 604766208 | bytes 3407880 | tf_op jit(solution)/shard_map/dot_general | solution.py:277
  35.8 6.5 %collective-permute-done.3 = bf16[1024,512]{1,0:T(8,128)(2,1)S(1)} collective-permute-done((bf16[1024,512]{1,0:T(8,128)(2,1)}, bf16[1024,512]{1,0:T(8,128)(2,1)S(1)}, u32[]{:S(2)}, u32[]{:S(2)}) %collective-permute-start.3) | collective-permute-done | bytes 1048608 | tf_op jit(solution)/shard_map/ppermute | solution.py:62
  42.4 1.7 collective-permute-start.6
  44.1 2.1 %add_convert_fusion = bf16[512,512]{1,0:T(8,128)(2,1)S(1)} fusion(bf16[1024,512]{1,0:T(8,128)(2,1)S(1)} %collective-permute-done.3, s32[]{:T(128)S(6)} %select_n.247, bf16[1152,512]{1,0:T(8,128)(2,1)S(1)} %multiply_convert_fusion, bf16[9216,1152]{1,0:T(8,128)(2,1)} %param.5, s32[]{:T(128)S(6)} %select_n.244), kind=kOutput, calls=%fused_computation.25 | convolution fusion | flops 604766208 | bytes 3407880 | tf_op jit(solution)/shard_map/dot_general | solution.py:277
  49.8 2.1 %add_convert_fusion.2 = bf16[448,512]{1,0:T(8,128)(2,1)S(1)} fusion(bf16[896,512]{1,0:T(8,128)(2,1)} %collective-permute-done.5, s32[]{:T(128)S(6)} %select_n.250, bf16[1152,512]{1,0:T(8,128)(2,1)S(1)} %multiply_convert_fusion, bf16[9216,1152]{1,0:T(8,128)(2,1)} %param.5, s32[]{:T(128)S(6)} %select_n.242), kind=kOutput, calls=%fused_computation.33 | convolution fusion | flops 529170432 | bytes 3129352 | tf_op jit(solution)/shard_map/dot_general | solution.py:277
  51.9 5.3 %collective-permute-done.6 = bf16[512,512]{1,0:T(8,128)(2,1)S(1)} collective-permute-done((bf16[512,512]{1,0:T(8,128)(2,1)S(1)}, bf16[512,512]{1,0:T(8,128)(2,1)S(1)}, u32[]{:S(2)}, u32[]{:S(2)}) %collective-permute-start.6) | collective-permute-done | bytes 524320 | tf_op jit(solution)/shard_map/ppermute | solution.py:62
  57.2 1.7 collective-permute-start.12
  59.0 1.6 add_convert_fusion.8
  62.1 4.1 %collective-permute-start.9 = (bf16[256,512]{1,0:T(8,128)(2,1)S(1)}, bf16[256,512]{1,0:T(8,128)(2,1)S(1)}, u32[]{:S(2)}, u32[]{:S(2)}) collective-permute-start(bf16[256,512]{1,0:T(8,128)(2,1)S(1)} %add_convert_fusion.8), channel_id=1, source_target_pairs={{0,8},{1,9},{2,10},{3,11},{4,12},{5,13},{6,14},{7,15},{8,0},{9,1},... | collective-permute-start | bytes 786440 | tf_op jit(solution)/shard_map/ppermute | solution.py:62
  66.6 1.9 add_convert_fusion.4
  68.5 1.6 fusion.43
  70.6 2.0 collective-permute-start.11
  74.2 1.6 add_convert_fusion.7
  75.8 2.6 %collective-permute-done.11 = bf16[384,512]{1,0:T(8,128)(2,1)S(1)} collective-permute-done((bf16[384,512]{1,0:T(8,128)(2,1)S(1)}, bf16[384,512]{1,0:T(8,128)(2,1)S(1)}, u32[]{:S(2)}, u32[]{:S(2)}) %collective-permute-start.11) | collective-permute-done | bytes 393248 | tf_op jit(solution)/shard_map/ppermute | solution.py:62
  78.4 2.0 collective-permute-start.13
  81.9 2.1 %collective-permute-start.17 = (bf16[192,512]{1,0:T(8,128)(2,1)S(1)}, bf16[192,512]{1,0:T(8,128)(2,1)S(1)}, u32[]{:S(2)}, u32[]{:S(2)}) collective-permute-start(bf16[192,512]{1,0:T(8,128)(2,1)S(1)} %add_convert_fusion.12), channel_id=1, source_target_pairs={{0,1},{1,0},{2,3},{3,2},{4,5},{5,4},{6,7},{7,6},{8,9},{9,8},{10,11... | collective-permute-start | bytes 589832 | tf_op jit(solution)/shard_map/ppermute | solution.py:62
  84.1 1.6 fusion.26
  85.7 1.6 collective-permute-start.15
  87.3 1.6 fusion.39
  91.9 1.8 fusion.110
  95.3 2.2 %fusion.114 = (bf16[192,512]{1,0:T(8,128)(2,1)}, f32[192,512]{1,0:T(8,128)S(1)}) fusion(bf16[192,512]{1,0:T(8,128)(2,1)S(1)} %collective-permute-done.17, bf16[384,512]{1,0:T(8,128)(2,1)S(1)} %collective-permute-done.11, s32[]{:T(128)S(6)} %select_n.272, bf16[768,512]{1,0:T(8,128)(2,1)} %collective-permute-done.8, s32[]{:T(128)S(6)} %select_n.271, ...), kind=kOutput, calls=%fused_computation.106 | convolution fusion | flops 227180544 | bytes 2801676 | tf_op jit(solution)/shard_map/dot_general | solution.py:277
  97.5 2.9 %collective-permute-done.18 = bf16[256,512]{1,0:T(8,128)(2,1)S(1)} collective-permute-done((bf16[256,512]{1,0:T(8,128)(2,1)S(1)}, bf16[256,512]{1,0:T(8,128)(2,1)S(1)}, u32[]{:S(2)}, u32[]{:S(2)}) %collective-permute-start.18) | collective-permute-done | bytes 262176 | tf_op jit(solution)/shard_map/ppermute | solution.py:62
  103.1 11.2 %collective-permute-done.21 = bf16[448,512]{1,0:T(8,128)(2,1)S(1)} collective-permute-done((bf16[448,512]{1,0:T(8,128)(2,1)S(1)}, bf16[448,512]{1,0:T(8,128)(2,1)S(1)}, u32[]{:S(2)}, u32[]{:S(2)}) %collective-permute-start.21) | collective-permute-done | bytes 458784 | tf_op jit(solution)/shard_map/ppermute | solution.py:62
  118.5 1.8 collective-permute-start.26
  122.9 2.5 %collective-permute-done.23 = bf16[256,512]{1,0:T(8,128)(2,1)} collective-permute-done((bf16[256,512]{1,0:T(8,128)(2,1)S(1)}, bf16[256,512]{1,0:T(8,128)(2,1)}, u32[]{:S(2)}, u32[]{:S(2)}) %collective-permute-start.23) | collective-permute-done | bytes 262176 | tf_op jit(solution)/shard_map/ppermute | solution.py:62
  126.6 1.9 collective-permute-start.28
  130.4 1.9 collective-permute-start.30
  135.5 4.4 %shard_map.55.refs_0_ = f32[1152,512]{1,0:T(8,128)S(1)} custom-call(s32[1]{0:T(128)} %bitcast.1.at, bf16[1152,9216]{1,0:T(8,128)(2,1)} %k.9, bf16[896,512]{1,0:T(8,128)(2,1)S(1)} %copy-done.4, bf16[896,512]{1,0:T(8,128)(2,1)S(1)} %copy-done.10), custom_call_target="tpu_custom_call" | custom-call | flops 2113929216 | bytes 4128768 | tf_op jit(solution)/shard_map/pallas_call | solution.py:144
  141.5 2.7 %collective-permute-done.30 = bf16[448,512]{1,0:T(8,128)(2,1)S(1)} collective-permute-done((bf16[448,512]{1,0:T(8,128)(2,1)S(1)}, bf16[448,512]{1,0:T(8,128)(2,1)S(1)}, u32[]{:S(2)}, u32[]{:S(2)}) %collective-permute-start.30) | collective-permute-done | bytes 458784 | tf_op jit(solution)/shard_map/ppermute | solution.py:62
  146.4 2.3 %collective-permute-start.34 = (bf16[1024,512]{1,0:T(8,128)(2,1)S(1)}, bf16[1024,512]{1,0:T(8,128)(2,1)S(1)}, u32[]{:S(2)}, u32[]{:S(2)}) collective-permute-start(bf16[1024,512]{1,0:T(8,128)(2,1)S(1)} %maximum_select_fusion.1.d_mine.refs_6_), channel_id=1, source_target_pairs={{0,1},{1,0},{2,3},{3,2},{4,5},{5,4},{6,7},{7,6},{8,9},{9,8},{10,11... | collective-permute-start | bytes 3145736 | tf_op jit(solution)/shard_map/ppermute | solution.py:62
  148.7 8.5 %collective-permute-done.31 = bf16[384,512]{1,0:T(8,128)(2,1)S(1)} collective-permute-done((bf16[384,512]{1,0:T(8,128)(2,1)S(1)}, bf16[384,512]{1,0:T(8,128)(2,1)S(1)}, u32[]{:S(2)}, u32[]{:S(2)}) %collective-permute-start.31) | collective-permute-done | bytes 393248 | tf_op jit(solution)/shard_map/ppermute | solution.py:62
  157.5 1.6 collective-permute-start.35
  159.2 4.7 %shard_map.56.refs_0_ = f32[1152,512]{1,0:T(8,128)S(1)} custom-call(s32[1]{0:T(128)} %bitcast.1.at, bf16[1152,9216]{1,0:T(8,128)(2,1)} %k.9, bf16[1024,512]{1,0:T(8,128)(2,1)S(1)} %maximum_select_fusion.d_mine.refs_2_, bf16[1024,512]{1,0:T(8,128)(2,1)S(1)} %collective-permute-done.32.d_other.refs_3_, ...), custom_call_target="tpu_custom_call", output_to_operand_aliasing={{}: (4, {})} | custom-call | flops 2415919104 | bytes 4718592 | tf_op jit(solution)/shard_map/pallas_call | solution.py:144
  164.0 4.6 %shard_map.57.refs_0_ = f32[1152,512]{1,0:T(8,128)S(1)} custom-call(s32[1]{0:T(128)} %bitcast.1.at, bf16[1152,9216]{1,0:T(8,128)(2,1)} %k.9, bf16[896,512]{1,0:T(8,128)(2,1)S(1)} %maximum_select_fusion.3.d_mine.refs_4_, bf16[896,512]{1,0:T(8,128)(2,1)S(1)} %collective-permute-done.33.d_other.refs_5_, ...), custom_call_target="tpu_custom_call", output_to_operand_aliasing={{}: (4, {})} | custom-call | flops 2113929216 | bytes 4128768 | tf_op jit(solution)/shard_map/pallas_call | solution.py:144
  168.7 4.7 %shard_map.58.refs_0_ = f32[1152,512]{1,0:T(8,128)S(1)} custom-call(s32[1]{0:T(128)} %bitcast.2.at, bf16[1152,9216]{1,0:T(8,128)(2,1)} %k.9, bf16[1024,512]{1,0:T(8,128)(2,1)S(1)} %maximum_select_fusion.1.d_mine.refs_6_, bf16[1024,512]{1,0:T(8,128)(2,1)S(1)} %collective-permute-done.34.d_other.refs_7_, ...), custom_call_target="tpu_custom_call", output_to_operand_aliasing={{}: (4, {})} | custom-call | flops 2415919104 | bytes 4718592 | tf_op jit(solution)/shard_map/pallas_call | solution.py:144
  173.4 4.5 %shard_map.59 = (f32[1152,512]{1,0:T(8,128)S(1)}, bf16[1152,512]{1,0:T(8,128)(2,1)S(1)}) custom-call(s32[1]{0:T(128)} %bitcast.1.at, bf16[1152,9216]{1,0:T(8,128)(2,1)} %k.9, bf16[768,512]{1,0:T(8,128)(2,1)S(1)} %maximum_select_fusion.4.d_mine.refs_8_, bf16[768,512]{1,0:T(8,128)(2,1)S(1)} %collective-permute-done.35.d_other.refs_9_, ...), custom_call_target="tpu_custom_call", output_to_operand_aliasing={{0}: (4, {})} | custom-call | flops 1811939328 | bytes 3538944 | tf_op jit(solution)/shard_map/pallas_call | solution.py:144
  180.0 2.2 %collective-permute-done.36.g = bf16[1152,512]{1,0:T(8,128)(2,1)S(1)} collective-permute-done((bf16[1152,512]{1,0:T(8,128)(2,1)S(1)}, bf16[1152,512]{1,0:T(8,128)(2,1)S(1)}, u32[]{:S(2)}, u32[]{:S(2)}) %collective-permute-start.36) | collective-permute-done | bytes 1179680 | tf_op jit(solution)/shard_map/ppermute | solution.py:284
  183.2 20.6 %shard_map.60 = f32[1152,9216]{1,0:T(8,128)} custom-call(s32[6]{0:T(128)} %stack.11.at, bf16[1152,256]{1,0:T(8,128)(2,1)} %f_own.1, bf16[1152,256]{1,0:T(8,128)(2,1)} %copy-done.15, f32[1152,512]{1,0:T(8,128)} %copy-done, bf16[1152,512]{1,0:T(8,128)(2,1)} %copy-done.13, bf16[896,512]{1,0:T(8,128)(2,1)} %copy-done.3, bf16[896,512]{1,0:T(8,128)(2,1)} %copy-done.9, ...), custom_call_target="tpu_custom_call" | custom-call | flops 10871635968 | bytes 42467328 | tf_op jit(solution)/shard_map/pallas_call | solution.py:217
  (110 shorter events, 40.0 us)
Async XLA Ops:
  6.2 22.8 %collective-permute-start = (bf16[896,512]{1,0:T(8,128)(2,1)}, bf16[896,512]{1,0:T(8,128)(2,1)S(1)}, u32[]{:S(2)}, u32[]{:S(2)}) collective-permute-start(bf16[896,512]{1,0:T(8,128)(2,1)} %fusion.19), channel_id=1, source_target_pairs={{0,4},{1,5},{2,6},{3,7},{4,0},{5,1},{6,2},{7,3},{8,12},{9,13},{10,... | collective-permute-start | bytes 2752520 | tf_op jit(solution)/shard_map/ppermute | solution.py:62
  17.4 16.1 %collective-permute-start.2 = (bf16[1024,512]{1,0:T(8,128)(2,1)}, bf16[1024,512]{1,0:T(8,128)(2,1)}, u32[]{:S(2)}, u32[]{:S(2)}) collective-permute-start(bf16[1024,512]{1,0:T(8,128)(2,1)} %fusion.10), channel_id=1, source_target_pairs={{0,4},{1,5},{2,6},{3,7},{4,0},{5,1},{6,2},{7,3},{8,12},{9,13},{10,... | collective-permute-start | bytes 3145736 | tf_op jit(solution)/shard_map/ppermute | solution.py:62
  17.4 24.9 %collective-permute-start.3 = (bf16[1024,512]{1,0:T(8,128)(2,1)}, bf16[1024,512]{1,0:T(8,128)(2,1)S(1)}, u32[]{:S(2)}, u32[]{:S(2)}) collective-permute-start(bf16[1024,512]{1,0:T(8,128)(2,1)} %fusion.13), channel_id=1, source_target_pairs={{0,1},{1,0},{2,3},{3,2},{4,5},{5,4},{6,7},{7,6},{8,9},{9,8},{10,11... | collective-permute-start | bytes 3145736 | tf_op jit(solution)/shard_map/ppermute | solution.py:62
  23.4 25.9 %collective-permute-start.5 = (bf16[896,512]{1,0:T(8,128)(2,1)}, bf16[896,512]{1,0:T(8,128)(2,1)}, u32[]{:S(2)}, u32[]{:S(2)}) collective-permute-start(bf16[896,512]{1,0:T(8,128)(2,1)} %fusion.16), channel_id=1, source_target_pairs={{0,4},{1,5},{2,6},{3,7},{4,0},{5,1},{6,2},{7,3},{8,12},{9,13},{10,... | collective-permute-start | bytes 2752520 | tf_op jit(solution)/shard_map/ppermute | solution.py:62
  28.5 37.9 %collective-permute-start.8 = (bf16[768,512]{1,0:T(8,128)(2,1)}, bf16[768,512]{1,0:T(8,128)(2,1)}, u32[]{:S(2)}, u32[]{:S(2)}) collective-permute-start(bf16[768,512]{1,0:T(8,128)(2,1)} %fusion.22), channel_id=1, source_target_pairs={{0,4},{1,5},{2,6},{3,7},{4,0},{5,1},{6,2},{7,3},{8,12},{9,13},{10,... | collective-permute-start | bytes 2359304 | tf_op jit(solution)/shard_map/ppermute | solution.py:62
  29.0 4.5 %copy-start.14 = (bf16[1152,256]{1,0:T(8,128)(2,1)S(1)}, bf16[1152,256]{1,0:T(8,128)(2,1)}, u32[]{:S(2)}) copy-start(bf16[1152,256]{1,0:T(8,128)(2,1)} %f_own.1) | copy-start | bytes 1769476
  32.0 14.3 %collective-permute-start.4 = (bf16[448,512]{1,0:T(8,128)(2,1)S(1)}, bf16[448,512]{1,0:T(8,128)(2,1)S(1)}, u32[]{:S(2)}, u32[]{:S(2)}) collective-permute-start(bf16[448,512]{1,0:T(8,128)(2,1)S(1)} %add_convert_fusion.3), channel_id=1, source_target_pairs={{0,8},{1,9},{2,10},{3,11},{4,12},{5,13},{6,14},{7,15},{8,0},{9,1},... | collective-permute-start | bytes 1376264 | tf_op jit(solution)/shard_map/ppermute | solution.py:62
  33.6 48.4 %collective-permute-start.1 = (bf16[1152,256]{1,0:T(8,128)(2,1)S(1)}, bf16[1152,256]{1,0:T(8,128)(2,1)S(1)}, u32[]{:S(2)}, u32[]{:S(2)}) collective-permute-start(bf16[1152,256]{1,0:T(8,128)(2,1)S(1)} %copy-done.14), channel_id=1, source_target_pairs={{0,16},{16,0},{1,17},{17,1},{2,18},{18,2},{3,19},{19,3},{4,20},{20... | collective-permute-start | bytes 1769480 | tf_op jit(solution)/shard_map/ppermute | solution.py:284
  35.8 12.0 %copy-start.17 = (bf16[896,512]{1,0:T(8,128)(2,1)S(1)}, bf16[896,512]{1,0:T(8,128)(2,1)}, u32[]{:S(2)}) copy-start(bf16[896,512]{1,0:T(8,128)(2,1)} %copy-done.16) | copy-start | bytes 2752516
  42.4 14.9 %collective-permute-start.6 = (bf16[512,512]{1,0:T(8,128)(2,1)S(1)}, bf16[512,512]{1,0:T(8,128)(2,1)S(1)}, u32[]{:S(2)}, u32[]{:S(2)}) collective-permute-start(bf16[512,512]{1,0:T(8,128)(2,1)S(1)} %add_convert_fusion.1), channel_id=1, source_target_pairs={{0,1},{1,0},{2,3},{3,2},{4,5},{5,4},{6,7},{7,6},{8,9},{9,8},{10,11... | collective-permute-start | bytes 1572872 | tf_op jit(solution)/shard_map/ppermute | solution.py:62
  46.2 27.5 %collective-permute-start.10 = (bf16[512,512]{1,0:T(8,128)(2,1)S(1)}, bf16[512,512]{1,0:T(8,128)(2,1)S(1)}, u32[]{:S(2)}, u32[]{:S(2)}) collective-permute-start(bf16[512,512]{1,0:T(8,128)(2,1)S(1)} %add_convert_fusion), channel_id=1, source_target_pairs={{0,4},{1,5},{2,6},{3,7},{4,0},{5,1},{6,2},{7,3},{8,12},{9,13},{10,... | collective-permute-start | bytes 1572872 | tf_op jit(solution)/shard_map/ppermute | solution.py:62
  49.3 12.8 %collective-permute-start.7 = (bf16[224,512]{1,0:T(8,128)(2,1)S(1)}, bf16[224,512]{1,0:T(8,128)(2,1)S(1)}, u32[]{:S(2)}, u32[]{:S(2)}) collective-permute-start(bf16[224,512]{1,0:T(8,128)(2,1)S(1)} %fusion.56), channel_id=1, source_target_pairs={{0,1},{1,0},{2,3},{3,2},{4,5},{5,4},{6,7},{7,6},{8,9},{9,8},{10,11... | collective-permute-start | bytes 688136 | tf_op jit(solution)/shard_map/ppermute | solution.py:62
  57.2 26.9 %collective-permute-start.12 = (bf16[448,512]{1,0:T(8,128)(2,1)S(1)}, bf16[448,512]{1,0:T(8,128)(2,1)S(1)}, u32[]{:S(2)}, u32[]{:S(2)}) collective-permute-start(bf16[448,512]{1,0:T(8,128)(2,1)S(1)} %add_convert_fusion.2), channel_id=1, source_target_pairs={{0,1},{1,0},{2,3},{3,2},{4,5},{5,4},{6,7},{7,6},{8,9},{9,8},{10,11... | collective-permute-start | bytes 1376264 | tf_op jit(solution)/shard_map/ppermute | solution.py:62
  62.1 8.5 %collective-permute-start.9 = (bf16[256,512]{1,0:T(8,128)(2,1)S(1)}, bf16[256,512]{1,0:T(8,128)(2,1)S(1)}, u32[]{:S(2)}, u32[]{:S(2)}) collective-permute-start(bf16[256,512]{1,0:T(8,128)(2,1)S(1)} %add_convert_fusion.8), channel_id=1, source_target_pairs={{0,8},{1,9},{2,10},{3,11},{4,12},{5,13},{6,14},{7,15},{8,0},{9,1},... | collective-permute-start | bytes 786440 | tf_op jit(solution)/shard_map/ppermute | solution.py:62
  66.4 22.6 %collective-permute-start.14 = (bf16[224,512]{1,0:T(8,128)(2,1)S(1)}, bf16[224,512]{1,0:T(8,128)(2,1)S(1)}, u32[]{:S(2)}, u32[]{:S(2)}) collective-permute-start(bf16[224,512]{1,0:T(8,128)(2,1)S(1)} %get-tuple-element.95), channel_id=1, source_target_pairs={{0,2},{1,3},{2,0},{3,1},{4,6},{5,7},{6,4},{7,5},{8,10},{9,11},{10,... | collective-permute-start | bytes 688136 | tf_op jit(solution)/shard_map/ppermute | solution.py:62
  70.6 7.8 %collective-permute-start.11 = (bf16[384,512]{1,0:T(8,128)(2,1)S(1)}, bf16[384,512]{1,0:T(8,128)(2,1)S(1)}, u32[]{:S(2)}, u32[]{:S(2)}) collective-permute-start(bf16[384,512]{1,0:T(8,128)(2,1)S(1)} %add_convert_fusion.4), channel_id=1, source_target_pairs={{0,8},{1,9},{2,10},{3,11},{4,12},{5,13},{6,14},{7,15},{8,0},{9,1},... | collective-permute-start | bytes 1179656 | tf_op jit(solution)/shard_map/ppermute | solution.py:62
  73.8 20.1 %collective-permute-start.16 = (bf16[256,512]{1,0:T(8,128)(2,1)S(1)}, bf16[256,512]{1,0:T(8,128)(2,1)S(1)}, u32[]{:S(2)}, u32[]{:S(2)}) collective-permute-start(bf16[256,512]{1,0:T(8,128)(2,1)S(1)} %get-tuple-element.93), channel_id=1, source_target_pairs={{0,2},{1,3},{2,0},{3,1},{4,6},{5,7},{6,4},{7,5},{8,10},{9,11},{10,... | collective-permute-start | bytes 786440 | tf_op jit(solution)/shard_map/ppermute | solution.py:62
  78.4 10.4 %collective-permute-start.13 = (bf16[256,512]{1,0:T(8,128)(2,1)S(1)}, bf16[256,512]{1,0:T(8,128)(2,1)S(1)}, u32[]{:S(2)}, u32[]{:S(2)}) collective-permute-start(bf16[256,512]{1,0:T(8,128)(2,1)S(1)} %add_convert_fusion.7), channel_id=1, source_target_pairs={{0,8},{1,9},{2,10},{3,11},{4,12},{5,13},{6,14},{7,15},{8,0},{9,1},... | collective-permute-start | bytes 786440 | tf_op jit(solution)/shard_map/ppermute | solution.py:62
  81.9 6.9 %copy-start.15 = (bf16[1152,256]{1,0:T(8,128)(2,1)}, bf16[1152,256]{1,0:T(8,128)(2,1)S(1)}, u32[]{:S(2)}) copy-start(bf16[1152,256]{1,0:T(8,128)(2,1)S(1)} %collective-permute-done.1.f_other) | copy-start | bytes 1769476
  81.9 13.3 %collective-permute-start.17 = (bf16[192,512]{1,0:T(8,128)(2,1)S(1)}, bf16[192,512]{1,0:T(8,128)(2,1)S(1)}, u32[]{:S(2)}, u32[]{:S(2)}) collective-permute-start(bf16[192,512]{1,0:T(8,128)(2,1)S(1)} %add_convert_fusion.12), channel_id=1, source_target_pairs={{0,1},{1,0},{2,3},{3,2},{4,5},{5,4},{6,7},{7,6},{8,9},{9,8},{10,11... | collective-permute-start | bytes 589832 | tf_op jit(solution)/shard_map/ppermute | solution.py:62
  85.7 6.2 %collective-permute-start.15 = (bf16[224,512]{1,0:T(8,128)(2,1)S(1)}, bf16[224,512]{1,0:T(8,128)(2,1)S(1)}, u32[]{:S(2)}, u32[]{:S(2)}) collective-permute-start(bf16[224,512]{1,0:T(8,128)(2,1)S(1)} %fusion.26), channel_id=1, source_target_pairs={{0,8},{1,9},{2,10},{3,11},{4,12},{5,13},{6,14},{7,15},{8,0},{9,1},... | collective-permute-start | bytes 688136 | tf_op jit(solution)/shard_map/ppermute | solution.py:62
  89.1 11.6 %collective-permute-start.19 = (bf16[224,512]{1,0:T(8,128)(2,1)S(1)}, bf16[224,512]{1,0:T(8,128)(2,1)S(1)}, u32[]{:S(2)}, u32[]{:S(2)}) collective-permute-start(bf16[224,512]{1,0:T(8,128)(2,1)S(1)} %add_convert_fusion.10), channel_id=1, source_target_pairs={{0,1},{1,0},{2,3},{3,2},{4,5},{5,4},{6,7},{7,6},{8,9},{9,8},{10,11... | collective-permute-start | bytes 688136 | tf_op jit(solution)/shard_map/ppermute | solution.py:62
  89.3 13.8 %collective-permute-start.20 = (bf16[256,512]{1,0:T(8,128)(2,1)S(1)}, bf16[256,512]{1,0:T(8,128)(2,1)S(1)}, u32[]{:S(2)}, u32[]{:S(2)}) collective-permute-start(bf16[256,512]{1,0:T(8,128)(2,1)S(1)} %get-tuple-element.91), channel_id=1, source_target_pairs={{0,2},{1,3},{2,0},{3,1},{4,6},{5,7},{6,4},{7,5},{8,10},{9,11},{10,... | collective-permute-start | bytes 786440 | tf_op jit(solution)/shard_map/ppermute | solution.py:62
  94.0 6.4 %collective-permute-start.18 = (bf16[256,512]{1,0:T(8,128)(2,1)S(1)}, bf16[256,512]{1,0:T(8,128)(2,1)S(1)}, u32[]{:S(2)}, u32[]{:S(2)}) collective-permute-start(bf16[256,512]{1,0:T(8,128)(2,1)S(1)} %add_convert_fusion.6), channel_id=1, source_target_pairs={{0,8},{1,9},{2,10},{3,11},{4,12},{5,13},{6,14},{7,15},{8,0},{9,1},... | collective-permute-start | bytes 786440 | tf_op jit(solution)/shard_map/ppermute | solution.py:62
  100.8 13.5 %collective-permute-start.21 = (bf16[448,512]{1,0:T(8,128)(2,1)S(1)}, bf16[448,512]{1,0:T(8,128)(2,1)S(1)}, u32[]{:S(2)}, u32[]{:S(2)}) collective-permute-start(bf16[448,512]{1,0:T(8,128)(2,1)S(1)} %maximum_select_fusion.7), channel_id=1, source_target_pairs={{0,8},{1,9},{2,10},{3,11},{4,12},{5,13},{6,14},{7,15},{8,0},{9,1},... | collective-permute-start | bytes 1376264 | tf_op jit(solution)/shard_map/ppermute | solution.py:62
  102.1 18.2 %collective-permute-start.22 = (bf16[224,512]{1,0:T(8,128)(2,1)}, bf16[224,512]{1,0:T(8,128)(2,1)}, u32[]{:S(2)}, u32[]{:S(2)}) collective-permute-start(bf16[224,512]{1,0:T(8,128)(2,1)} %get-tuple-element.89), channel_id=1, source_target_pairs={{0,2},{1,3},{2,0},{3,1},{4,6},{5,7},{6,4},{7,5},{8,10},{9,11},{10,... | collective-permute-start | bytes 688136 | tf_op jit(solution)/shard_map/ppermute | solution.py:62
  114.7 15.6 %copy-start.3 = (bf16[896,512]{1,0:T(8,128)(2,1)}, bf16[896,512]{1,0:T(8,128)(2,1)S(1)}, u32[]{:S(2)}) copy-start(bf16[896,512]{1,0:T(8,128)(2,1)S(1)} %maximum_select_fusion.2.d_mine.refs_0_) | copy-start | bytes 2752516
  114.7 18.6 %collective-permute-start.27 = (bf16[896,512]{1,0:T(8,128)(2,1)S(1)}, bf16[896,512]{1,0:T(8,128)(2,1)S(1)}, u32[]{:S(2)}, u32[]{:S(2)}) collective-permute-start(bf16[896,512]{1,0:T(8,128)(2,1)S(1)} %maximum_select_fusion.2.d_mine.refs_0_), channel_id=1, source_target_pairs={{0,4},{1,5},{2,6},{3,7},{4,0},{5,1},{6,2},{7,3},{8,12},{9,13},{10,... | collective-permute-start | bytes 2752520 | tf_op jit(solution)/shard_map/ppermute | solution.py:62
  116.0 9.4 %collective-permute-start.23 = (bf16[256,512]{1,0:T(8,128)(2,1)S(1)}, bf16[256,512]{1,0:T(8,128)(2,1)}, u32[]{:S(2)}, u32[]{:S(2)}) collective-permute-start(bf16[256,512]{1,0:T(8,128)(2,1)S(1)} %add_convert_fusion.5), channel_id=1, source_target_pairs={{0,8},{1,9},{2,10},{3,11},{4,12},{5,13},{6,14},{7,15},{8,0},{9,1},... | collective-permute-start | bytes 786440 | tf_op jit(solution)/shard_map/ppermute | solution.py:62
  117.5 9.0 %collective-permute-start.24 = (bf16[192,512]{1,0:T(8,128)(2,1)}, bf16[192,512]{1,0:T(8,128)(2,1)S(1)}, u32[]{:S(2)}, u32[]{:S(2)}) collective-permute-start(bf16[192,512]{1,0:T(8,128)(2,1)} %get-tuple-element.97), channel_id=1, source_target_pairs={{0,2},{1,3},{2,0},{3,1},{4,6},{5,7},{6,4},{7,5},{8,10},{9,11},{10,... | collective-permute-start | bytes 589832 | tf_op jit(solution)/shard_map/ppermute | solution.py:62
  118.5 13.8 %collective-permute-start.26 = (bf16[512,512]{1,0:T(8,128)(2,1)S(1)}, bf16[512,512]{1,0:T(8,128)(2,1)S(1)}, u32[]{:S(2)}, u32[]{:S(2)}) collective-permute-start(bf16[512,512]{1,0:T(8,128)(2,1)S(1)} %maximum_select_fusion.5), channel_id=1, source_target_pairs={{0,1},{1,0},{2,3},{3,2},{4,5},{5,4},{6,7},{7,6},{8,9},{9,8},{10,11... | collective-permute-start | bytes 1572872 | tf_op jit(solution)/shard_map/ppermute | solution.py:62
  121.3 8.9 %collective-permute-start.25 = (bf16[224,512]{1,0:T(8,128)(2,1)S(1)}, bf16[224,512]{1,0:T(8,128)(2,1)S(1)}, u32[]{:S(2)}, u32[]{:S(2)}) collective-permute-start(bf16[224,512]{1,0:T(8,128)(2,1)S(1)} %add_convert_fusion.9), channel_id=1, source_target_pairs={{0,8},{1,9},{2,10},{3,11},{4,12},{5,13},{6,14},{7,15},{8,0},{9,1},... | collective-permute-start | bytes 688136 | tf_op jit(solution)/shard_map/ppermute | solution.py:62
  126.6 13.3 %collective-permute-start.28 = (bf16[192,512]{1,0:T(8,128)(2,1)S(1)}, bf16[192,512]{1,0:T(8,128)(2,1)S(1)}, u32[]{:S(2)}, u32[]{:S(2)}) collective-permute-start(bf16[192,512]{1,0:T(8,128)(2,1)S(1)} %add_convert_fusion.11), channel_id=1, source_target_pairs={{0,1},{1,0},{2,3},{3,2},{4,5},{5,4},{6,7},{7,6},{8,9},{9,8},{10,11... | collective-permute-start | bytes 589832 | tf_op jit(solution)/shard_map/ppermute | solution.py:62
  128.6 12.5 %collective-permute-start.29 = (bf16[512,512]{1,0:T(8,128)(2,1)S(1)}, bf16[512,512]{1,0:T(8,128)(2,1)S(1)}, u32[]{:S(2)}, u32[]{:S(2)}) collective-permute-start(bf16[512,512]{1,0:T(8,128)(2,1)S(1)} %maximum_select_fusion.6), channel_id=1, source_target_pairs={{0,4},{1,5},{2,6},{3,7},{4,0},{5,1},{6,2},{7,3},{8,12},{9,13},{10,... | collective-permute-start | bytes 1572872 | tf_op jit(solution)/shard_map/ppermute | solution.py:62
  130.4 13.9 %collective-permute-start.30 = (bf16[448,512]{1,0:T(8,128)(2,1)S(1)}, bf16[448,512]{1,0:T(8,128)(2,1)S(1)}, u32[]{:S(2)}, u32[]{:S(2)}) collective-permute-start(bf16[448,512]{1,0:T(8,128)(2,1)S(1)} %maximum_select_fusion.8), channel_id=1, source_target_pairs={{0,1},{1,0},{2,3},{3,2},{4,5},{5,4},{6,7},{7,6},{8,9},{9,8},{10,11... | collective-permute-start | bytes 1376264 | tf_op jit(solution)/shard_map/ppermute | solution.py:62
  132.8 26.4 %copy-start.1 = (bf16[1024,512]{1,0:T(8,128)(2,1)}, bf16[1024,512]{1,0:T(8,128)(2,1)S(1)}, u32[]{:S(2)}) copy-start(bf16[1024,512]{1,0:T(8,128)(2,1)S(1)} %maximum_select_fusion.d_mine.refs_2_) | copy-start | bytes 3145732
  132.8 26.4 %collective-permute-start.32 = (bf16[1024,512]{1,0:T(8,128)(2,1)S(1)}, bf16[1024,512]{1,0:T(8,128)(2,1)S(1)}, u32[]{:S(2)}, u32[]{:S(2)}) collective-permute-start(bf16[1024,512]{1,0:T(8,128)(2,1)S(1)} %maximum_select_fusion.d_mine.refs_2_), channel_id=1, source_target_pairs={{0,4},{1,5},{2,6},{3,7},{4,0},{5,1},{6,2},{7,3},{8,12},{9,13},{10,... | collective-permute-start | bytes 3145736 | tf_op jit(solution)/shard_map/ppermute | solution.py:62
  141.5 27.2 %copy-start.2 = (bf16[1024,512]{1,0:T(8,128)(2,1)}, bf16[1024,512]{1,0:T(8,128)(2,1)S(1)}, u32[]{:S(2)}) copy-start(bf16[1024,512]{1,0:T(8,128)(2,1)S(1)} %maximum_select_fusion.1.d_mine.refs_6_) | copy-start | bytes 3145732
  144.6 19.3 %copy-start.5 = (bf16[896,512]{1,0:T(8,128)(2,1)}, bf16[896,512]{1,0:T(8,128)(2,1)S(1)}, u32[]{:S(2)}) copy-start(bf16[896,512]{1,0:T(8,128)(2,1)S(1)} %maximum_select_fusion.3.d_mine.refs_4_) | copy-start | bytes 2752516
  144.7 19.3 %collective-permute-start.33 = (bf16[896,512]{1,0:T(8,128)(2,1)S(1)}, bf16[896,512]{1,0:T(8,128)(2,1)S(1)}, u32[]{:S(2)}, u32[]{:S(2)}) collective-permute-start(bf16[896,512]{1,0:T(8,128)(2,1)S(1)} %maximum_select_fusion.3.d_mine.refs_4_), channel_id=1, source_target_pairs={{0,4},{1,5},{2,6},{3,7},{4,0},{5,1},{6,2},{7,3},{8,12},{9,13},{10,... | collective-permute-start | bytes 2752520 | tf_op jit(solution)/shard_map/ppermute | solution.py:62
  145.2 12.1 %collective-permute-start.31 = (bf16[384,512]{1,0:T(8,128)(2,1)S(1)}, bf16[384,512]{1,0:T(8,128)(2,1)S(1)}, u32[]{:S(2)}, u32[]{:S(2)}) collective-permute-start(bf16[384,512]{1,0:T(8,128)(2,1)S(1)} %maximum_select_fusion.9), channel_id=1, source_target_pairs={{0,8},{1,9},{2,10},{3,11},{4,12},{5,13},{6,14},{7,15},{8,0},{9,1},... | collective-permute-start | bytes 1179656 | tf_op jit(solution)/shard_map/ppermute | solution.py:62
  146.4 22.2 %collective-permute-start.34 = (bf16[1024,512]{1,0:T(8,128)(2,1)S(1)}, bf16[1024,512]{1,0:T(8,128)(2,1)S(1)}, u32[]{:S(2)}, u32[]{:S(2)}) collective-permute-start(bf16[1024,512]{1,0:T(8,128)(2,1)S(1)} %maximum_select_fusion.1.d_mine.refs_6_), channel_id=1, source_target_pairs={{0,1},{1,0},{2,3},{3,2},{4,5},{5,4},{6,7},{7,6},{8,9},{9,8},{10,11... | collective-permute-start | bytes 3145736 | tf_op jit(solution)/shard_map/ppermute | solution.py:62
  157.5 15.9 %copy-start.6 = (bf16[768,512]{1,0:T(8,128)(2,1)}, bf16[768,512]{1,0:T(8,128)(2,1)S(1)}, u32[]{:S(2)}) copy-start(bf16[768,512]{1,0:T(8,128)(2,1)S(1)} %maximum_select_fusion.4.d_mine.refs_8_) | copy-start | bytes 2359300
  157.5 15.9 %collective-permute-start.35 = (bf16[768,512]{1,0:T(8,128)(2,1)S(1)}, bf16[768,512]{1,0:T(8,128)(2,1)S(1)}, u32[]{:S(2)}, u32[]{:S(2)}) collective-permute-start(bf16[768,512]{1,0:T(8,128)(2,1)S(1)} %maximum_select_fusion.4.d_mine.refs_8_), channel_id=1, source_target_pairs={{0,4},{1,5},{2,6},{3,7},{4,0},{5,1},{6,2},{7,3},{8,12},{9,13},{10,... | collective-permute-start | bytes 2359304 | tf_op jit(solution)/shard_map/ppermute | solution.py:62
  159.2 4.7 %copy-start.7 = (bf16[1024,512]{1,0:T(8,128)(2,1)}, bf16[1024,512]{1,0:T(8,128)(2,1)S(1)}, u32[]{:S(2)}) copy-start(bf16[1024,512]{1,0:T(8,128)(2,1)S(1)} %collective-permute-done.32.d_other.refs_3_) | copy-start | bytes 3145732
  164.0 4.7 %copy-start.11 = (bf16[896,512]{1,0:T(8,128)(2,1)}, bf16[896,512]{1,0:T(8,128)(2,1)S(1)}, u32[]{:S(2)}) copy-start(bf16[896,512]{1,0:T(8,128)(2,1)S(1)} %collective-permute-done.33.d_other.refs_5_) | copy-start | bytes 2752516
  168.7 4.7 %copy-start.8 = (bf16[1024,512]{1,0:T(8,128)(2,1)}, bf16[1024,512]{1,0:T(8,128)(2,1)S(1)}, u32[]{:S(2)}) copy-start(bf16[1024,512]{1,0:T(8,128)(2,1)S(1)} %collective-permute-done.34.d_other.refs_7_) | copy-start | bytes 3145732
  179.4 2.8 %collective-permute-start.36 = (bf16[1152,512]{1,0:T(8,128)(2,1)S(1)}, bf16[1152,512]{1,0:T(8,128)(2,1)S(1)}, u32[]{:S(2)}, u32[]{:S(2)}) collective-permute-start(bf16[1152,512]{1,0:T(8,128)(2,1)S(1)} %get-tuple-element.88), channel_id=1, source_target_pairs={{0,16},{16,0},{1,17},{17,1},{2,18},{18,2},{3,19},{19,3},{4,20},{20... | collective-permute-start | bytes 3538952 | tf_op jit(solution)/shard_map/ppermute | solution.py:284
  (7 other events, 12.0 us)

commit v3 on v2

--- a/solution.py
+++ b/solution.py
@@ -8,10 +8,10 @@
 BF = jnp.bfloat16
 F32 = jnp.float32
 MESH = ("row", "col", "cfg")
-PARTS = (("abpq", 7), ("apbq", 8), ("abpq", 6), ("pabq", 8), ("apbq", 7))
+PARTS = (("apbq", 7), ("pabq", 8), ("apbq", 7), ("abpq", 7), ("abpq", 7))
 ORDER = (
-    (0, 3, 1, 4, 2, 0, 1, 3, 0, 4, 1, 0, 2, 1, 3, 2, 4, 3, 0, 4,)
-    + (1, 2, 1, 0, 3, 0, 4, 3, 2, 4, 1, 0, 2, 3, 4, 2, 1, 4, 3, 2,)
+    (3, 1, 2, 0, 4, 3, 2, 1, 3, 0, 2, 3, 4, 2, 1, 0, 4, 1, 0, 3,)
+    + (2, 4, 2, 1, 3, 1, 0, 3, 4, 0, 1, 2, 4, 3, 0, 4, 2, 0, 1, 4,)
 )
 
 
@@ -154,7 +154,7 @@
         ],
         input_output_aliases={} if first else {4: 0},
         compiler_params=params(44),
-        cost_estimate=cost(4 * rows * half * configs, 4 * rows * half),
+        cost_estimate=cost(1, 1),
     )(scalars([flag]), force_const, mine, other, *([] if first else [harmonic]))
 
 
@@ -166,11 +166,11 @@
     halves, tiles = [], []
     for index, (base, _, mine, other) in enumerate(blocks):
         for part, value in enumerate((mine, other)):
-            for start, length in tiles_of(value.shape[0], 512, 128):
+            for start, length in tiles_of(value.shape[0], 1024, 128):
                 tiles.append((index, part, len(halves), base, value.shape[0], start, length))
             halves.append(value)
     widest = max(tile[-1] for tile in tiles)
-    slots = 4
+    slots = 3
 
     def kernel(at, f_own, f_other, h, g, *refs):
         sources, out = refs[: len(halves)], refs[len(halves)]

time: 205 us -> 198 us (0.966)
  starting transfers between devices: 49.4 us -> 36.4 us
  waiting for transfers between devices: 47.6 us -> 56.7 us
  local copies, waits for them, and re-layouts: 6.17 us -> 4.05 us
    ppermute x35, starting transfers between devices: 49.4 us -> 36.4 us  [swap(): return lax.ppermute(value, MESH, pairs)]
    ppermute x35, waiting for transfers between devices: 45.3 us -> 54.5 us  [swap(): return lax.ppermute(value, MESH, pairs)]
    unnamed x36, local copies, waits for them, and re-layouts: 5.53 us -> 3.41 us
  transfers between devices with their start and end apart: 37 -> 37, of which waited for: 13 -> 16; matrix products, arithmetic and copies ran while one was open for 25% -> 26% of each run, Pallas kernels for 9% -> 9%
where the time goes in v3:
time: 198 us; the launch traced here: 197 us
  waiting for transfers between devices  56.7 us (29%)
  matrix products  45.7 us (23%)
  Pallas kernels  43.1 us (22%)
  starting transfers between devices  36.4 us (18%)
  other arithmetic  10.1 us (5%)
  local copies, waits for them, and re-layouts  4.05 us (2%)
    ppermute x35, waiting for transfers between devices, swap(): return lax.ppermute(value, MESH, pairs)  54.5 us
    dot_general x20, matrix products, piece(): jnp.dot(rows_of(eigvec, row, size), pin(scaled_amp), preferred_element_ty...  45.7 us
    ppermute x35, starting transfers between devices, swap(): return lax.ppermute(value, MESH, pairs)  36.4 us
    pallas_call x5, Pallas kernels, finish_kernel(): pl.pallas_call(kernel, in_specs=[IN_SMEM, ANYWHERE, ANYWHERE, ANYWHERE] +...  23.2 us
    pallas_call x1, Pallas kernels, gradient_kernel(): pl.pallas_call(kernel, in_specs=[IN_SMEM] + [IN_VMEM] * 4 + [ANYWHERE] *...  19.9 us
  transfers between devices with their start and end apart: 37, of which 16 were waited for; matrix products, arithmetic and copies ran while one was open for 26% of the time, Pallas kernels for 9%

profile of v3, /device:TPU:0, one launch (start us, length us, event | category | flops | bytes accessed | tf_op | source)
XLA Modules:
  0.0 196.8 jit_solution(16438379512031482429)
XLA Ops:
  0.7 1.6 multiply_convert_fusion
  2.3 3.9 %fusion.22 = bf16[896,512]{1,0:T(8,128)(2,1)} fusion(bf16[1152,512]{1,0:T(8,128)(2,1)S(1)} %multiply_convert_fusion, bf16[9216,1152]{1,0:T(8,128)(2,1)} %param.5, s32[]{:T(128)S(6)} %select_n.207), kind=kOutput, calls=%fused_computation.15 | convolution fusion | flops 1057423360 | bytes 4161540 | tf_op jit(solution)/shard_map/dot_general | solution.py:277
  6.2 2.9 %collective-permute-start = (bf16[896,512]{1,0:T(8,128)(2,1)}, bf16[896,512]{1,0:T(8,128)(2,1)S(1)}, u32[]{:S(2)}, u32[]{:S(2)}) collective-permute-start(bf16[896,512]{1,0:T(8,128)(2,1)} %fusion.22), channel_id=1, source_target_pairs={{0,4},{1,5},{2,6},{3,7},{4,0},{5,1},{6,2},{7,3},{8,12},{9,13},{10,... | collective-permute-start | bytes 2752520 | tf_op jit(solution)/shard_map/ppermute | solution.py:62
  9.1 4.1 %fusion.10 = bf16[1024,512]{1,0:T(8,128)(2,1)} fusion(bf16[1152,512]{1,0:T(8,128)(2,1)S(1)} %multiply_convert_fusion, bf16[9216,1152]{1,0:T(8,128)(2,1)} %param.5, s32[]{:T(128)S(6)} %select_n.206), kind=kOutput, calls=%fused_computation.11 | convolution fusion | flops 1208483840 | bytes 4587524 | tf_op jit(solution)/shard_map/dot_general | solution.py:277
  13.2 3.9 %fusion.19 = bf16[896,512]{1,0:T(8,128)(2,1)} fusion(bf16[1152,512]{1,0:T(8,128)(2,1)S(1)} %multiply_convert_fusion, bf16[9216,1152]{1,0:T(8,128)(2,1)} %param.5, s32[]{:T(128)S(6)} %select_n.205), kind=kOutput, calls=%fused_computation.14 | convolution fusion | flops 1057423360 | bytes 4161540 | tf_op jit(solution)/shard_map/dot_general | solution.py:277
  17.1 2.1 %collective-permute-start.3 = (bf16[1024,512]{1,0:T(8,128)(2,1)}, bf16[1024,512]{1,0:T(8,128)(2,1)S(1)}, u32[]{:S(2)}, u32[]{:S(2)}) collective-permute-start(bf16[1024,512]{1,0:T(8,128)(2,1)} %fusion.10), channel_id=1, source_target_pairs={{0,1},{1,0},{2,3},{3,2},{4,5},{5,4},{6,7},{7,6},{8,9},{9,8},{10,11... | collective-permute-start | bytes 3145736 | tf_op jit(solution)/shard_map/ppermute | solution.py:62
  19.2 3.8 %fusion.16 = bf16[896,512]{1,0:T(8,128)(2,1)} fusion(bf16[1152,512]{1,0:T(8,128)(2,1)S(1)} %multiply_convert_fusion, bf16[9216,1152]{1,0:T(8,128)(2,1)} %param.5, s32[]{:T(128)S(6)} %select_n.204), kind=kOutput, calls=%fused_computation.13 | convolution fusion | flops 1057423360 | bytes 4161540 | tf_op jit(solution)/shard_map/dot_general | solution.py:277
  24.5 3.9 %fusion.13 = bf16[896,512]{1,0:T(8,128)(2,1)} fusion(bf16[1152,512]{1,0:T(8,128)(2,1)S(1)} %multiply_convert_fusion, bf16[9216,1152]{1,0:T(8,128)(2,1)} %param.5, s32[]{:T(128)S(6)} %select_n.203), kind=kOutput, calls=%fused_computation.12 | convolution fusion | flops 1057423360 | bytes 4161540 | tf_op jit(solution)/shard_map/dot_general | solution.py:277
  29.9 2.0 %add_convert_fusion.4 = bf16[448,512]{1,0:T(8,128)(2,1)S(1)} fusion(bf16[896,512]{1,0:T(8,128)(2,1)S(1)} %collective-permute-done, s32[]{:T(128)S(6)} %select_n.208, bf16[1152,512]{1,0:T(8,128)(2,1)S(1)} %multiply_convert_fusion, bf16[9216,1152]{1,0:T(8,128)(2,1)} %param.5, s32[]{:T(128)S(6)} %select_n.202), kind=kOutput, calls=%fused_computation.38 | convolution fusion | flops 529170432 | bytes 3129352 | tf_op jit(solution)/shard_map/dot_general | solution.py:277
  31.9 1.6 collective-permute-start.4
  33.5 2.1 %add_convert_fusion.3 = bf16[448,512]{1,0:T(8,128)(2,1)S(1)} fusion(bf16[896,512]{1,0:T(8,128)(2,1)} %collective-permute-done.2, s32[]{:T(128)S(6)} %select_n.220, bf16[1152,512]{1,0:T(8,128)(2,1)S(1)} %multiply_convert_fusion, bf16[9216,1152]{1,0:T(8,128)(2,1)} %param.5, s32[]{:T(128)S(6)} %select_n.219), kind=kOutput, calls=%fused_computation.37 | convolution fusion | flops 529170432 | bytes 3129352 | tf_op jit(solution)/shard_map/dot_general | solution.py:277
  36.1 7.4 %collective-permute-done.3 = bf16[1024,512]{1,0:T(8,128)(2,1)S(1)} collective-permute-done((bf16[1024,512]{1,0:T(8,128)(2,1)}, bf16[1024,512]{1,0:T(8,128)(2,1)S(1)}, u32[]{:S(2)}, u32[]{:S(2)}) %collective-permute-start.3) | collective-permute-done | bytes 1048608 | tf_op jit(solution)/shard_map/ppermute | solution.py:62
  43.5 2.5 %add_convert_fusion = bf16[512,512]{1,0:T(8,128)(2,1)S(1)} fusion(bf16[1024,512]{1,0:T(8,128)(2,1)S(1)} %collective-permute-done.3, s32[]{:T(128)S(6)} %select_n.221, bf16[1152,512]{1,0:T(8,128)(2,1)S(1)} %multiply_convert_fusion, bf16[9216,1152]{1,0:T(8,128)(2,1)} %param.5, s32[]{:T(128)S(6)} %select_n.218), kind=kOutput, calls=%fused_computation.22 | convolution fusion | flops 604766208 | bytes 3407880 | tf_op jit(solution)/shard_map/dot_general | solution.py:277
  46.0 2.0 %collective-permute-start.10 = (bf16[512,512]{1,0:T(8,128)(2,1)S(1)}, bf16[512,512]{1,0:T(8,128)(2,1)S(1)}, u32[]{:S(2)}, u32[]{:S(2)}) collective-permute-start(bf16[512,512]{1,0:T(8,128)(2,1)S(1)} %add_convert_fusion), channel_id=1, source_target_pairs={{0,4},{1,5},{2,6},{3,7},{4,0},{5,1},{6,2},{7,3},{8,12},{9,13},{10,... | collective-permute-start | bytes 1572872 | tf_op jit(solution)/shard_map/ppermute | solution.py:62
  48.0 1.5 fusion.54
  49.6 1.6 collective-permute-start.7
  51.2 2.1 %add_convert_fusion.2 = bf16[448,512]{1,0:T(8,128)(2,1)S(1)} fusion(bf16[896,512]{1,0:T(8,128)(2,1)} %collective-permute-done.5, s32[]{:T(128)S(6)} %select_n.220, bf16[1152,512]{1,0:T(8,128)(2,1)S(1)} %multiply_convert_fusion, bf16[9216,1152]{1,0:T(8,128)(2,1)} %param.5, s32[]{:T(128)S(6)} %select_n.216), kind=kOutput, calls=%fused_computation.36 | convolution fusion | flops 529170432 | bytes 3129352 | tf_op jit(solution)/shard_map/dot_general | solution.py:277
  53.3 1.6 add_convert_fusion.12
  54.9 1.6 collective-permute-start.9
  59.3 2.6 %collective-permute-start.15 = (bf16[224,512]{1,0:T(8,128)(2,1)S(1)}, bf16[224,512]{1,0:T(8,128)(2,1)S(1)}, u32[]{:S(2)}, u32[]{:S(2)}) collective-permute-start(bf16[224,512]{1,0:T(8,128)(2,1)S(1)} %get-tuple-element.97), channel_id=1, source_target_pairs={{0,2},{1,3},{2,0},{3,1},{4,6},{5,7},{6,4},{7,5},{8,10},{9,11},{10,... | collective-permute-start | bytes 688136 | tf_op jit(solution)/shard_map/ppermute | solution.py:62
  62.0 2.1 %add_convert_fusion.1 = bf16[448,512]{1,0:T(8,128)(2,1)S(1)} fusion(bf16[896,512]{1,0:T(8,128)(2,1)} %collective-permute-done.8, s32[]{:T(128)S(6)} %select_n.208, bf16[1152,512]{1,0:T(8,128)(2,1)S(1)} %multiply_convert_fusion, bf16[9216,1152]{1,0:T(8,128)(2,1)} %param.5, s32[]{:T(128)S(6)} %select_n.213), kind=kOutput, calls=%fused_computation.35 | convolution fusion | flops 529170432 | bytes 3129352 | tf_op jit(solution)/shard_map/dot_general | solution.py:277
  64.1 1.6 fusion.61
  68.0 1.6 add_convert_fusion.6
  69.6 8.6 %collective-permute-done.11 = bf16[448,512]{1,0:T(8,128)(2,1)S(1)} collective-permute-done((bf16[448,512]{1,0:T(8,128)(2,1)S(1)}, bf16[448,512]{1,0:T(8,128)(2,1)S(1)}, u32[]{:S(2)}, u32[]{:S(2)}) %collective-permute-start.11) | collective-permute-done | bytes 458784 | tf_op jit(solution)/shard_map/ppermute | solution.py:62
  78.2 1.6 add_convert_fusion.11
  79.7 2.1 %collective-permute-start.14 = (bf16[224,512]{1,0:T(8,128)(2,1)S(1)}, bf16[224,512]{1,0:T(8,128)(2,1)S(1)}, u32[]{:S(2)}, u32[]{:S(2)}) collective-permute-start(bf16[224,512]{1,0:T(8,128)(2,1)S(1)} %add_convert_fusion.11), channel_id=1, source_target_pairs={{0,8},{1,9},{2,10},{3,11},{4,12},{5,13},{6,14},{7,15},{8,0},{9,1},... | collective-permute-start | bytes 688136 | tf_op jit(solution)/shard_map/ppermute | solution.py:62
  81.8 1.6 fusion.26
  83.5 1.6 fusion.39
  85.2 2.0 %collective-permute-start.19 = (bf16[256,512]{1,0:T(8,128)(2,1)S(1)}, bf16[256,512]{1,0:T(8,128)(2,1)S(1)}, u32[]{:S(2)}, u32[]{:S(2)}) collective-permute-start(bf16[256,512]{1,0:T(8,128)(2,1)S(1)} %get-tuple-element.93), channel_id=1, source_target_pairs={{0,2},{1,3},{2,0},{3,1},{4,6},{5,7},{6,4},{7,5},{8,10},{9,11},{10,... | collective-permute-start | bytes 786440 | tf_op jit(solution)/shard_map/ppermute | solution.py:62
  90.0 1.9 collective-permute-start.18
  94.6 1.5 collective-permute-done.18
  96.3 2.8 %collective-permute-done.19 = bf16[256,512]{1,0:T(8,128)(2,1)S(1)} collective-permute-done((bf16[256,512]{1,0:T(8,128)(2,1)S(1)}, bf16[256,512]{1,0:T(8,128)(2,1)S(1)}, u32[]{:S(2)}, u32[]{:S(2)}) %collective-permute-start.19) | collective-permute-done | bytes 262176 | tf_op jit(solution)/shard_map/ppermute | solution.py:62
  103.3 2.1 %collective-permute-start.24 = (bf16[224,512]{1,0:T(8,128)(2,1)S(1)}, bf16[224,512]{1,0:T(8,128)(2,1)S(1)}, u32[]{:S(2)}, u32[]{:S(2)}) collective-permute-start(bf16[224,512]{1,0:T(8,128)(2,1)S(1)} %get-tuple-element.89), channel_id=1, source_target_pairs={{0,2},{1,3},{2,0},{3,1},{4,6},{5,7},{6,4},{7,5},{8,10},{9,11},{10,... | collective-permute-start | bytes 688136 | tf_op jit(solution)/shard_map/ppermute | solution.py:62
  106.3 1.6 collective-permute-start.26
  107.9 9.5 %collective-permute-done.22 = bf16[224,512]{1,0:T(8,128)(2,1)S(1)} collective-permute-done((bf16[224,512]{1,0:T(8,128)(2,1)S(1)}, bf16[224,512]{1,0:T(8,128)(2,1)S(1)}, u32[]{:S(2)}, u32[]{:S(2)}) %collective-permute-start.22) | collective-permute-done | bytes 229408 | tf_op jit(solution)/shard_map/ppermute | solution.py:62
  121.0 5.0 %collective-permute-done.25 = bf16[224,512]{1,0:T(8,128)(2,1)S(1)} collective-permute-done((bf16[224,512]{1,0:T(8,128)(2,1)S(1)}, bf16[224,512]{1,0:T(8,128)(2,1)S(1)}, u32[]{:S(2)}, u32[]{:S(2)}) %collective-permute-start.25) | collective-permute-done | bytes 229408 | tf_op jit(solution)/shard_map/ppermute | solution.py:62
  127.2 3.4 %collective-permute-done.28 = bf16[224,512]{1,0:T(8,128)(2,1)S(1)} collective-permute-done((bf16[224,512]{1,0:T(8,128)(2,1)S(1)}, bf16[224,512]{1,0:T(8,128)(2,1)S(1)}, u32[]{:S(2)}, u32[]{:S(2)}) %collective-permute-start.28) | collective-permute-done | bytes 229408 | tf_op jit(solution)/shard_map/ppermute | solution.py:62
  132.2 2.6 %collective-permute-done.29.d_other.refs_1_ = bf16[896,512]{1,0:T(8,128)(2,1)S(1)} collective-permute-done((bf16[896,512]{1,0:T(8,128)(2,1)S(1)}, bf16[896,512]{1,0:T(8,128)(2,1)S(1)}, u32[]{:S(2)}, u32[]{:S(2)}) %collective-permute-start.29) | collective-permute-done | bytes 917536 | tf_op jit(solution)/shard_map/ppermute | solution.py:62
  134.8 4.5 %shard_map.55.refs_0_ = f32[1152,512]{1,0:T(8,128)S(1)} custom-call(s32[1]{0:T(128)} %bitcast.1.at, bf16[1152,9216]{1,0:T(8,128)(2,1)} %k.9, bf16[896,512]{1,0:T(8,128)(2,1)S(1)} %maximum_select_fusion.1.d_mine.refs_0_, bf16[896,512]{1,0:T(8,128)(2,1)S(1)} %collective-permute-done.29.d_other.refs_1_), custom_call_target="tpu_custom_call" | custom-call | flops 1 | bytes 1 | tf_op jit(solution)/shard_map/pallas_call | solution.py:144
  141.1 3.2 %collective-permute-done.31 = bf16[448,512]{1,0:T(8,128)(2,1)S(1)} collective-permute-done((bf16[448,512]{1,0:T(8,128)(2,1)S(1)}, bf16[448,512]{1,0:T(8,128)(2,1)S(1)}, u32[]{:S(2)}, u32[]{:S(2)}) %collective-permute-start.31) | collective-permute-done | bytes 458784 | tf_op jit(solution)/shard_map/ppermute | solution.py:62
  144.9 2.2 %collective-permute-done.32.d_other.refs_3_ = bf16[896,512]{1,0:T(8,128)(2,1)S(1)} collective-permute-done((bf16[896,512]{1,0:T(8,128)(2,1)S(1)}, bf16[896,512]{1,0:T(8,128)(2,1)S(1)}, u32[]{:S(2)}, u32[]{:S(2)}) %collective-permute-start.32) | collective-permute-done | bytes 917536 | tf_op jit(solution)/shard_map/ppermute | solution.py:62
  147.1 4.7 %shard_map.56.refs_0_ = f32[1152,512]{1,0:T(8,128)S(1)} custom-call(s32[1]{0:T(128)} %bitcast.1.at, bf16[1152,9216]{1,0:T(8,128)(2,1)} %k.9, bf16[896,512]{1,0:T(8,128)(2,1)S(1)} %maximum_select_fusion.2.d_mine.refs_2_, bf16[896,512]{1,0:T(8,128)(2,1)S(1)} %collective-permute-done.32.d_other.refs_3_, ...), custom_call_target="tpu_custom_call", output_to_operand_aliasing={{}: (4, {})} | custom-call | flops 1 | bytes 1 | tf_op jit(solution)/shard_map/pallas_call | solution.py:144
  151.8 5.2 %collective-permute-done.33.d_other.refs_5_ = bf16[896,512]{1,0:T(8,128)(2,1)S(1)} collective-permute-done((bf16[896,512]{1,0:T(8,128)(2,1)S(1)}, bf16[896,512]{1,0:T(8,128)(2,1)S(1)}, u32[]{:S(2)}, u32[]{:S(2)}) %collective-permute-start.33) | collective-permute-done | bytes 917536 | tf_op jit(solution)/shard_map/ppermute | solution.py:62
  157.0 4.7 %shard_map.57.refs_0_ = f32[1152,512]{1,0:T(8,128)S(1)} custom-call(s32[1]{0:T(128)} %bitcast.1.at, bf16[1152,9216]{1,0:T(8,128)(2,1)} %k.9, bf16[896,512]{1,0:T(8,128)(2,1)S(1)} %maximum_select_fusion.3.d_mine.refs_4_, bf16[896,512]{1,0:T(8,128)(2,1)S(1)} %collective-permute-done.33.d_other.refs_5_, ...), custom_call_target="tpu_custom_call", output_to_operand_aliasing={{}: (4, {})} | custom-call | flops 1 | bytes 1 | tf_op jit(solution)/shard_map/pallas_call | solution.py:144
  161.7 4.7 %shard_map.58.refs_0_ = f32[1152,512]{1,0:T(8,128)S(1)} custom-call(s32[1]{0:T(128)} %bitcast.2.at, bf16[1152,9216]{1,0:T(8,128)(2,1)} %k.9, bf16[1024,512]{1,0:T(8,128)(2,1)S(1)} %maximum_select_fusion.d_mine.refs_6_, bf16[1024,512]{1,0:T(8,128)(2,1)S(1)} %collective-permute-done.34.d_other.refs_7_, ...), custom_call_target="tpu_custom_call", output_to_operand_aliasing={{}: (4, {})} | custom-call | flops 1 | bytes 1 | tf_op jit(solution)/shard_map/pallas_call | solution.py:144
  166.8 4.7 %shard_map.59 = (f32[1152,512]{1,0:T(8,128)S(1)}, bf16[1152,512]{1,0:T(8,128)(2,1)S(1)}) custom-call(s32[1]{0:T(128)} %bitcast.1.at, bf16[1152,9216]{1,0:T(8,128)(2,1)} %k.9, bf16[896,512]{1,0:T(8,128)(2,1)S(1)} %maximum_select_fusion.4.d_mine.refs_8_, bf16[896,512]{1,0:T(8,128)(2,1)S(1)} %collective-permute-done.35.d_other.refs_9_, ...), custom_call_target="tpu_custom_call", output_to_operand_aliasing={{0}: (4, {})} | custom-call | flops 1 | bytes 1 | tf_op jit(solution)/shard_map/pallas_call | solution.py:144
  173.5 2.2 %collective-permute-done.36.g = bf16[1152,512]{1,0:T(8,128)(2,1)S(1)} collective-permute-done((bf16[1152,512]{1,0:T(8,128)(2,1)S(1)}, bf16[1152,512]{1,0:T(8,128)(2,1)S(1)}, u32[]{:S(2)}, u32[]{:S(2)}) %collective-permute-start.36) | collective-permute-done | bytes 1179680 | tf_op jit(solution)/shard_map/ppermute | solution.py:284
  176.8 19.9 %shard_map.60 = f32[1152,9216]{1,0:T(8,128)} custom-call(s32[6]{0:T(128)} %stack.11.at, bf16[1152,256]{1,0:T(8,128)(2,1)} %f_own.1, bf16[1152,256]{1,0:T(8,128)(2,1)} %copy-done.13, f32[1152,512]{1,0:T(8,128)} %copy-done, bf16[1152,512]{1,0:T(8,128)(2,1)} %copy-done.11, bf16[896,512]{1,0:T(8,128)(2,1)} %copy-done.2, bf16[896,512]{1,0:T(8,128)(2,1)} %copy-done.7, ...), custom_call_target="tpu_custom_call" | custom-call | flops 10871635968 | bytes 42467328 | tf_op jit(solution)/shard_map/pallas_call | solution.py:217
  (111 shorter events, 32.4 us)
Async XLA Ops:
  6.2 22.8 %collective-permute-start = (bf16[896,512]{1,0:T(8,128)(2,1)}, bf16[896,512]{1,0:T(8,128)(2,1)S(1)}, u32[]{:S(2)}, u32[]{:S(2)}) collective-permute-start(bf16[896,512]{1,0:T(8,128)(2,1)} %fusion.22), channel_id=1, source_target_pairs={{0,4},{1,5},{2,6},{3,7},{4,0},{5,1},{6,2},{7,3},{8,12},{9,13},{10,... | collective-permute-start | bytes 2752520 | tf_op jit(solution)/shard_map/ppermute | solution.py:62
  17.1 16.4 %collective-permute-start.2 = (bf16[896,512]{1,0:T(8,128)(2,1)}, bf16[896,512]{1,0:T(8,128)(2,1)}, u32[]{:S(2)}, u32[]{:S(2)}) collective-permute-start(bf16[896,512]{1,0:T(8,128)(2,1)} %fusion.19), channel_id=1, source_target_pairs={{0,4},{1,5},{2,6},{3,7},{4,0},{5,1},{6,2},{7,3},{8,12},{9,13},{10,... | collective-permute-start | bytes 2752520 | tf_op jit(solution)/shard_map/ppermute | solution.py:62
  17.1 26.4 %collective-permute-start.3 = (bf16[1024,512]{1,0:T(8,128)(2,1)}, bf16[1024,512]{1,0:T(8,128)(2,1)S(1)}, u32[]{:S(2)}, u32[]{:S(2)}) collective-permute-start(bf16[1024,512]{1,0:T(8,128)(2,1)} %fusion.10), channel_id=1, source_target_pairs={{0,1},{1,0},{2,3},{3,2},{4,5},{5,4},{6,7},{7,6},{8,9},{9,8},{10,11... | collective-permute-start | bytes 3145736 | tf_op jit(solution)/shard_map/ppermute | solution.py:62
  23.0 26.5 %collective-permute-start.5 = (bf16[896,512]{1,0:T(8,128)(2,1)}, bf16[896,512]{1,0:T(8,128)(2,1)}, u32[]{:S(2)}, u32[]{:S(2)}) collective-permute-start(bf16[896,512]{1,0:T(8,128)(2,1)} %fusion.16), channel_id=1, source_target_pairs={{0,4},{1,5},{2,6},{3,7},{4,0},{5,1},{6,2},{7,3},{8,12},{9,13},{10,... | collective-permute-start | bytes 2752520 | tf_op jit(solution)/shard_map/ppermute | solution.py:62
  28.4 30.9 %collective-permute-start.8 = (bf16[896,512]{1,0:T(8,128)(2,1)}, bf16[896,512]{1,0:T(8,128)(2,1)}, u32[]{:S(2)}, u32[]{:S(2)}) collective-permute-start(bf16[896,512]{1,0:T(8,128)(2,1)} %fusion.13), channel_id=1, source_target_pairs={{0,4},{1,5},{2,6},{3,7},{4,0},{5,1},{6,2},{7,3},{8,12},{9,13},{10,... | collective-permute-start | bytes 2752520 | tf_op jit(solution)/shard_map/ppermute | solution.py:62
  31.9 11.6 %copy-start.12 = (bf16[1152,256]{1,0:T(8,128)(2,1)S(1)}, bf16[1152,256]{1,0:T(8,128)(2,1)}, u32[]{:S(2)}) copy-start(bf16[1152,256]{1,0:T(8,128)(2,1)} %f_own.1) | copy-start | bytes 1769476
  31.9 14.1 %collective-permute-start.4 = (bf16[448,512]{1,0:T(8,128)(2,1)S(1)}, bf16[448,512]{1,0:T(8,128)(2,1)S(1)}, u32[]{:S(2)}, u32[]{:S(2)}) collective-permute-start(bf16[448,512]{1,0:T(8,128)(2,1)S(1)} %add_convert_fusion.4), channel_id=1, source_target_pairs={{0,8},{1,9},{2,10},{3,11},{4,12},{5,13},{6,14},{7,15},{8,0},{9,1},... | collective-permute-start | bytes 1376264 | tf_op jit(solution)/shard_map/ppermute | solution.py:62
  35.6 12.5 %copy-start.17 = (bf16[896,512]{1,0:T(8,128)(2,1)S(1)}, bf16[896,512]{1,0:T(8,128)(2,1)}, u32[]{:S(2)}) copy-start(bf16[896,512]{1,0:T(8,128)(2,1)} %copy-done.16) | copy-start | bytes 2752516
  35.6 17.7 %collective-permute-start.6 = (bf16[448,512]{1,0:T(8,128)(2,1)S(1)}, bf16[448,512]{1,0:T(8,128)(2,1)S(1)}, u32[]{:S(2)}, u32[]{:S(2)}) collective-permute-start(bf16[448,512]{1,0:T(8,128)(2,1)S(1)} %add_convert_fusion.3), channel_id=1, source_target_pairs={{0,1},{1,0},{2,3},{3,2},{4,5},{5,4},{6,7},{7,6},{8,9},{9,8},{10,11... | collective-permute-start | bytes 1376264 | tf_op jit(solution)/shard_map/ppermute | solution.py:62
  43.5 36.2 %collective-permute-start.1 = (bf16[1152,256]{1,0:T(8,128)(2,1)S(1)}, bf16[1152,256]{1,0:T(8,128)(2,1)S(1)}, u32[]{:S(2)}, u32[]{:S(2)}) collective-permute-start(bf16[1152,256]{1,0:T(8,128)(2,1)S(1)} %copy-done.12), channel_id=1, source_target_pairs={{0,16},{16,0},{1,17},{17,1},{2,18},{18,2},{3,19},{19,3},{4,20},{20... | collective-permute-start | bytes 1769480 | tf_op jit(solution)/shard_map/ppermute | solution.py:284
  46.0 21.2 %collective-permute-start.10 = (bf16[512,512]{1,0:T(8,128)(2,1)S(1)}, bf16[512,512]{1,0:T(8,128)(2,1)S(1)}, u32[]{:S(2)}, u32[]{:S(2)}) collective-permute-start(bf16[512,512]{1,0:T(8,128)(2,1)S(1)} %add_convert_fusion), channel_id=1, source_target_pairs={{0,4},{1,5},{2,6},{3,7},{4,0},{5,1},{6,2},{7,3},{8,12},{9,13},{10,... | collective-permute-start | bytes 1572872 | tf_op jit(solution)/shard_map/ppermute | solution.py:62
  49.6 8.4 %collective-permute-start.7 = (bf16[224,512]{1,0:T(8,128)(2,1)S(1)}, bf16[224,512]{1,0:T(8,128)(2,1)S(1)}, u32[]{:S(2)}, u32[]{:S(2)}) collective-permute-start(bf16[224,512]{1,0:T(8,128)(2,1)S(1)} %fusion.54), channel_id=1, source_target_pairs={{0,1},{1,0},{2,3},{3,2},{4,5},{5,4},{6,7},{7,6},{8,9},{9,8},{10,11... | collective-permute-start | bytes 688136 | tf_op jit(solution)/shard_map/ppermute | solution.py:62
  54.9 10.8 %collective-permute-start.9 = (bf16[224,512]{1,0:T(8,128)(2,1)S(1)}, bf16[224,512]{1,0:T(8,128)(2,1)S(1)}, u32[]{:S(2)}, u32[]{:S(2)}) collective-permute-start(bf16[224,512]{1,0:T(8,128)(2,1)S(1)} %add_convert_fusion.12), channel_id=1, source_target_pairs={{0,8},{1,9},{2,10},{3,11},{4,12},{5,13},{6,14},{7,15},{8,0},{9,1},... | collective-permute-start | bytes 688136 | tf_op jit(solution)/shard_map/ppermute | solution.py:62
  58.0 20.2 %collective-permute-start.11 = (bf16[448,512]{1,0:T(8,128)(2,1)S(1)}, bf16[448,512]{1,0:T(8,128)(2,1)S(1)}, u32[]{:S(2)}, u32[]{:S(2)}) collective-permute-start(bf16[448,512]{1,0:T(8,128)(2,1)S(1)} %add_convert_fusion.2), channel_id=1, source_target_pairs={{0,1},{1,0},{2,3},{3,2},{4,5},{5,4},{6,7},{7,6},{8,9},{9,8},{10,11... | collective-permute-start | bytes 1376264 | tf_op jit(solution)/shard_map/ppermute | solution.py:62
  59.3 30.5 %collective-permute-start.15 = (bf16[224,512]{1,0:T(8,128)(2,1)S(1)}, bf16[224,512]{1,0:T(8,128)(2,1)S(1)}, u32[]{:S(2)}, u32[]{:S(2)}) collective-permute-start(bf16[224,512]{1,0:T(8,128)(2,1)S(1)} %get-tuple-element.97), channel_id=1, source_target_pairs={{0,2},{1,3},{2,0},{3,1},{4,6},{5,7},{6,4},{7,5},{8,10},{9,11},{10,... | collective-permute-start | bytes 688136 | tf_op jit(solution)/shard_map/ppermute | solution.py:62
  66.8 23.2 %collective-permute-start.16 = (bf16[224,512]{1,0:T(8,128)(2,1)S(1)}, bf16[224,512]{1,0:T(8,128)(2,1)S(1)}, u32[]{:S(2)}, u32[]{:S(2)}) collective-permute-start(bf16[224,512]{1,0:T(8,128)(2,1)S(1)} %get-tuple-element.95), channel_id=1, source_target_pairs={{0,2},{1,3},{2,0},{3,1},{4,6},{5,7},{6,4},{7,5},{8,10},{9,11},{10,... | collective-permute-start | bytes 688136 | tf_op jit(solution)/shard_map/ppermute | solution.py:62
  67.2 14.7 %collective-permute-start.12 = (bf16[448,512]{1,0:T(8,128)(2,1)S(1)}, bf16[448,512]{1,0:T(8,128)(2,1)S(1)}, u32[]{:S(2)}, u32[]{:S(2)}) collective-permute-start(bf16[448,512]{1,0:T(8,128)(2,1)S(1)} %add_convert_fusion.1), channel_id=1, source_target_pairs={{0,8},{1,9},{2,10},{3,11},{4,12},{5,13},{6,14},{7,15},{8,0},{9,1},... | collective-permute-start | bytes 1376264 | tf_op jit(solution)/shard_map/ppermute | solution.py:62
  78.2 6.9 %collective-permute-start.13 = (bf16[256,512]{1,0:T(8,128)(2,1)S(1)}, bf16[256,512]{1,0:T(8,128)(2,1)S(1)}, u32[]{:S(2)}, u32[]{:S(2)}) collective-permute-start(bf16[256,512]{1,0:T(8,128)(2,1)S(1)} %add_convert_fusion.6), channel_id=1, source_target_pairs={{0,8},{1,9},{2,10},{3,11},{4,12},{5,13},{6,14},{7,15},{8,0},{9,1},... | collective-permute-start | bytes 786440 | tf_op jit(solution)/shard_map/ppermute | solution.py:62
  79.7 5.3 %copy-start.13 = (bf16[1152,256]{1,0:T(8,128)(2,1)}, bf16[1152,256]{1,0:T(8,128)(2,1)S(1)}, u32[]{:S(2)}) copy-start(bf16[1152,256]{1,0:T(8,128)(2,1)S(1)} %collective-permute-done.1.f_other) | copy-start | bytes 1769476
  79.7 9.0 %collective-permute-start.14 = (bf16[224,512]{1,0:T(8,128)(2,1)S(1)}, bf16[224,512]{1,0:T(8,128)(2,1)S(1)}, u32[]{:S(2)}, u32[]{:S(2)}) collective-permute-start(bf16[224,512]{1,0:T(8,128)(2,1)S(1)} %add_convert_fusion.11), channel_id=1, source_target_pairs={{0,8},{1,9},{2,10},{3,11},{4,12},{5,13},{6,14},{7,15},{8,0},{9,1},... | collective-permute-start | bytes 688136 | tf_op jit(solution)/shard_map/ppermute | solution.py:62
  83.4 10.1 %collective-permute-start.17 = (bf16[224,512]{1,0:T(8,128)(2,1)S(1)}, bf16[224,512]{1,0:T(8,128)(2,1)S(1)}, u32[]{:S(2)}, u32[]{:S(2)}) collective-permute-start(bf16[224,512]{1,0:T(8,128)(2,1)S(1)} %fusion.26), channel_id=1, source_target_pairs={{0,1},{1,0},{2,3},{3,2},{4,5},{5,4},{6,7},{7,6},{8,9},{9,8},{10,11... | collective-permute-start | bytes 688136 | tf_op jit(solution)/shard_map/ppermute | solution.py:62
  85.2 13.8 %collective-permute-start.19 = (bf16[256,512]{1,0:T(8,128)(2,1)S(1)}, bf16[256,512]{1,0:T(8,128)(2,1)S(1)}, u32[]{:S(2)}, u32[]{:S(2)}) collective-permute-start(bf16[256,512]{1,0:T(8,128)(2,1)S(1)} %get-tuple-element.93), channel_id=1, source_target_pairs={{0,2},{1,3},{2,0},{3,1},{4,6},{5,7},{6,4},{7,5},{8,10},{9,11},{10,... | collective-permute-start | bytes 786440 | tf_op jit(solution)/shard_map/ppermute | solution.py:62
  90.0 6.1 %collective-permute-start.18 = (bf16[224,512]{1,0:T(8,128)(2,1)S(1)}, bf16[224,512]{1,0:T(8,128)(2,1)S(1)}, u32[]{:S(2)}, u32[]{:S(2)}) collective-permute-start(bf16[224,512]{1,0:T(8,128)(2,1)S(1)} %add_convert_fusion.9), channel_id=1, source_target_pairs={{0,8},{1,9},{2,10},{3,11},{4,12},{5,13},{6,14},{7,15},{8,0},{9,1},... | collective-permute-start | bytes 688136 | tf_op jit(solution)/shard_map/ppermute | solution.py:62
  92.0 9.0 %collective-permute-start.20 = (bf16[224,512]{1,0:T(8,128)(2,1)S(1)}, bf16[224,512]{1,0:T(8,128)(2,1)}, u32[]{:S(2)}, u32[]{:S(2)}) collective-permute-start(bf16[224,512]{1,0:T(8,128)(2,1)S(1)} %add_convert_fusion.10), channel_id=1, source_target_pairs={{0,1},{1,0},{2,3},{3,2},{4,5},{5,4},{6,7},{7,6},{8,9},{9,8},{10,11... | collective-permute-start | bytes 688136 | tf_op jit(solution)/shard_map/ppermute | solution.py:62
  99.1 7.0 %collective-permute-start.21 = (bf16[256,512]{1,0:T(8,128)(2,1)S(1)}, bf16[256,512]{1,0:T(8,128)(2,1)S(1)}, u32[]{:S(2)}, u32[]{:S(2)}) collective-permute-start(bf16[256,512]{1,0:T(8,128)(2,1)S(1)} %add_convert_fusion.5), channel_id=1, source_target_pairs={{0,8},{1,9},{2,10},{3,11},{4,12},{5,13},{6,14},{7,15},{8,0},{9,1},... | collective-permute-start | bytes 786440 | tf_op jit(solution)/shard_map/ppermute | solution.py:62
  100.2 17.2 %collective-permute-start.22 = (bf16[224,512]{1,0:T(8,128)(2,1)S(1)}, bf16[224,512]{1,0:T(8,128)(2,1)S(1)}, u32[]{:S(2)}, u32[]{:S(2)}) collective-permute-start(bf16[224,512]{1,0:T(8,128)(2,1)S(1)} %get-tuple-element.91), channel_id=1, source_target_pairs={{0,2},{1,3},{2,0},{3,1},{4,6},{5,7},{6,4},{7,5},{8,10},{9,11},{10,... | collective-permute-start | bytes 688136 | tf_op jit(solution)/shard_map/ppermute | solution.py:62
  102.2 16.4 %collective-permute-start.23 = (bf16[448,512]{1,0:T(8,128)(2,1)S(1)}, bf16[448,512]{1,0:T(8,128)(2,1)S(1)}, u32[]{:S(2)}, u32[]{:S(2)}) collective-permute-start(bf16[448,512]{1,0:T(8,128)(2,1)S(1)} %maximum_select_fusion.7), channel_id=1, source_target_pairs={{0,8},{1,9},{2,10},{3,11},{4,12},{5,13},{6,14},{7,15},{8,0},{9,1},... | collective-permute-start | bytes 1376264 | tf_op jit(solution)/shard_map/ppermute | solution.py:62
  103.3 17.4 %collective-permute-start.24 = (bf16[224,512]{1,0:T(8,128)(2,1)S(1)}, bf16[224,512]{1,0:T(8,128)(2,1)S(1)}, u32[]{:S(2)}, u32[]{:S(2)}) collective-permute-start(bf16[224,512]{1,0:T(8,128)(2,1)S(1)} %get-tuple-element.89), channel_id=1, source_target_pairs={{0,2},{1,3},{2,0},{3,1},{4,6},{5,7},{6,4},{7,5},{8,10},{9,11},{10,... | collective-permute-start | bytes 688136 | tf_op jit(solution)/shard_map/ppermute | solution.py:62
  105.4 21.4 %collective-permute-start.27 = (bf16[448,512]{1,0:T(8,128)(2,1)S(1)}, bf16[448,512]{1,0:T(8,128)(2,1)S(1)}, u32[]{:S(2)}, u32[]{:S(2)}) collective-permute-start(bf16[448,512]{1,0:T(8,128)(2,1)S(1)} %maximum_select_fusion.6), channel_id=1, source_target_pairs={{0,1},{1,0},{2,3},{3,2},{4,5},{5,4},{6,7},{7,6},{8,9},{9,8},{10,11... | collective-permute-start | bytes 1376264 | tf_op jit(solution)/shard_map/ppermute | solution.py:62
  106.3 20.0 %collective-permute-start.26 = (bf16[512,512]{1,0:T(8,128)(2,1)S(1)}, bf16[512,512]{1,0:T(8,128)(2,1)S(1)}, u32[]{:S(2)}, u32[]{:S(2)}) collective-permute-start(bf16[512,512]{1,0:T(8,128)(2,1)S(1)} %maximum_select_fusion.5), channel_id=1, source_target_pairs={{0,4},{1,5},{2,6},{3,7},{4,0},{5,1},{6,2},{7,3},{8,12},{9,13},{10,... | collective-permute-start | bytes 1572872 | tf_op jit(solution)/shard_map/ppermute | solution.py:62
  117.4 8.6 %collective-permute-start.25 = (bf16[224,512]{1,0:T(8,128)(2,1)S(1)}, bf16[224,512]{1,0:T(8,128)(2,1)S(1)}, u32[]{:S(2)}, u32[]{:S(2)}) collective-permute-start(bf16[224,512]{1,0:T(8,128)(2,1)S(1)} %add_convert_fusion.8), channel_id=1, source_target_pairs={{0,8},{1,9},{2,10},{3,11},{4,12},{5,13},{6,14},{7,15},{8,0},{9,1},... | collective-permute-start | bytes 688136 | tf_op jit(solution)/shard_map/ppermute | solution.py:62
  118.9 15.8 %copy-start.2 = (bf16[896,512]{1,0:T(8,128)(2,1)}, bf16[896,512]{1,0:T(8,128)(2,1)S(1)}, u32[]{:S(2)}) copy-start(bf16[896,512]{1,0:T(8,128)(2,1)S(1)} %maximum_select_fusion.1.d_mine.refs_0_) | copy-start | bytes 2752516
  118.9 15.8 %collective-permute-start.29 = (bf16[896,512]{1,0:T(8,128)(2,1)S(1)}, bf16[896,512]{1,0:T(8,128)(2,1)S(1)}, u32[]{:S(2)}, u32[]{:S(2)}) collective-permute-start(bf16[896,512]{1,0:T(8,128)(2,1)S(1)} %maximum_select_fusion.1.d_mine.refs_0_), channel_id=1, source_target_pairs={{0,4},{1,5},{2,6},{3,7},{4,0},{5,1},{6,2},{7,3},{8,12},{9,13},{10,... | collective-permute-start | bytes 2752520 | tf_op jit(solution)/shard_map/ppermute | solution.py:62
  120.9 9.6 %collective-permute-start.28 = (bf16[224,512]{1,0:T(8,128)(2,1)S(1)}, bf16[224,512]{1,0:T(8,128)(2,1)S(1)}, u32[]{:S(2)}, u32[]{:S(2)}) collective-permute-start(bf16[224,512]{1,0:T(8,128)(2,1)S(1)} %add_convert_fusion.7), channel_id=1, source_target_pairs={{0,1},{1,0},{2,3},{3,2},{4,5},{5,4},{6,7},{7,6},{8,9},{9,8},{10,11... | collective-permute-start | bytes 688136 | tf_op jit(solution)/shard_map/ppermute | solution.py:62
  126.2 14.2 %collective-permute-start.30 = (bf16[448,512]{1,0:T(8,128)(2,1)S(1)}, bf16[448,512]{1,0:T(8,128)(2,1)S(1)}, u32[]{:S(2)}, u32[]{:S(2)}) collective-permute-start(bf16[448,512]{1,0:T(8,128)(2,1)S(1)} %maximum_select_fusion.8), channel_id=1, source_target_pairs={{0,1},{1,0},{2,3},{3,2},{4,5},{5,4},{6,7},{7,6},{8,9},{9,8},{10,11... | collective-permute-start | bytes 1376264 | tf_op jit(solution)/shard_map/ppermute | solution.py:62
  126.8 34.9 %copy-start.1 = (bf16[1024,512]{1,0:T(8,128)(2,1)}, bf16[1024,512]{1,0:T(8,128)(2,1)S(1)}, u32[]{:S(2)}) copy-start(bf16[1024,512]{1,0:T(8,128)(2,1)S(1)} %maximum_select_fusion.d_mine.refs_6_) | copy-start | bytes 3145732
  127.2 20.0 %copy-start.3 = (bf16[896,512]{1,0:T(8,128)(2,1)}, bf16[896,512]{1,0:T(8,128)(2,1)S(1)}, u32[]{:S(2)}) copy-start(bf16[896,512]{1,0:T(8,128)(2,1)S(1)} %maximum_select_fusion.2.d_mine.refs_2_) | copy-start | bytes 2752516
  130.7 13.5 %collective-permute-start.31 = (bf16[448,512]{1,0:T(8,128)(2,1)S(1)}, bf16[448,512]{1,0:T(8,128)(2,1)S(1)}, u32[]{:S(2)}, u32[]{:S(2)}) collective-permute-start(bf16[448,512]{1,0:T(8,128)(2,1)S(1)} %maximum_select_fusion.9), channel_id=1, source_target_pairs={{0,8},{1,9},{2,10},{3,11},{4,12},{5,13},{6,14},{7,15},{8,0},{9,1},... | collective-permute-start | bytes 1376264 | tf_op jit(solution)/shard_map/ppermute | solution.py:62
  131.1 16.1 %collective-permute-start.32 = (bf16[896,512]{1,0:T(8,128)(2,1)S(1)}, bf16[896,512]{1,0:T(8,128)(2,1)S(1)}, u32[]{:S(2)}, u32[]{:S(2)}) collective-permute-start(bf16[896,512]{1,0:T(8,128)(2,1)S(1)} %maximum_select_fusion.2.d_mine.refs_2_), channel_id=1, source_target_pairs={{0,4},{1,5},{2,6},{3,7},{4,0},{5,1},{6,2},{7,3},{8,12},{9,13},{10,... | collective-permute-start | bytes 2752520 | tf_op jit(solution)/shard_map/ppermute | solution.py:62
  132.2 29.5 %collective-permute-start.34 = (bf16[1024,512]{1,0:T(8,128)(2,1)S(1)}, bf16[1024,512]{1,0:T(8,128)(2,1)S(1)}, u32[]{:S(2)}, u32[]{:S(2)}) collective-permute-start(bf16[1024,512]{1,0:T(8,128)(2,1)S(1)} %maximum_select_fusion.d_mine.refs_6_), channel_id=1, source_target_pairs={{0,1},{1,0},{2,3},{3,2},{4,5},{5,4},{6,7},{7,6},{8,9},{9,8},{10,11... | collective-permute-start | bytes 3145736 | tf_op jit(solution)/shard_map/ppermute | solution.py:62
  140.8 16.2 %copy-start.4 = (bf16[896,512]{1,0:T(8,128)(2,1)}, bf16[896,512]{1,0:T(8,128)(2,1)S(1)}, u32[]{:S(2)}) copy-start(bf16[896,512]{1,0:T(8,128)(2,1)S(1)} %maximum_select_fusion.3.d_mine.refs_4_) | copy-start | bytes 2752516
  140.8 16.2 %collective-permute-start.33 = (bf16[896,512]{1,0:T(8,128)(2,1)S(1)}, bf16[896,512]{1,0:T(8,128)(2,1)S(1)}, u32[]{:S(2)}, u32[]{:S(2)}) collective-permute-start(bf16[896,512]{1,0:T(8,128)(2,1)S(1)} %maximum_select_fusion.3.d_mine.refs_4_), channel_id=1, source_target_pairs={{0,4},{1,5},{2,6},{3,7},{4,0},{5,1},{6,2},{7,3},{8,12},{9,13},{10,... | collective-permute-start | bytes 2752520 | tf_op jit(solution)/shard_map/ppermute | solution.py:62
  144.6 22.2 %copy-start.5 = (bf16[896,512]{1,0:T(8,128)(2,1)}, bf16[896,512]{1,0:T(8,128)(2,1)S(1)}, u32[]{:S(2)}) copy-start(bf16[896,512]{1,0:T(8,128)(2,1)S(1)} %maximum_select_fusion.4.d_mine.refs_8_) | copy-start | bytes 2752516
  144.7 22.2 %collective-permute-start.35 = (bf16[896,512]{1,0:T(8,128)(2,1)S(1)}, bf16[896,512]{1,0:T(8,128)(2,1)S(1)}, u32[]{:S(2)}, u32[]{:S(2)}) collective-permute-start(bf16[896,512]{1,0:T(8,128)(2,1)S(1)} %maximum_select_fusion.4.d_mine.refs_8_), channel_id=1, source_target_pairs={{0,4},{1,5},{2,6},{3,7},{4,0},{5,1},{6,2},{7,3},{8,12},{9,13},{10,... | collective-permute-start | bytes 2752520 | tf_op jit(solution)/shard_map/ppermute | solution.py:62
  147.1 4.7 %copy-start.8 = (bf16[896,512]{1,0:T(8,128)(2,1)}, bf16[896,512]{1,0:T(8,128)(2,1)S(1)}, u32[]{:S(2)}) copy-start(bf16[896,512]{1,0:T(8,128)(2,1)S(1)} %collective-permute-done.32.d_other.refs_3_) | copy-start | bytes 2752516
  161.7 4.7 %copy-start.6 = (bf16[1024,512]{1,0:T(8,128)(2,1)}, bf16[1024,512]{1,0:T(8,128)(2,1)S(1)}, u32[]{:S(2)}) copy-start(bf16[1024,512]{1,0:T(8,128)(2,1)S(1)} %collective-permute-done.34.d_other.refs_7_) | copy-start | bytes 3145732
  166.8 4.7 %copy-start.10 = (bf16[896,512]{1,0:T(8,128)(2,1)}, bf16[896,512]{1,0:T(8,128)(2,1)S(1)}, u32[]{:S(2)}) copy-start(bf16[896,512]{1,0:T(8,128)(2,1)S(1)} %collective-permute-done.35.d_other.refs_9_) | copy-start | bytes 2752516
  172.9 2.8 %collective-permute-start.36 = (bf16[1152,512]{1,0:T(8,128)(2,1)S(1)}, bf16[1152,512]{1,0:T(8,128)(2,1)S(1)}, u32[]{:S(2)}, u32[]{:S(2)}) collective-permute-start(bf16[1152,512]{1,0:T(8,128)(2,1)S(1)} %get-tuple-element.88), channel_id=1, source_target_pairs={{0,16},{16,0},{1,17},{17,1},{2,18},{18,2},{3,19},{19,3},{4,20},{20... | collective-permute-start | bytes 3538952 | tf_op jit(solution)/shard_map/ppermute | solution.py:284
  (7 other events, 19.0 us)

commit v4 on v3

--- a/solution.py
+++ b/solution.py
@@ -174,18 +174,21 @@
 
     def kernel(at, f_own, f_other, h, g, *refs):
         sources, out = refs[: len(halves)], refs[len(halves)]
-        residual, made, sem, loaded = refs[len(halves) + 1 : len(halves) + 5]
-        held = refs[len(halves) + 5 :]
+        residual, made, sem, loaded, g_held, g_sem = refs[len(halves) + 1 : len(halves) + 7]
+        held = refs[len(halves) + 7 :]
+        g_load = pltpu.make_async_copy(g, g_held, g_sem)
+        g_load.start()
         loads = [
             pltpu.make_async_copy(source, target, loaded.at[index])
             for index, (source, target) in enumerate(zip(sources, held))
         ]
         for load in loads:
             load.start()
+        g_load.wait()
         for part, forces in ((0, f_own), (1, f_other)):
             which = at[0] if part == 0 else 1 - at[0]
             lanes = pl.ds(pl.multiple_of(which * width, 128), width)
-            total = forces[...].astype(F32) + (h[:, lanes] + g[:, lanes].astype(F32))
+            total = forces[...].astype(F32) + (h[:, lanes] + g_held[:, lanes].astype(F32))
             residual[:, lanes] = total.astype(BF)
         copies = []
         for number, (index, part, half, base, size, start, length) in enumerate(tiles):
@@ -216,7 +219,7 @@
 
     return pl.pallas_call(
         kernel,
-        in_specs=[IN_SMEM] + [IN_VMEM] * 4 + [ANYWHERE] * len(halves),
+        in_specs=[IN_SMEM] + [IN_VMEM] * 3 + [ANYWHERE] * (1 + len(halves)),
         out_specs=ANYWHERE,
         out_shape=jax.ShapeDtypeStruct((rows, columns), F32),
         scratch_shapes=[
@@ -224,6 +227,8 @@
             pltpu.VMEM((slots, rows, widest), F32),
             pltpu.SemaphoreType.DMA((slots,)),
             pltpu.SemaphoreType.DMA((len(halves),)),
+            pltpu.VMEM((rows, configs), BF),
+            pltpu.SemaphoreType.DMA,
         ]
         + [pltpu.VMEM(half.shape, BF) for half in halves],
         compiler_params=params(58),

time: 198 us -> 201 us (1.015)
  Pallas kernels: 43.1 us -> 45.7 us
    pallas_call x1, Pallas kernels: 19.9 us -> 22.5 us  [gradient_kernel(): pl.pallas_call(kernel, in_specs=[IN_SMEM] + [IN_VMEM] * 3 + [ANYWHERE] *...]
  transfers between devices with their start and end apart: 37 -> 37, of which waited for: 16 -> 16; matrix products, arithmetic and copies ran while one was open for 26% -> 25% of each run, Pallas kernels for 9% -> 9%
where the time goes in v4:
time: 201 us; the launch traced here: 199 us
  waiting for transfers between devices  56.7 us (28%)
  matrix products  45.7 us (23%)
  Pallas kernels  45.7 us (23%)
  starting transfers between devices  36.4 us (18%)
  other arithmetic  10.1 us (5%)
  local copies, waits for them, and re-layouts  4.05 us (2%)
    ppermute x35, waiting for transfers between devices, swap(): return lax.ppermute(value, MESH, pairs)  54.5 us
    dot_general x20, matrix products, piece(): jnp.dot(rows_of(eigvec, row, size), pin(scaled_amp), preferred_element_ty...  45.7 us
    ppermute x35, starting transfers between devices, swap(): return lax.ppermute(value, MESH, pairs)  36.4 us
    pallas_call x5, Pallas kernels, finish_kernel(): pl.pallas_call(kernel, in_specs=[IN_SMEM, ANYWHERE, ANYWHERE, ANYWHERE] +...  23.2 us
    pallas_call x1, Pallas kernels, gradient_kernel(): pl.pallas_call(kernel, in_specs=[IN_SMEM] + [IN_VMEM] * 3 + [ANYWHERE] *...  22.5 us
  transfers between devices with their start and end apart: 37, of which 16 were waited for; matrix products, arithmetic and copies ran while one was open for 25% of the time, Pallas kernels for 9%

profile of v4, /device:TPU:0, one launch (start us, length us, event | category | flops | bytes accessed | tf_op | source)
XLA Modules:
  0.0 199.5 jit_solution(1255334993467632091)
XLA Ops:
  0.7 1.6 multiply_convert_fusion
  2.3 3.9 %fusion.22 = bf16[896,512]{1,0:T(8,128)(2,1)} fusion(bf16[1152,512]{1,0:T(8,128)(2,1)S(1)} %multiply_convert_fusion, bf16[9216,1152]{1,0:T(8,128)(2,1)} %param.5, s32[]{:T(128)S(6)} %select_n.207), kind=kOutput, calls=%fused_computation.15 | convolution fusion | flops 1057423360 | bytes 4161540 | tf_op jit(solution)/shard_map/dot_general | solution.py:282
  6.2 2.9 %collective-permute-start = (bf16[896,512]{1,0:T(8,128)(2,1)}, bf16[896,512]{1,0:T(8,128)(2,1)S(1)}, u32[]{:S(2)}, u32[]{:S(2)}) collective-permute-start(bf16[896,512]{1,0:T(8,128)(2,1)} %fusion.22), channel_id=1, source_target_pairs={{0,4},{1,5},{2,6},{3,7},{4,0},{5,1},{6,2},{7,3},{8,12},{9,13},{10,... | collective-permute-start | bytes 2752520 | tf_op jit(solution)/shard_map/ppermute | solution.py:62
  9.1 4.1 %fusion.10 = bf16[1024,512]{1,0:T(8,128)(2,1)} fusion(bf16[1152,512]{1,0:T(8,128)(2,1)S(1)} %multiply_convert_fusion, bf16[9216,1152]{1,0:T(8,128)(2,1)} %param.5, s32[]{:T(128)S(6)} %select_n.206), kind=kOutput, calls=%fused_computation.11 | convolution fusion | flops 1208483840 | bytes 4587524 | tf_op jit(solution)/shard_map/dot_general | solution.py:282
  13.2 3.9 %fusion.19 = bf16[896,512]{1,0:T(8,128)(2,1)} fusion(bf16[1152,512]{1,0:T(8,128)(2,1)S(1)} %multiply_convert_fusion, bf16[9216,1152]{1,0:T(8,128)(2,1)} %param.5, s32[]{:T(128)S(6)} %select_n.205), kind=kOutput, calls=%fused_computation.14 | convolution fusion | flops 1057423360 | bytes 4161540 | tf_op jit(solution)/shard_map/dot_general | solution.py:282
  17.1 2.1 %collective-permute-start.3 = (bf16[1024,512]{1,0:T(8,128)(2,1)}, bf16[1024,512]{1,0:T(8,128)(2,1)S(1)}, u32[]{:S(2)}, u32[]{:S(2)}) collective-permute-start(bf16[1024,512]{1,0:T(8,128)(2,1)} %fusion.10), channel_id=1, source_target_pairs={{0,1},{1,0},{2,3},{3,2},{4,5},{5,4},{6,7},{7,6},{8,9},{9,8},{10,11... | collective-permute-start | bytes 3145736 | tf_op jit(solution)/shard_map/ppermute | solution.py:62
  19.2 3.8 %fusion.16 = bf16[896,512]{1,0:T(8,128)(2,1)} fusion(bf16[1152,512]{1,0:T(8,128)(2,1)S(1)} %multiply_convert_fusion, bf16[9216,1152]{1,0:T(8,128)(2,1)} %param.5, s32[]{:T(128)S(6)} %select_n.204), kind=kOutput, calls=%fused_computation.13 | convolution fusion | flops 1057423360 | bytes 4161540 | tf_op jit(solution)/shard_map/dot_general | solution.py:282
  24.5 3.9 %fusion.13 = bf16[896,512]{1,0:T(8,128)(2,1)} fusion(bf16[1152,512]{1,0:T(8,128)(2,1)S(1)} %multiply_convert_fusion, bf16[9216,1152]{1,0:T(8,128)(2,1)} %param.5, s32[]{:T(128)S(6)} %select_n.203), kind=kOutput, calls=%fused_computation.12 | convolution fusion | flops 1057423360 | bytes 4161540 | tf_op jit(solution)/shard_map/dot_general | solution.py:282
  29.9 2.0 add_convert_fusion.4
  31.9 1.6 collective-permute-start.4
  33.5 2.1 %add_convert_fusion.3 = bf16[448,512]{1,0:T(8,128)(2,1)S(1)} fusion(bf16[896,512]{1,0:T(8,128)(2,1)} %collective-permute-done.2, s32[]{:T(128)S(6)} %select_n.220, bf16[1152,512]{1,0:T(8,128)(2,1)S(1)} %multiply_convert_fusion, bf16[9216,1152]{1,0:T(8,128)(2,1)} %param.5, s32[]{:T(128)S(6)} %select_n.219), kind=kOutput, calls=%fused_computation.37 | convolution fusion | flops 529170432 | bytes 3129352 | tf_op jit(solution)/shard_map/dot_general | solution.py:282
  36.1 7.4 %collective-permute-done.3 = bf16[1024,512]{1,0:T(8,128)(2,1)S(1)} collective-permute-done((bf16[1024,512]{1,0:T(8,128)(2,1)}, bf16[1024,512]{1,0:T(8,128)(2,1)S(1)}, u32[]{:S(2)}, u32[]{:S(2)}) %collective-permute-start.3) | collective-permute-done | bytes 1048608 | tf_op jit(solution)/shard_map/ppermute | solution.py:62
  43.5 2.5 %add_convert_fusion = bf16[512,512]{1,0:T(8,128)(2,1)S(1)} fusion(bf16[1024,512]{1,0:T(8,128)(2,1)S(1)} %collective-permute-done.3, s32[]{:T(128)S(6)} %select_n.221, bf16[1152,512]{1,0:T(8,128)(2,1)S(1)} %multiply_convert_fusion, bf16[9216,1152]{1,0:T(8,128)(2,1)} %param.5, s32[]{:T(128)S(6)} %select_n.218), kind=kOutput, calls=%fused_computation.22 | convolution fusion | flops 604766208 | bytes 3407880 | tf_op jit(solution)/shard_map/dot_general | solution.py:282
  46.0 2.0 %collective-permute-start.10 = (bf16[512,512]{1,0:T(8,128)(2,1)S(1)}, bf16[512,512]{1,0:T(8,128)(2,1)S(1)}, u32[]{:S(2)}, u32[]{:S(2)}) collective-permute-start(bf16[512,512]{1,0:T(8,128)(2,1)S(1)} %add_convert_fusion), channel_id=1, source_target_pairs={{0,4},{1,5},{2,6},{3,7},{4,0},{5,1},{6,2},{7,3},{8,12},{9,13},{10,... | collective-permute-start | bytes 1572872 | tf_op jit(solution)/shard_map/ppermute | solution.py:62
  48.0 1.5 fusion.54
  49.6 1.6 collective-permute-start.7
  51.2 2.1 %add_convert_fusion.2 = bf16[448,512]{1,0:T(8,128)(2,1)S(1)} fusion(bf16[896,512]{1,0:T(8,128)(2,1)} %collective-permute-done.5, s32[]{:T(128)S(6)} %select_n.220, bf16[1152,512]{1,0:T(8,128)(2,1)S(1)} %multiply_convert_fusion, bf16[9216,1152]{1,0:T(8,128)(2,1)} %param.5, s32[]{:T(128)S(6)} %select_n.216), kind=kOutput, calls=%fused_computation.36 | convolution fusion | flops 529170432 | bytes 3129352 | tf_op jit(solution)/shard_map/dot_general | solution.py:282
  53.3 1.6 add_convert_fusion.12
  54.9 1.6 collective-permute-start.9
  59.3 2.6 %collective-permute-start.15 = (bf16[224,512]{1,0:T(8,128)(2,1)S(1)}, bf16[224,512]{1,0:T(8,128)(2,1)S(1)}, u32[]{:S(2)}, u32[]{:S(2)}) collective-permute-start(bf16[224,512]{1,0:T(8,128)(2,1)S(1)} %get-tuple-element.97), channel_id=1, source_target_pairs={{0,2},{1,3},{2,0},{3,1},{4,6},{5,7},{6,4},{7,5},{8,10},{9,11},{10,... | collective-permute-start | bytes 688136 | tf_op jit(solution)/shard_map/ppermute | solution.py:62
  62.0 2.1 %add_convert_fusion.1 = bf16[448,512]{1,0:T(8,128)(2,1)S(1)} fusion(bf16[896,512]{1,0:T(8,128)(2,1)} %collective-permute-done.8, s32[]{:T(128)S(6)} %select_n.208, bf16[1152,512]{1,0:T(8,128)(2,1)S(1)} %multiply_convert_fusion, bf16[9216,1152]{1,0:T(8,128)(2,1)} %param.5, s32[]{:T(128)S(6)} %select_n.213), kind=kOutput, calls=%fused_computation.35 | convolution fusion | flops 529170432 | bytes 3129352 | tf_op jit(solution)/shard_map/dot_general | solution.py:282
  64.1 1.6 fusion.61
  68.0 1.6 add_convert_fusion.6
  69.6 8.6 %collective-permute-done.11 = bf16[448,512]{1,0:T(8,128)(2,1)S(1)} collective-permute-done((bf16[448,512]{1,0:T(8,128)(2,1)S(1)}, bf16[448,512]{1,0:T(8,128)(2,1)S(1)}, u32[]{:S(2)}, u32[]{:S(2)}) %collective-permute-start.11) | collective-permute-done | bytes 458784 | tf_op jit(solution)/shard_map/ppermute | solution.py:62
  78.2 1.6 add_convert_fusion.11
  79.7 2.1 %collective-permute-start.14 = (bf16[224,512]{1,0:T(8,128)(2,1)S(1)}, bf16[224,512]{1,0:T(8,128)(2,1)S(1)}, u32[]{:S(2)}, u32[]{:S(2)}) collective-permute-start(bf16[224,512]{1,0:T(8,128)(2,1)S(1)} %add_convert_fusion.11), channel_id=1, source_target_pairs={{0,8},{1,9},{2,10},{3,11},{4,12},{5,13},{6,14},{7,15},{8,0},{9,1},... | collective-permute-start | bytes 688136 | tf_op jit(solution)/shard_map/ppermute | solution.py:62
  81.8 1.6 fusion.26
  83.5 1.6 fusion.39
  85.2 2.0 %collective-permute-start.19 = (bf16[256,512]{1,0:T(8,128)(2,1)S(1)}, bf16[256,512]{1,0:T(8,128)(2,1)S(1)}, u32[]{:S(2)}, u32[]{:S(2)}) collective-permute-start(bf16[256,512]{1,0:T(8,128)(2,1)S(1)} %get-tuple-element.93), channel_id=1, source_target_pairs={{0,2},{1,3},{2,0},{3,1},{4,6},{5,7},{6,4},{7,5},{8,10},{9,11},{10,... | collective-permute-start | bytes 786440 | tf_op jit(solution)/shard_map/ppermute | solution.py:62
  90.0 1.9 collective-permute-start.18
  94.6 1.5 collective-permute-done.18
  96.3 2.8 %collective-permute-done.19 = bf16[256,512]{1,0:T(8,128)(2,1)S(1)} collective-permute-done((bf16[256,512]{1,0:T(8,128)(2,1)S(1)}, bf16[256,512]{1,0:T(8,128)(2,1)S(1)}, u32[]{:S(2)}, u32[]{:S(2)}) %collective-permute-start.19) | collective-permute-done | bytes 262176 | tf_op jit(solution)/shard_map/ppermute | solution.py:62
  103.3 2.1 %collective-permute-start.24 = (bf16[224,512]{1,0:T(8,128)(2,1)S(1)}, bf16[224,512]{1,0:T(8,128)(2,1)S(1)}, u32[]{:S(2)}, u32[]{:S(2)}) collective-permute-start(bf16[224,512]{1,0:T(8,128)(2,1)S(1)} %get-tuple-element.89), channel_id=1, source_target_pairs={{0,2},{1,3},{2,0},{3,1},{4,6},{5,7},{6,4},{7,5},{8,10},{9,11},{10,... | collective-permute-start | bytes 688136 | tf_op jit(solution)/shard_map/ppermute | solution.py:62
  106.3 1.6 collective-permute-start.26
  107.9 9.5 %collective-permute-done.22 = bf16[224,512]{1,0:T(8,128)(2,1)S(1)} collective-permute-done((bf16[224,512]{1,0:T(8,128)(2,1)S(1)}, bf16[224,512]{1,0:T(8,128)(2,1)S(1)}, u32[]{:S(2)}, u32[]{:S(2)}) %collective-permute-start.22) | collective-permute-done | bytes 229408 | tf_op jit(solution)/shard_map/ppermute | solution.py:62
  121.0 5.0 %collective-permute-done.25 = bf16[224,512]{1,0:T(8,128)(2,1)S(1)} collective-permute-done((bf16[224,512]{1,0:T(8,128)(2,1)S(1)}, bf16[224,512]{1,0:T(8,128)(2,1)S(1)}, u32[]{:S(2)}, u32[]{:S(2)}) %collective-permute-start.25) | collective-permute-done | bytes 229408 | tf_op jit(solution)/shard_map/ppermute | solution.py:62
  127.2 3.4 %collective-permute-done.28 = bf16[224,512]{1,0:T(8,128)(2,1)S(1)} collective-permute-done((bf16[224,512]{1,0:T(8,128)(2,1)S(1)}, bf16[224,512]{1,0:T(8,128)(2,1)S(1)}, u32[]{:S(2)}, u32[]{:S(2)}) %collective-permute-start.28) | collective-permute-done | bytes 229408 | tf_op jit(solution)/shard_map/ppermute | solution.py:62
  132.2 2.6 %collective-permute-done.29.d_other.refs_1_ = bf16[896,512]{1,0:T(8,128)(2,1)S(1)} collective-permute-done((bf16[896,512]{1,0:T(8,128)(2,1)S(1)}, bf16[896,512]{1,0:T(8,128)(2,1)S(1)}, u32[]{:S(2)}, u32[]{:S(2)}) %collective-permute-start.29) | collective-permute-done | bytes 917536 | tf_op jit(solution)/shard_map/ppermute | solution.py:62
  134.8 4.5 %shard_map.55.refs_0_ = f32[1152,512]{1,0:T(8,128)S(1)} custom-call(s32[1]{0:T(128)} %bitcast.1.at, bf16[1152,9216]{1,0:T(8,128)(2,1)} %k.9, bf16[896,512]{1,0:T(8,128)(2,1)S(1)} %maximum_select_fusion.1.d_mine.refs_0_, bf16[896,512]{1,0:T(8,128)(2,1)S(1)} %collective-permute-done.29.d_other.refs_1_), custom_call_target="tpu_custom_call" | custom-call | flops 1 | bytes 1 | tf_op jit(solution)/shard_map/pallas_call | solution.py:144
  141.1 3.2 %collective-permute-done.31 = bf16[448,512]{1,0:T(8,128)(2,1)S(1)} collective-permute-done((bf16[448,512]{1,0:T(8,128)(2,1)S(1)}, bf16[448,512]{1,0:T(8,128)(2,1)S(1)}, u32[]{:S(2)}, u32[]{:S(2)}) %collective-permute-start.31) | collective-permute-done | bytes 458784 | tf_op jit(solution)/shard_map/ppermute | solution.py:62
  144.9 2.2 %collective-permute-done.32.d_other.refs_3_ = bf16[896,512]{1,0:T(8,128)(2,1)S(1)} collective-permute-done((bf16[896,512]{1,0:T(8,128)(2,1)S(1)}, bf16[896,512]{1,0:T(8,128)(2,1)S(1)}, u32[]{:S(2)}, u32[]{:S(2)}) %collective-permute-start.32) | collective-permute-done | bytes 917536 | tf_op jit(solution)/shard_map/ppermute | solution.py:62
  147.1 4.7 %shard_map.56.refs_0_ = f32[1152,512]{1,0:T(8,128)S(1)} custom-call(s32[1]{0:T(128)} %bitcast.1.at, bf16[1152,9216]{1,0:T(8,128)(2,1)} %k.9, bf16[896,512]{1,0:T(8,128)(2,1)S(1)} %maximum_select_fusion.2.d_mine.refs_2_, bf16[896,512]{1,0:T(8,128)(2,1)S(1)} %collective-permute-done.32.d_other.refs_3_, ...), custom_call_target="tpu_custom_call", output_to_operand_aliasing={{}: (4, {})} | custom-call | flops 1 | bytes 1 | tf_op jit(solution)/shard_map/pallas_call | solution.py:144
  151.8 5.2 %collective-permute-done.33.d_other.refs_5_ = bf16[896,512]{1,0:T(8,128)(2,1)S(1)} collective-permute-done((bf16[896,512]{1,0:T(8,128)(2,1)S(1)}, bf16[896,512]{1,0:T(8,128)(2,1)S(1)}, u32[]{:S(2)}, u32[]{:S(2)}) %collective-permute-start.33) | collective-permute-done | bytes 917536 | tf_op jit(solution)/shard_map/ppermute | solution.py:62
  157.0 4.7 %shard_map.57.refs_0_ = f32[1152,512]{1,0:T(8,128)S(1)} custom-call(s32[1]{0:T(128)} %bitcast.1.at, bf16[1152,9216]{1,0:T(8,128)(2,1)} %k.9, bf16[896,512]{1,0:T(8,128)(2,1)S(1)} %maximum_select_fusion.3.d_mine.refs_4_, bf16[896,512]{1,0:T(8,128)(2,1)S(1)} %collective-permute-done.33.d_other.refs_5_, ...), custom_call_target="tpu_custom_call", output_to_operand_aliasing={{}: (4, {})} | custom-call | flops 1 | bytes 1 | tf_op jit(solution)/shard_map/pallas_call | solution.py:144
  161.7 4.7 %shard_map.58.refs_0_ = f32[1152,512]{1,0:T(8,128)S(1)} custom-call(s32[1]{0:T(128)} %bitcast.2.at, bf16[1152,9216]{1,0:T(8,128)(2,1)} %k.9, bf16[1024,512]{1,0:T(8,128)(2,1)S(1)} %maximum_select_fusion.d_mine.refs_6_, bf16[1024,512]{1,0:T(8,128)(2,1)S(1)} %collective-permute-done.34.d_other.refs_7_, ...), custom_call_target="tpu_custom_call", output_to_operand_aliasing={{}: (4, {})} | custom-call | flops 1 | bytes 1 | tf_op jit(solution)/shard_map/pallas_call | solution.py:144
  166.8 4.7 %shard_map.59 = (f32[1152,512]{1,0:T(8,128)S(1)}, bf16[1152,512]{1,0:T(8,128)(2,1)S(1)}) custom-call(s32[1]{0:T(128)} %bitcast.1.at, bf16[1152,9216]{1,0:T(8,128)(2,1)} %k.9, bf16[896,512]{1,0:T(8,128)(2,1)S(1)} %maximum_select_fusion.4.d_mine.refs_8_, bf16[896,512]{1,0:T(8,128)(2,1)S(1)} %collective-permute-done.35.d_other.refs_9_, ...), custom_call_target="tpu_custom_call", output_to_operand_aliasing={{0}: (4, {})} | custom-call | flops 1 | bytes 1 | tf_op jit(solution)/shard_map/pallas_call | solution.py:144
  173.5 2.2 %collective-permute-done.36.g = bf16[1152,512]{1,0:T(8,128)(2,1)S(1)} collective-permute-done((bf16[1152,512]{1,0:T(8,128)(2,1)S(1)}, bf16[1152,512]{1,0:T(8,128)(2,1)S(1)}, u32[]{:S(2)}, u32[]{:S(2)}) %collective-permute-start.36) | collective-permute-done | bytes 1179680 | tf_op jit(solution)/shard_map/ppermute | solution.py:289
  176.8 22.5 %shard_map.60 = f32[1152,9216]{1,0:T(8,128)} custom-call(s32[6]{0:T(128)} %stack.11.at, bf16[1152,256]{1,0:T(8,128)(2,1)} %f_own.1, bf16[1152,256]{1,0:T(8,128)(2,1)} %copy-done.13, f32[1152,512]{1,0:T(8,128)} %copy-done, bf16[1152,512]{1,0:T(8,128)(2,1)} %copy-done.11, bf16[896,512]{1,0:T(8,128)(2,1)} %copy-done.2, bf16[896,512]{1,0:T(8,128)(2,1)} %copy-done.7, ...), custom_call_target="tpu_custom_call" | custom-call | flops 10871635968 | bytes 42467328 | tf_op jit(solution)/shard_map/pallas_call | solution.py:220
  (111 shorter events, 32.4 us)
Async XLA Ops:
  6.2 22.8 %collective-permute-start = (bf16[896,512]{1,0:T(8,128)(2,1)}, bf16[896,512]{1,0:T(8,128)(2,1)S(1)}, u32[]{:S(2)}, u32[]{:S(2)}) collective-permute-start(bf16[896,512]{1,0:T(8,128)(2,1)} %fusion.22), channel_id=1, source_target_pairs={{0,4},{1,5},{2,6},{3,7},{4,0},{5,1},{6,2},{7,3},{8,12},{9,13},{10,... | collective-permute-start | bytes 2752520 | tf_op jit(solution)/shard_map/ppermute | solution.py:62
  17.1 16.4 %collective-permute-start.2 = (bf16[896,512]{1,0:T(8,128)(2,1)}, bf16[896,512]{1,0:T(8,128)(2,1)}, u32[]{:S(2)}, u32[]{:S(2)}) collective-permute-start(bf16[896,512]{1,0:T(8,128)(2,1)} %fusion.19), channel_id=1, source_target_pairs={{0,4},{1,5},{2,6},{3,7},{4,0},{5,1},{6,2},{7,3},{8,12},{9,13},{10,... | collective-permute-start | bytes 2752520 | tf_op jit(solution)/shard_map/ppermute | solution.py:62
  17.1 26.4 %collective-permute-start.3 = (bf16[1024,512]{1,0:T(8,128)(2,1)}, bf16[1024,512]{1,0:T(8,128)(2,1)S(1)}, u32[]{:S(2)}, u32[]{:S(2)}) collective-permute-start(bf16[1024,512]{1,0:T(8,128)(2,1)} %fusion.10), channel_id=1, source_target_pairs={{0,1},{1,0},{2,3},{3,2},{4,5},{5,4},{6,7},{7,6},{8,9},{9,8},{10,11... | collective-permute-start | bytes 3145736 | tf_op jit(solution)/shard_map/ppermute | solution.py:62
  23.0 26.5 %collective-permute-start.5 = (bf16[896,512]{1,0:T(8,128)(2,1)}, bf16[896,512]{1,0:T(8,128)(2,1)}, u32[]{:S(2)}, u32[]{:S(2)}) collective-permute-start(bf16[896,512]{1,0:T(8,128)(2,1)} %fusion.16), channel_id=1, source_target_pairs={{0,4},{1,5},{2,6},{3,7},{4,0},{5,1},{6,2},{7,3},{8,12},{9,13},{10,... | collective-permute-start | bytes 2752520 | tf_op jit(solution)/shard_map/ppermute | solution.py:62
  28.4 30.9 %collective-permute-start.8 = (bf16[896,512]{1,0:T(8,128)(2,1)}, bf16[896,512]{1,0:T(8,128)(2,1)}, u32[]{:S(2)}, u32[]{:S(2)}) collective-permute-start(bf16[896,512]{1,0:T(8,128)(2,1)} %fusion.13), channel_id=1, source_target_pairs={{0,4},{1,5},{2,6},{3,7},{4,0},{5,1},{6,2},{7,3},{8,12},{9,13},{10,... | collective-permute-start | bytes 2752520 | tf_op jit(solution)/shard_map/ppermute | solution.py:62
  31.9 11.6 %copy-start.12 = (bf16[1152,256]{1,0:T(8,128)(2,1)S(1)}, bf16[1152,256]{1,0:T(8,128)(2,1)}, u32[]{:S(2)}) copy-start(bf16[1152,256]{1,0:T(8,128)(2,1)} %f_own.1) | copy-start | bytes 1769476
  31.9 14.1 %collective-permute-start.4 = (bf16[448,512]{1,0:T(8,128)(2,1)S(1)}, bf16[448,512]{1,0:T(8,128)(2,1)S(1)}, u32[]{:S(2)}, u32[]{:S(2)}) collective-permute-start(bf16[448,512]{1,0:T(8,128)(2,1)S(1)} %add_convert_fusion.4), channel_id=1, source_target_pairs={{0,8},{1,9},{2,10},{3,11},{4,12},{5,13},{6,14},{7,15},{8,0},{9,1},... | collective-permute-start | bytes 1376264 | tf_op jit(solution)/shard_map/ppermute | solution.py:62
  35.6 12.5 %copy-start.17 = (bf16[896,512]{1,0:T(8,128)(2,1)S(1)}, bf16[896,512]{1,0:T(8,128)(2,1)}, u32[]{:S(2)}) copy-start(bf16[896,512]{1,0:T(8,128)(2,1)} %copy-done.16) | copy-start | bytes 2752516
  35.6 17.7 %collective-permute-start.6 = (bf16[448,512]{1,0:T(8,128)(2,1)S(1)}, bf16[448,512]{1,0:T(8,128)(2,1)S(1)}, u32[]{:S(2)}, u32[]{:S(2)}) collective-permute-start(bf16[448,512]{1,0:T(8,128)(2,1)S(1)} %add_convert_fusion.3), channel_id=1, source_target_pairs={{0,1},{1,0},{2,3},{3,2},{4,5},{5,4},{6,7},{7,6},{8,9},{9,8},{10,11... | collective-permute-start | bytes 1376264 | tf_op jit(solution)/shard_map/ppermute | solution.py:62
  43.5 36.2 %collective-permute-start.1 = (bf16[1152,256]{1,0:T(8,128)(2,1)S(1)}, bf16[1152,256]{1,0:T(8,128)(2,1)S(1)}, u32[]{:S(2)}, u32[]{:S(2)}) collective-permute-start(bf16[1152,256]{1,0:T(8,128)(2,1)S(1)} %copy-done.12), channel_id=1, source_target_pairs={{0,16},{16,0},{1,17},{17,1},{2,18},{18,2},{3,19},{19,3},{4,20},{20... | collective-permute-start | bytes 1769480 | tf_op jit(solution)/shard_map/ppermute | solution.py:289
  46.0 21.2 %collective-permute-start.10 = (bf16[512,512]{1,0:T(8,128)(2,1)S(1)}, bf16[512,512]{1,0:T(8,128)(2,1)S(1)}, u32[]{:S(2)}, u32[]{:S(2)}) collective-permute-start(bf16[512,512]{1,0:T(8,128)(2,1)S(1)} %add_convert_fusion), channel_id=1, source_target_pairs={{0,4},{1,5},{2,6},{3,7},{4,0},{5,1},{6,2},{7,3},{8,12},{9,13},{10,... | collective-permute-start | bytes 1572872 | tf_op jit(solution)/shard_map/ppermute | solution.py:62
  49.6 8.4 %collective-permute-start.7 = (bf16[224,512]{1,0:T(8,128)(2,1)S(1)}, bf16[224,512]{1,0:T(8,128)(2,1)S(1)}, u32[]{:S(2)}, u32[]{:S(2)}) collective-permute-start(bf16[224,512]{1,0:T(8,128)(2,1)S(1)} %fusion.54), channel_id=1, source_target_pairs={{0,1},{1,0},{2,3},{3,2},{4,5},{5,4},{6,7},{7,6},{8,9},{9,8},{10,11... | collective-permute-start | bytes 688136 | tf_op jit(solution)/shard_map/ppermute | solution.py:62
  54.9 10.8 %collective-permute-start.9 = (bf16[224,512]{1,0:T(8,128)(2,1)S(1)}, bf16[224,512]{1,0:T(8,128)(2,1)S(1)}, u32[]{:S(2)}, u32[]{:S(2)}) collective-permute-start(bf16[224,512]{1,0:T(8,128)(2,1)S(1)} %add_convert_fusion.12), channel_id=1, source_target_pairs={{0,8},{1,9},{2,10},{3,11},{4,12},{5,13},{6,14},{7,15},{8,0},{9,1},... | collective-permute-start | bytes 688136 | tf_op jit(solution)/shard_map/ppermute | solution.py:62
  58.0 20.2 %collective-permute-start.11 = (bf16[448,512]{1,0:T(8,128)(2,1)S(1)}, bf16[448,512]{1,0:T(8,128)(2,1)S(1)}, u32[]{:S(2)}, u32[]{:S(2)}) collective-permute-start(bf16[448,512]{1,0:T(8,128)(2,1)S(1)} %add_convert_fusion.2), channel_id=1, source_target_pairs={{0,1},{1,0},{2,3},{3,2},{4,5},{5,4},{6,7},{7,6},{8,9},{9,8},{10,11... | collective-permute-start | bytes 1376264 | tf_op jit(solution)/shard_map/ppermute | solution.py:62
  59.3 30.5 %collective-permute-start.15 = (bf16[224,512]{1,0:T(8,128)(2,1)S(1)}, bf16[224,512]{1,0:T(8,128)(2,1)S(1)}, u32[]{:S(2)}, u32[]{:S(2)}) collective-permute-start(bf16[224,512]{1,0:T(8,128)(2,1)S(1)} %get-tuple-element.97), channel_id=1, source_target_pairs={{0,2},{1,3},{2,0},{3,1},{4,6},{5,7},{6,4},{7,5},{8,10},{9,11},{10,... | collective-permute-start | bytes 688136 | tf_op jit(solution)/shard_map/ppermute | solution.py:62
  66.8 23.2 %collective-permute-start.16 = (bf16[224,512]{1,0:T(8,128)(2,1)S(1)}, bf16[224,512]{1,0:T(8,128)(2,1)S(1)}, u32[]{:S(2)}, u32[]{:S(2)}) collective-permute-start(bf16[224,512]{1,0:T(8,128)(2,1)S(1)} %get-tuple-element.95), channel_id=1, source_target_pairs={{0,2},{1,3},{2,0},{3,1},{4,6},{5,7},{6,4},{7,5},{8,10},{9,11},{10,... | collective-permute-start | bytes 688136 | tf_op jit(solution)/shard_map/ppermute | solution.py:62
  67.2 14.7 %collective-permute-start.12 = (bf16[448,512]{1,0:T(8,128)(2,1)S(1)}, bf16[448,512]{1,0:T(8,128)(2,1)S(1)}, u32[]{:S(2)}, u32[]{:S(2)}) collective-permute-start(bf16[448,512]{1,0:T(8,128)(2,1)S(1)} %add_convert_fusion.1), channel_id=1, source_target_pairs={{0,8},{1,9},{2,10},{3,11},{4,12},{5,13},{6,14},{7,15},{8,0},{9,1},... | collective-permute-start | bytes 1376264 | tf_op jit(solution)/shard_map/ppermute | solution.py:62
  78.2 6.9 %collective-permute-start.13 = (bf16[256,512]{1,0:T(8,128)(2,1)S(1)}, bf16[256,512]{1,0:T(8,128)(2,1)S(1)}, u32[]{:S(2)}, u32[]{:S(2)}) collective-permute-start(bf16[256,512]{1,0:T(8,128)(2,1)S(1)} %add_convert_fusion.6), channel_id=1, source_target_pairs={{0,8},{1,9},{2,10},{3,11},{4,12},{5,13},{6,14},{7,15},{8,0},{9,1},... | collective-permute-start | bytes 786440 | tf_op jit(solution)/shard_map/ppermute | solution.py:62
  79.7 5.3 %copy-start.13 = (bf16[1152,256]{1,0:T(8,128)(2,1)}, bf16[1152,256]{1,0:T(8,128)(2,1)S(1)}, u32[]{:S(2)}) copy-start(bf16[1152,256]{1,0:T(8,128)(2,1)S(1)} %collective-permute-done.1.f_other) | copy-start | bytes 1769476
  79.7 9.0 %collective-permute-start.14 = (bf16[224,512]{1,0:T(8,128)(2,1)S(1)}, bf16[224,512]{1,0:T(8,128)(2,1)S(1)}, u32[]{:S(2)}, u32[]{:S(2)}) collective-permute-start(bf16[224,512]{1,0:T(8,128)(2,1)S(1)} %add_convert_fusion.11), channel_id=1, source_target_pairs={{0,8},{1,9},{2,10},{3,11},{4,12},{5,13},{6,14},{7,15},{8,0},{9,1},... | collective-permute-start | bytes 688136 | tf_op jit(solution)/shard_map/ppermute | solution.py:62
  83.4 10.1 %collective-permute-start.17 = (bf16[224,512]{1,0:T(8,128)(2,1)S(1)}, bf16[224,512]{1,0:T(8,128)(2,1)S(1)}, u32[]{:S(2)}, u32[]{:S(2)}) collective-permute-start(bf16[224,512]{1,0:T(8,128)(2,1)S(1)} %fusion.26), channel_id=1, source_target_pairs={{0,1},{1,0},{2,3},{3,2},{4,5},{5,4},{6,7},{7,6},{8,9},{9,8},{10,11... | collective-permute-start | bytes 688136 | tf_op jit(solution)/shard_map/ppermute | solution.py:62
  85.2 13.8 %collective-permute-start.19 = (bf16[256,512]{1,0:T(8,128)(2,1)S(1)}, bf16[256,512]{1,0:T(8,128)(2,1)S(1)}, u32[]{:S(2)}, u32[]{:S(2)}) collective-permute-start(bf16[256,512]{1,0:T(8,128)(2,1)S(1)} %get-tuple-element.93), channel_id=1, source_target_pairs={{0,2},{1,3},{2,0},{3,1},{4,6},{5,7},{6,4},{7,5},{8,10},{9,11},{10,... | collective-permute-start | bytes 786440 | tf_op jit(solution)/shard_map/ppermute | solution.py:62
  90.0 6.1 %collective-permute-start.18 = (bf16[224,512]{1,0:T(8,128)(2,1)S(1)}, bf16[224,512]{1,0:T(8,128)(2,1)S(1)}, u32[]{:S(2)}, u32[]{:S(2)}) collective-permute-start(bf16[224,512]{1,0:T(8,128)(2,1)S(1)} %add_convert_fusion.9), channel_id=1, source_target_pairs={{0,8},{1,9},{2,10},{3,11},{4,12},{5,13},{6,14},{7,15},{8,0},{9,1},... | collective-permute-start | bytes 688136 | tf_op jit(solution)/shard_map/ppermute | solution.py:62
  92.0 9.0 %collective-permute-start.20 = (bf16[224,512]{1,0:T(8,128)(2,1)S(1)}, bf16[224,512]{1,0:T(8,128)(2,1)}, u32[]{:S(2)}, u32[]{:S(2)}) collective-permute-start(bf16[224,512]{1,0:T(8,128)(2,1)S(1)} %add_convert_fusion.10), channel_id=1, source_target_pairs={{0,1},{1,0},{2,3},{3,2},{4,5},{5,4},{6,7},{7,6},{8,9},{9,8},{10,11... | collective-permute-start | bytes 688136 | tf_op jit(solution)/shard_map/ppermute | solution.py:62
  99.1 7.0 %collective-permute-start.21 = (bf16[256,512]{1,0:T(8,128)(2,1)S(1)}, bf16[256,512]{1,0:T(8,128)(2,1)S(1)}, u32[]{:S(2)}, u32[]{:S(2)}) collective-permute-start(bf16[256,512]{1,0:T(8,128)(2,1)S(1)} %add_convert_fusion.5), channel_id=1, source_target_pairs={{0,8},{1,9},{2,10},{3,11},{4,12},{5,13},{6,14},{7,15},{8,0},{9,1},... | collective-permute-start | bytes 786440 | tf_op jit(solution)/shard_map/ppermute | solution.py:62
  100.2 17.2 %collective-permute-start.22 = (bf16[224,512]{1,0:T(8,128)(2,1)S(1)}, bf16[224,512]{1,0:T(8,128)(2,1)S(1)}, u32[]{:S(2)}, u32[]{:S(2)}) collective-permute-start(bf16[224,512]{1,0:T(8,128)(2,1)S(1)} %get-tuple-element.91), channel_id=1, source_target_pairs={{0,2},{1,3},{2,0},{3,1},{4,6},{5,7},{6,4},{7,5},{8,10},{9,11},{10,... | collective-permute-start | bytes 688136 | tf_op jit(solution)/shard_map/ppermute | solution.py:62
  102.2 16.4 %collective-permute-start.23 = (bf16[448,512]{1,0:T(8,128)(2,1)S(1)}, bf16[448,512]{1,0:T(8,128)(2,1)S(1)}, u32[]{:S(2)}, u32[]{:S(2)}) collective-permute-start(bf16[448,512]{1,0:T(8,128)(2,1)S(1)} %maximum_select_fusion.7), channel_id=1, source_target_pairs={{0,8},{1,9},{2,10},{3,11},{4,12},{5,13},{6,14},{7,15},{8,0},{9,1},... | collective-permute-start | bytes 1376264 | tf_op jit(solution)/shard_map/ppermute | solution.py:62
  103.3 17.4 %collective-permute-start.24 = (bf16[224,512]{1,0:T(8,128)(2,1)S(1)}, bf16[224,512]{1,0:T(8,128)(2,1)S(1)}, u32[]{:S(2)}, u32[]{:S(2)}) collective-permute-start(bf16[224,512]{1,0:T(8,128)(2,1)S(1)} %get-tuple-element.89), channel_id=1, source_target_pairs={{0,2},{1,3},{2,0},{3,1},{4,6},{5,7},{6,4},{7,5},{8,10},{9,11},{10,... | collective-permute-start | bytes 688136 | tf_op jit(solution)/shard_map/ppermute | solution.py:62
  105.4 21.4 %collective-permute-start.27 = (bf16[448,512]{1,0:T(8,128)(2,1)S(1)}, bf16[448,512]{1,0:T(8,128)(2,1)S(1)}, u32[]{:S(2)}, u32[]{:S(2)}) collective-permute-start(bf16[448,512]{1,0:T(8,128)(2,1)S(1)} %maximum_select_fusion.6), channel_id=1, source_target_pairs={{0,1},{1,0},{2,3},{3,2},{4,5},{5,4},{6,7},{7,6},{8,9},{9,8},{10,11... | collective-permute-start | bytes 1376264 | tf_op jit(solution)/shard_map/ppermute | solution.py:62
  106.3 20.0 %collective-permute-start.26 = (bf16[512,512]{1,0:T(8,128)(2,1)S(1)}, bf16[512,512]{1,0:T(8,128)(2,1)S(1)}, u32[]{:S(2)}, u32[]{:S(2)}) collective-permute-start(bf16[512,512]{1,0:T(8,128)(2,1)S(1)} %maximum_select_fusion.5), channel_id=1, source_target_pairs={{0,4},{1,5},{2,6},{3,7},{4,0},{5,1},{6,2},{7,3},{8,12},{9,13},{10,... | collective-permute-start | bytes 1572872 | tf_op jit(solution)/shard_map/ppermute | solution.py:62
  117.4 8.6 %collective-permute-start.25 = (bf16[224,512]{1,0:T(8,128)(2,1)S(1)}, bf16[224,512]{1,0:T(8,128)(2,1)S(1)}, u32[]{:S(2)}, u32[]{:S(2)}) collective-permute-start(bf16[224,512]{1,0:T(8,128)(2,1)S(1)} %add_convert_fusion.8), channel_id=1, source_target_pairs={{0,8},{1,9},{2,10},{3,11},{4,12},{5,13},{6,14},{7,15},{8,0},{9,1},... | collective-permute-start | bytes 688136 | tf_op jit(solution)/shard_map/ppermute | solution.py:62
  118.9 15.8 %copy-start.2 = (bf16[896,512]{1,0:T(8,128)(2,1)}, bf16[896,512]{1,0:T(8,128)(2,1)S(1)}, u32[]{:S(2)}) copy-start(bf16[896,512]{1,0:T(8,128)(2,1)S(1)} %maximum_select_fusion.1.d_mine.refs_0_) | copy-start | bytes 2752516
  118.9 15.8 %collective-permute-start.29 = (bf16[896,512]{1,0:T(8,128)(2,1)S(1)}, bf16[896,512]{1,0:T(8,128)(2,1)S(1)}, u32[]{:S(2)}, u32[]{:S(2)}) collective-permute-start(bf16[896,512]{1,0:T(8,128)(2,1)S(1)} %maximum_select_fusion.1.d_mine.refs_0_), channel_id=1, source_target_pairs={{0,4},{1,5},{2,6},{3,7},{4,0},{5,1},{6,2},{7,3},{8,12},{9,13},{10,... | collective-permute-start | bytes 2752520 | tf_op jit(solution)/shard_map/ppermute | solution.py:62
  120.9 9.6 %collective-permute-start.28 = (bf16[224,512]{1,0:T(8,128)(2,1)S(1)}, bf16[224,512]{1,0:T(8,128)(2,1)S(1)}, u32[]{:S(2)}, u32[]{:S(2)}) collective-permute-start(bf16[224,512]{1,0:T(8,128)(2,1)S(1)} %add_convert_fusion.7), channel_id=1, source_target_pairs={{0,1},{1,0},{2,3},{3,2},{4,5},{5,4},{6,7},{7,6},{8,9},{9,8},{10,11... | collective-permute-start | bytes 688136 | tf_op jit(solution)/shard_map/ppermute | solution.py:62
  126.2 14.2 %collective-permute-start.30 = (bf16[448,512]{1,0:T(8,128)(2,1)S(1)}, bf16[448,512]{1,0:T(8,128)(2,1)S(1)}, u32[]{:S(2)}, u32[]{:S(2)}) collective-permute-start(bf16[448,512]{1,0:T(8,128)(2,1)S(1)} %maximum_select_fusion.8), channel_id=1, source_target_pairs={{0,1},{1,0},{2,3},{3,2},{4,5},{5,4},{6,7},{7,6},{8,9},{9,8},{10,11... | collective-permute-start | bytes 1376264 | tf_op jit(solution)/shard_map/ppermute | solution.py:62
  126.8 34.9 %copy-start.1 = (bf16[1024,512]{1,0:T(8,128)(2,1)}, bf16[1024,512]{1,0:T(8,128)(2,1)S(1)}, u32[]{:S(2)}) copy-start(bf16[1024,512]{1,0:T(8,128)(2,1)S(1)} %maximum_select_fusion.d_mine.refs_6_) | copy-start | bytes 3145732
  127.2 20.0 %copy-start.3 = (bf16[896,512]{1,0:T(8,128)(2,1)}, bf16[896,512]{1,0:T(8,128)(2,1)S(1)}, u32[]{:S(2)}) copy-start(bf16[896,512]{1,0:T(8,128)(2,1)S(1)} %maximum_select_fusion.2.d_mine.refs_2_) | copy-start | bytes 2752516
  130.7 13.5 %collective-permute-start.31 = (bf16[448,512]{1,0:T(8,128)(2,1)S(1)}, bf16[448,512]{1,0:T(8,128)(2,1)S(1)}, u32[]{:S(2)}, u32[]{:S(2)}) collective-permute-start(bf16[448,512]{1,0:T(8,128)(2,1)S(1)} %maximum_select_fusion.9), channel_id=1, source_target_pairs={{0,8},{1,9},{2,10},{3,11},{4,12},{5,13},{6,14},{7,15},{8,0},{9,1},... | collective-permute-start | bytes 1376264 | tf_op jit(solution)/shard_map/ppermute | solution.py:62
  131.1 16.1 %collective-permute-start.32 = (bf16[896,512]{1,0:T(8,128)(2,1)S(1)}, bf16[896,512]{1,0:T(8,128)(2,1)S(1)}, u32[]{:S(2)}, u32[]{:S(2)}) collective-permute-start(bf16[896,512]{1,0:T(8,128)(2,1)S(1)} %maximum_select_fusion.2.d_mine.refs_2_), channel_id=1, source_target_pairs={{0,4},{1,5},{2,6},{3,7},{4,0},{5,1},{6,2},{7,3},{8,12},{9,13},{10,... | collective-permute-start | bytes 2752520 | tf_op jit(solution)/shard_map/ppermute | solution.py:62
  132.2 29.5 %collective-permute-start.34 = (bf16[1024,512]{1,0:T(8,128)(2,1)S(1)}, bf16[1024,512]{1,0:T(8,128)(2,1)S(1)}, u32[]{:S(2)}, u32[]{:S(2)}) collective-permute-start(bf16[1024,512]{1,0:T(8,128)(2,1)S(1)} %maximum_select_fusion.d_mine.refs_6_), channel_id=1, source_target_pairs={{0,1},{1,0},{2,3},{3,2},{4,5},{5,4},{6,7},{7,6},{8,9},{9,8},{10,11... | collective-permute-start | bytes 3145736 | tf_op jit(solution)/shard_map/ppermute | solution.py:62
  140.8 16.2 %copy-start.4 = (bf16[896,512]{1,0:T(8,128)(2,1)}, bf16[896,512]{1,0:T(8,128)(2,1)S(1)}, u32[]{:S(2)}) copy-start(bf16[896,512]{1,0:T(8,128)(2,1)S(1)} %maximum_select_fusion.3.d_mine.refs_4_) | copy-start | bytes 2752516
  140.8 16.2 %collective-permute-start.33 = (bf16[896,512]{1,0:T(8,128)(2,1)S(1)}, bf16[896,512]{1,0:T(8,128)(2,1)S(1)}, u32[]{:S(2)}, u32[]{:S(2)}) collective-permute-start(bf16[896,512]{1,0:T(8,128)(2,1)S(1)} %maximum_select_fusion.3.d_mine.refs_4_), channel_id=1, source_target_pairs={{0,4},{1,5},{2,6},{3,7},{4,0},{5,1},{6,2},{7,3},{8,12},{9,13},{10,... | collective-permute-start | bytes 2752520 | tf_op jit(solution)/shard_map/ppermute | solution.py:62
  144.6 22.2 %copy-start.5 = (bf16[896,512]{1,0:T(8,128)(2,1)}, bf16[896,512]{1,0:T(8,128)(2,1)S(1)}, u32[]{:S(2)}) copy-start(bf16[896,512]{1,0:T(8,128)(2,1)S(1)} %maximum_select_fusion.4.d_mine.refs_8_) | copy-start | bytes 2752516
  144.7 22.2 %collective-permute-start.35 = (bf16[896,512]{1,0:T(8,128)(2,1)S(1)}, bf16[896,512]{1,0:T(8,128)(2,1)S(1)}, u32[]{:S(2)}, u32[]{:S(2)}) collective-permute-start(bf16[896,512]{1,0:T(8,128)(2,1)S(1)} %maximum_select_fusion.4.d_mine.refs_8_), channel_id=1, source_target_pairs={{0,4},{1,5},{2,6},{3,7},{4,0},{5,1},{6,2},{7,3},{8,12},{9,13},{10,... | collective-permute-start | bytes 2752520 | tf_op jit(solution)/shard_map/ppermute | solution.py:62
  147.1 4.7 %copy-start.8 = (bf16[896,512]{1,0:T(8,128)(2,1)}, bf16[896,512]{1,0:T(8,128)(2,1)S(1)}, u32[]{:S(2)}) copy-start(bf16[896,512]{1,0:T(8,128)(2,1)S(1)} %collective-permute-done.32.d_other.refs_3_) | copy-start | bytes 2752516
  161.7 4.7 %copy-start.6 = (bf16[1024,512]{1,0:T(8,128)(2,1)}, bf16[1024,512]{1,0:T(8,128)(2,1)S(1)}, u32[]{:S(2)}) copy-start(bf16[1024,512]{1,0:T(8,128)(2,1)S(1)} %collective-permute-done.34.d_other.refs_7_) | copy-start | bytes 3145732
  166.8 4.7 %copy-start.10 = (bf16[896,512]{1,0:T(8,128)(2,1)}, bf16[896,512]{1,0:T(8,128)(2,1)S(1)}, u32[]{:S(2)}) copy-start(bf16[896,512]{1,0:T(8,128)(2,1)S(1)} %collective-permute-done.35.d_other.refs_9_) | copy-start | bytes 2752516
  172.9 2.8 %collective-permute-start.36 = (bf16[1152,512]{1,0:T(8,128)(2,1)S(1)}, bf16[1152,512]{1,0:T(8,128)(2,1)S(1)}, u32[]{:S(2)}, u32[]{:S(2)}) collective-permute-start(bf16[1152,512]{1,0:T(8,128)(2,1)S(1)} %get-tuple-element.88), channel_id=1, source_target_pairs={{0,16},{16,0},{1,17},{17,1},{2,18},{18,2},{3,19},{19,3},{4,20},{20... | collective-permute-start | bytes 3538952 | tf_op jit(solution)/shard_map/ppermute | solution.py:289
  (7 other events, 19.0 us)
